TPU v7x, 32 devices: a whole 2x2x4 slice. The times are simulated.
32 devices in a mesh: px: 4 (over y, x), py: 8 (over z, core).
Axes of the slice: x: 2, y: 2, z: 4, core: 2. Of those that a mesh axis runs over, the one named last changes fastest.
Arguments:
- carried: bfloat16 [2, 512, 512, 128], P(None, 'px', 'py'), may hold values from -0.59765625 to 0.59765625
- velocity: bfloat16 [2, 128, 128], P(None, ('px', 'py')), may hold values from -4 to 4
- strip_column: int32 [128], P(('px', 'py')), may hold values from 0 to 262143, as said below
- thick: float32 [128], replicated, may hold values from 0.5 to 2
Outputs:
- pressure: bfloat16 [2, 512, 512, 128], P(None, 'px', 'py')
- added_mass: float32 [2, 2], replicated
Inputs may be any that keep to these rules, and one draw needn't show every extreme that they name: `strip_column`: no two strips share a grid column.
All inputs are finite; a program needn't handle non-finite values.
Results may differ from a plain program's by a relative error of at most 0.0081.
Values may be sent and summed in bfloat16 or wider, within the bound.
No kernel may reach another device: no remote copies, remote signals or barrier semaphores. Data moves between devices by JAX's collectives and lax.ppermute only.
A program may use at most 128 MiB of HBM per device.

v0:
```python
import math

import jax
import jax.numpy as jnp
from jax import lax
from jax.sharding import PartitionSpec as P


def sine_table(length):
    steps = jnp.arange(length, dtype=jnp.int32) + 1
    product = steps[:, None] * steps[None, :] % (2 * (length + 1))
    angle = product.astype(jnp.float32) * (math.pi / (length + 1))
    return (math.sqrt(2.0 / (length + 1)) * jnp.sin(angle)).astype(jnp.bfloat16)


def wave_numbers(position, length):
    return 2.0 - 2.0 * jnp.cos(math.pi * (position.astype(jnp.float32) + 1.0) / (length + 1))


def vertical_bands(thick):
    inv_gap = 2.0 / (thick[:-1] + thick[1:])
    nothing = jnp.zeros((1,), jnp.float32)
    sub_diag = -jnp.concatenate([nothing, inv_gap])
    super_diag = -jnp.concatenate([inv_gap, nothing])
    surface = jnp.concatenate([jnp.zeros((thick.shape[0] - 1,), jnp.float32), 2.0 / thick[-1:]])
    return (sub_diag, super_diag, surface - sub_diag - super_diag)


def shift_next(values, fill_value):
    return jnp.concatenate([values[..., 1:], jnp.full_like(values[..., :1], fill_value)], axis=-1)


def shift_prev(values):
    return jnp.concatenate([jnp.zeros_like(values[..., :1]), values[..., :-1]], axis=-1)


def reduce_solve(sub_diag, main_diag, super_diag, right_side):
    length = right_side.shape[-1]
    if length == 1:
        return right_side / main_diag
    sub_even, sub_odd = (sub_diag[..., 0::2], sub_diag[..., 1::2])
    main_even, main_odd = (main_diag[..., 0::2], main_diag[..., 1::2])
    super_even, super_odd = (super_diag[..., 0::2], super_diag[..., 1::2])
    right_even, right_odd = (right_side[..., 0::2], right_side[..., 1::2])
    alpha_left = -sub_odd / main_even
    gamma_right = -super_odd / shift_next(main_even, 1.0)
    new_sub = alpha_left * sub_even
    new_main = main_odd + alpha_left * super_even + gamma_right * shift_next(sub_even, 0.0)
    new_super = gamma_right * shift_next(super_even, 0.0)
    new_right = right_odd + alpha_left * right_even + gamma_right * shift_next(right_even, 0.0)
    odd_values = reduce_solve(new_sub, new_main, new_super, new_right)
    even_values = (
        right_even - sub_even * shift_prev(odd_values) - super_even * odd_values
    ) / main_even
    joined = jnp.stack([even_values, odd_values], axis=-1)
    return joined.reshape(joined.shape[:-2] + (length,))


def shards(carried, velocity, strip_column, thick):
    modes_here, x_local, y_local, layers = carried.shape
    count_px = lax.axis_size("px")
    count_py = lax.axis_size("py")
    index_px = lax.axis_index("px")
    index_py = lax.axis_index("py")
    width_x = x_local * count_px
    width_y = y_local * count_py
    y_column = width_y // (count_px * count_py)
    all_velocity, all_column = (
        lax.all_gather(velocity, ("px", "py"), axis=1, tiled=True),
        lax.all_gather(strip_column, ("px", "py"), axis=0, tiled=True),
    )
    strip_count = all_column.shape[0]
    local_x = all_column // width_y - index_px * x_local
    local_y = all_column % width_y - index_py * y_local
    inside = (local_x >= 0) & (local_x < x_local) & (local_y >= 0) & (local_y < y_local)
    target = jnp.where(inside, local_x * y_local + local_y, x_local * y_local)
    flat_grid = carried.astype(jnp.float32).reshape(modes_here, x_local * y_local, layers)
    flat_grid = flat_grid.at[:, target, :].add(all_velocity.astype(jnp.float32), mode="drop")
    source = flat_grid.reshape(modes_here, x_local, y_local, layers).astype(jnp.bfloat16)
    sine_x = sine_table(width_x)
    sine_y = sine_table(width_y)
    wave_x = wave_numbers(jnp.arange(width_x, dtype=jnp.int32), width_x)
    sub_diag, super_diag, base_diag = vertical_bands(thick)
    row_pencil = jnp.einsum(
        "mxyz,by->mxbz",
        lax.all_to_all(source, "py", split_axis=1, concat_axis=2, tiled=True),
        sine_y,
        preferred_element_type=jnp.float32,
    ).astype(jnp.bfloat16)
    y_start = (index_px * count_py + index_py) * y_column
    wave_y = wave_numbers(y_start + jnp.arange(y_column, dtype=jnp.int32), width_y)
    spectrum = jnp.einsum(
        "mxyz,ax->mayz",
        lax.all_to_all(row_pencil, ("px", "py"), split_axis=2, concat_axis=1, tiled=True),
        sine_x,
        preferred_element_type=jnp.float32,
    )
    main_diag = base_diag + (wave_x[:, None, None] + wave_y[None, :, None]) * thick
    solved = reduce_solve(sub_diag, main_diag, super_diag, spectrum * thick).astype(jnp.bfloat16)
    column_pencil = jnp.einsum(
        "mayz,xa->mxyz", solved, sine_x, preferred_element_type=jnp.float32
    ).astype(jnp.bfloat16)
    row_return = lax.all_to_all(
        column_pencil, ("px", "py"), split_axis=1, concat_axis=2, tiled=True
    )
    row_pressure = jnp.einsum(
        "mxbz,yb->mxyz", row_return, sine_y, preferred_element_type=jnp.float32
    ).astype(jnp.bfloat16)
    pressure = lax.all_to_all(row_pressure, "py", split_axis=2, concat_axis=1, tiled=True)
    safe_target = jnp.minimum(target, x_local * y_local - 1)
    at_panels = jnp.take(
        pressure.reshape(modes_here, x_local * y_local, layers), safe_target, axis=1
    ).astype(jnp.float32)
    at_panels = at_panels * inside.astype(jnp.float32)[None, :, None]
    local_mass = jnp.einsum(
        "isz,jsz,z->ij",
        at_panels,
        all_velocity.astype(jnp.float32),
        thick,
        precision=lax.Precision.HIGHEST,
    )
    added_mass = lax.psum(local_mass, ("px", "py")) / (strip_count * layers)
    return (pressure, added_mass)


def solution(mesh):
    return jax.shard_map(
        shards,
        mesh=mesh,
        in_specs=(P(None, "px", "py", None), P(None, ("px", "py"), None), P(("px", "py")), P()),
        out_specs=(P(None, "px", "py", None), P()),
        check_vma=False,
    )
```

profile of v0, /device:TPU:0, one launch (start us, length us, event | category | flops | bytes accessed | tf_op | source)
XLA Modules:
  0.0 885.2 jit_solution(2594700329667885531)
XLA Ops:
  0.7 13.9 %copy.156 = f32[2,128,64,128]{3,0,2,1:T(2,128)} copy(bf16[2,128,64,128]{3,2,1,0:T(8,128)(2,1)} %param.4) | data formatting | bytes 12582912 | tf_op jit(solution)/shard_map/reshape | solution.py:77
  14.8 42.0 %all-reduce.29 = s32[128]{0:T(128)S(1)} all-reduce(s32[128]{0:T(128)S(1)} %dynamic-update-slice), channel_id=1, replica_groups=mesh['px'=4,'py'=8] {'px','py'}, use_global_device_ids=true, to_apply=%add.29 | all-reduce | flops 128 | bytes 1024
  57.4 40.7 %all_gather.7 = bf16[2,128,128]{2,0,1:T(2,128)(2,1)S(1)} all-gather(bf16[2,4,128]{2,0,1:T(2,128)(2,1)S(1)} %copy.157), channel_id=1, replica_groups=mesh['px'=4,'py'=8] {'px','py'}, dimensions={1}, use_global_device_ids=true | all-gather | bytes 67584 | tf_op jit(solution)/shard_map/all_gather | solution.py:69
  98.7 13.9 %scatter_fusion = f32[2,8192,128]{2,0,1:T(2,128)} fusion(f32[2,8192,128]{2,0,1:T(2,128)} %bitcast.126, s32[128]{0:T(128)S(1)} %compare_select_fusion.1, f32[128,2,128]{2,1,0:T(2,128)S(1)} %convert_bitcast_fusion.3), kind=kCustom, calls=%fused_computation.1 | custom fusion | flops 32768 | bytes 393728 | tf_op jit(solution)/shard_map/scatter-add | solution.py:78
  125.8 94.0 %all-to-all-done = bf16[2,128,64,128]{3,2,0,1:T(8,128)(2,1)} async-done(((bf16[2,128,64,128]{3,2,0,1:T(8,128)(2,1)}), bf16[2,128,64,128]{3,2,0,1:T(8,128)(2,1)}, u32[]{:S(2)}, u32[]{:S(2)}) %all-to-all-start) | async-done | bytes 4194336 | tf_op jit(solution)/shard_map/all_to_all | solution.py:86
  223.0 7.0 convert_bitcast_fusion.2
  243.7 8.1 slice.282
  251.9 9.8 %slice.290 = f32[512,16,64]{0,2,1:T(8,128)} slice(f32[512,16,128]{0,2,1:T(8,128)} %multiply_add_fusion.1), slice={[0:512:1], [0:16:1], [1:128:2]} | slice | bytes 4194304 | tf_op jit(solution)/shard_map/slice | solution.py:42
  282.5 5.6 slice.289
  385.0 6.9 copy.163
  392.0 7.7 copy.164
  399.7 8.5 fusion.20
  412.7 18.5 %slice.275 = f32[2,512,16,64]{1,3,2,0:T(8,128)} slice(f32[2,512,16,128]{1,3,2,0:T(8,128)} %multiply_bitcast_fusion), slice={[0:2:1], [0:512:1], [0:16:1], [0:128:2]} | slice | bytes 8388608 | tf_op jit(solution)/shard_map/slice | solution.py:44
  431.2 18.5 %slice.279 = f32[2,512,16,64]{1,3,2,0:T(8,128)} slice(f32[2,512,16,128]{1,3,2,0:T(8,128)} %multiply_bitcast_fusion), slice={[0:2:1], [0:512:1], [0:16:1], [1:128:2]} | slice | bytes 8388608 | tf_op jit(solution)/shard_map/slice | solution.py:44
  454.8 8.3 multiply_add_fusion
  463.0 9.8 %slice.286 = f32[2,512,16,32]{1,3,2,0:T(8,128)} slice(f32[2,512,16,64]{1,3,2,0:T(8,128)} %multiply_add_fusion), slice={[0:2:1], [0:512:1], [0:16:1], [0:64:2]} | slice | bytes 4194304 | tf_op jit(solution)/shard_map/slice | solution.py:44
  472.9 9.9 %slice.288 = f32[2,512,16,32]{1,3,2,0:T(8,128)} slice(f32[2,512,16,64]{1,3,2,0:T(8,128)} %multiply_add_fusion), slice={[0:2:1], [0:512:1], [0:16:1], [1:64:2]} | slice | bytes 4194304 | tf_op jit(solution)/shard_map/slice | solution.py:44
  563.0 6.6 fusion.4
  572.4 14.5 %convert_bitcast_fusion.1 = bf16[2,512,16,128]{3,1,2,0:T(8,128)(2,1)S(1)} fusion(bf16[2,512,16,128]{1,2,3,0:T(8,128)(2,1)S(1)} %bitcast.144, s32[512]{0:T(512)S(1)} %iota_add_fusion), kind=kOutput, calls=%fused_computation.8 | convolution fusion | flops 2152464384 | bytes 8390656 | tf_op jit(solution)/shard_map/mayz,xa->mxyz/dot_general | solution.py:100
  589.6 101.1 %all_to_all.72 = bf16[2,512,16,128]{3,2,0,1:T(8,128)(2,1)S(1)} all-to-all(bf16[2,512,16,128]{3,2,0,1:T(8,128)(2,1)S(1)} %copy.187), channel_id=1, replica_groups=mesh['px'=4,'py'=8] {'px','py'}, dimensions={1} | all-to-all | bytes 8388608 | tf_op jit(solution)/shard_map/all_to_all | solution.py:103
  691.9 7.0 convert_bitcast_fusion
  708.8 93.8 %all-to-all-done.3 = bf16[2,16,512,128]{3,1,0,2:T(8,128)(2,1)} async-done(((bf16[2,16,512,128]{3,1,0,2:T(8,128)(2,1)}), bf16[2,16,512,128]{3,1,0,2:T(8,128)(2,1)}, u32[]{:S(2)}, u32[]{:S(2)}) %all-to-all-start.3) | async-done | bytes 4194336 | tf_op jit(solution)/shard_map/all_to_all | solution.py:109
  808.4 35.4 %copy.193 = bf16[2,8192,128]{2,0,1:T(2,128)(2,1)} copy(bf16[2,8192,128]{2,1,0:T(8,128)(2,1)S(1)} %bitcast.131) | data formatting | bytes 8388608 | tf_op jit(solution)/shard_map/reshape | solution.py:112
  847.5 36.9 %psum.7 = f32[2,2]{1,0:T(2,128)S(1)} all-reduce(f32[2,2]{1,0:T(2,128)S(1)} %bitcast.168), channel_id=1, replica_groups=mesh['px'=4,'py'=8] {'px','py'}, use_global_device_ids=true, to_apply=%region_1.2 | all-reduce | flops 4 | bytes 32 | tf_op jit(solution)/shard_map/psum | solution.py:122
  (263 shorter events, 264.2 us)
Async XLA Ops:
  0.6 13.9 %copy-start.45 = (s32[4]{0:T(128)S(1)}, s32[4]{0:T(128)}, u32[]{:S(2)}) copy-start(s32[4]{0:T(128)} %param.6) | copy-start | bytes 52
  0.6 56.7 %copy-start.41 = (bf16[2,4,128]{2,1,0:T(4,128)(2,1)S(1)}, bf16[2,4,128]{2,1,0:T(4,128)(2,1)}, u32[]{:S(2)}) copy-start(bf16[2,4,128]{2,1,0:T(4,128)(2,1)} %param.5) | copy-start | bytes 6148
  121.2 98.6 %all-to-all-start = ((bf16[2,128,64,128]{3,2,0,1:T(8,128)(2,1)}), bf16[2,128,64,128]{3,2,0,1:T(8,128)(2,1)}, u32[]{:S(2)}, u32[]{:S(2)}) async-start(bf16[2,128,64,128]{3,2,0,1:T(8,128)(2,1)} %copy.158), calls=%async_computation | async-start | bytes 8388608 | tf_op jit(solution)/shard_map/all_to_all | solution.py:86
  234.7 150.4 %all-to-all-start.1 = ((bf16[2,16,512,128]{3,1,0,2:T(8,128)(2,1)}), bf16[2,16,512,128]{3,1,0,2:T(8,128)(2,1)}, u32[]{:S(2)}, u32[]{:S(2)}) async-start(bf16[2,16,512,128]{3,1,0,2:T(8,128)(2,1)} %copy.161), calls=%async_computation.1 | async-start | bytes 8388608 | tf_op jit(solution)/shard_map/all_to_all | solution.py:94
  282.5 33.7 %copy-start.6 = (f32[512,16,32]{0,2,1:T(8,128)}, f32[512,16,32]{0,2,1:T(8,128)S(1)}, u32[]{:S(2)}) copy-start(f32[512,16,32]{0,2,1:T(8,128)S(1)} %slice.287) | copy-start | bytes 3145732
  321.5 21.9 %copy-start.13 = (f32[512,16,16]{0,2,1:T(8,128)}, f32[512,16,16]{0,2,1:T(8,128)S(1)}, u32[]{:S(2)}) copy-start(f32[512,16,16]{0,2,1:T(8,128)S(1)} %slice.299) | copy-start | bytes 1572868
  331.2 14.4 %copy-start.15 = (f32[512,16,16]{0,2,1:T(8,128)}, f32[512,16,16]{0,2,1:T(8,128)S(1)}, u32[]{:S(2)}) copy-start(f32[512,16,16]{0,2,1:T(8,128)S(1)} %slice.305) | copy-start | bytes 1572868
  340.0 24.4 %copy-start.23 = (f32[512,16,8]{0,2,1:T(8,128)}, f32[512,16,8]{0,2,1:T(8,128)S(1)}, u32[]{:S(2)}) copy-start(f32[512,16,8]{0,2,1:T(8,128)S(1)} %slice.327) | copy-start | bytes 786436
  347.6 12.5 %copy-start.19 = (f32[512,16,8]{0,2,1:T(8,128)}, f32[512,16,8]{0,2,1:T(8,128)S(1)}, u32[]{:S(2)}) copy-start(f32[512,16,8]{0,2,1:T(8,128)S(1)} %slice.311) | copy-start | bytes 786436
  352.5 18.9 %copy-start.21 = (f32[512,16,8]{0,2,1:T(8,128)}, f32[512,16,8]{0,2,1:T(8,128)S(1)}, u32[]{:S(2)}) copy-start(f32[512,16,8]{0,2,1:T(8,128)S(1)} %slice.317) | copy-start | bytes 786436
  355.0 23.5 %copy-start.25 = (f32[512,16,8]{0,2,1:T(8,128)}, f32[512,16,8]{0,2,1:T(8,128)S(1)}, u32[]{:S(2)}) copy-start(f32[512,16,8]{0,2,1:T(8,128)S(1)} %get-tuple-element.22) | copy-start | bytes 786436
  360.1 31.8 %copy-start.27 = (f32[512,16,8]{0,2,1:T(8,128)}, f32[512,16,8]{0,2,1:T(8,128)S(1)}, u32[]{:S(2)}) copy-start(f32[512,16,8]{0,2,1:T(8,128)S(1)} %get-tuple-element.20) | copy-start | bytes 786436
  360.1 17.3 %copy-start.29 = (f32[512,16,4]{0,2,1:T(4,128)S(1)}, f32[512,16,4]{0,2,1:T(4,128)}, u32[]{:S(2)}) copy-start(f32[512,16,4]{0,2,1:T(4,128)} %slice.339) | copy-start | bytes 393220
  368.0 24.0 %copy-start.28 = (f32[512,16,4]{0,2,1:T(4,128)}, f32[512,16,4]{0,2,1:T(4,128)S(1)}, u32[]{:S(2)}) copy-start(f32[512,16,4]{0,2,1:T(4,128)S(1)} %slice.329) | copy-start | bytes 393220
  372.4 19.6 %copy-start.30 = (f32[512,16,4]{0,2,1:T(4,128)}, f32[512,16,4]{0,2,1:T(4,128)S(1)}, u32[]{:S(2)}) copy-start(f32[512,16,4]{0,2,1:T(4,128)S(1)} %get-tuple-element.18) | copy-start | bytes 393220
  372.7 19.2 %copy-start.34 = (f32[512,16,2]{0,2,1:T(2,128)}, f32[512,16,2]{0,2,1:T(2,128)S(1)}, u32[]{:S(2)}) copy-start(f32[512,16,2]{0,2,1:T(2,128)S(1)} %slice.348) | copy-start | bytes 196612
  375.7 16.3 %copy-start.31 = (f32[512,8,8]{0,2,1:T(8,128)}, f32[512,8,8]{0,2,1:T(8,128)S(1)}, u32[]{:S(2)}) copy-start(f32[512,8,8]{0,2,1:T(8,128)S(1)} %get-tuple-element.45) | copy-start | bytes 393220
  376.0 15.9 %copy-start.32 = (f32[512,16,2]{0,2,1:T(2,128)}, f32[512,16,2]{0,2,1:T(2,128)S(1)}, u32[]{:S(2)}) copy-start(f32[512,16,2]{0,2,1:T(2,128)S(1)} %slice.335) | copy-start | bytes 196612
  378.8 13.2 %copy-start.33 = (f32[512,16,2]{0,2,1:T(2,128)}, f32[512,16,2]{0,2,1:T(2,128)S(1)}, u32[]{:S(2)}) copy-start(f32[512,16,2]{0,2,1:T(2,128)S(1)} %slice.341) | copy-start | bytes 196612
  380.2 11.8 %copy-start.38 = (f32[512,16,2]{0,2,1:T(2,128)}, f32[512,16,2]{0,2,1:T(2,128)S(1)}, u32[]{:S(2)}) copy-start(f32[512,16,2]{0,2,1:T(2,128)S(1)} %get-tuple-element.12) | copy-start | bytes 196612
  472.9 12.0 %copy-start.10 = (f32[512,16,32]{0,2,1:T(8,128)S(1)}, f32[512,16,32]{0,2,1:T(8,128)}, u32[]{:S(2)}) copy-start(f32[512,16,32]{0,2,1:T(8,128)} %get-tuple-element.30) | copy-start | bytes 3145732
  498.9 12.4 %copy-start.26 = (f32[512,16,8]{0,2,1:T(8,128)S(1)}, f32[512,16,8]{0,2,1:T(8,128)}, u32[]{:S(2)}) copy-start(f32[512,16,8]{0,2,1:T(8,128)} %copy-done.25) | copy-start | bytes 786436
  703.7 98.9 %all-to-all-start.3 = ((bf16[2,16,512,128]{3,1,0,2:T(8,128)(2,1)}), bf16[2,16,512,128]{3,1,0,2:T(8,128)(2,1)}, u32[]{:S(2)}, u32[]{:S(2)}) async-start(bf16[2,16,512,128]{3,1,0,2:T(8,128)(2,1)} %copy.189), calls=%async_computation.3 | async-start | bytes 8388608 | tf_op jit(solution)/shard_map/all_to_all | solution.py:109
  808.4 38.3 %copy-start.40 = (pred[128]{0:T(512)(128)(4,1)S(1)}, pred[128]{0:T(512)(128)(4,1)}, u32[]{:S(2)}) copy-start(pred[128]{0:T(512)(128)(4,1)} %get-tuple-element.2) | copy-start | bytes 388
  (25 other events, 84.9 us)
where the time goes:
time: 900 us; the launch traced here: 885 us
  local copies, waits for them, and re-layouts  320 us (36%)
  blocking collectives  221 us (25%)
  waiting for transfers between devices  188 us (21%)
  other arithmetic  102 us (11%)
  matrix products  37.6 us (4%)
  starting transfers between devices  13.5 us (2%)
    all_to_all x1, blocking collectives, shards(): lax.all_to_all(column_pencil, ('px', 'py'), split_axis=1, concat_axis=2,...  101 us
    all_to_all x1, waiting for transfers between devices, shards(): lax.all_to_all(source, 'py', split_axis=1, concat_axis=2, tiled=True)  94 us
    all_to_all x1, waiting for transfers between devices, shards(): lax.all_to_all(row_pressure, 'py', split_axis=2, concat_axis=1, tiled=True)  93.8 us
    slice x12, local copies, waits for them, and re-layouts, reduce_solve(): right_even, right_odd = (right_side[..., 0::2], right_side[..., 1::2])  88.8 us
    unnamed x1, blocking collectives  42 us
    slice x12, local copies, waits for them, and re-layouts, reduce_solve(): main_even, main_odd = (main_diag[..., 0::2], main_diag[..., 1::2])  40.8 us
    all_gather x1, blocking collectives, shards(): lax.all_gather(velocity, ('px', 'py'), axis=1, tiled=True)  40.7 us
    psum x1, blocking collectives, shards(): added_mass = lax.psum(local_mass, ('px', 'py')) / (strip_count * layers)  36.9 us
  transfers between devices with their start and end apart: 3, of which 2 were waited for; matrix products, arithmetic and copies ran while one was open for 16% of the time, Pallas kernels for 0%

commit v1 on v0

v1 whole, which is shorter than its diff:
```python
import functools
import math

import jax
import jax.numpy as jnp
import ml_dtypes
import numpy as np
from jax import lax
from jax.experimental import pallas as pl
from jax.experimental.pallas import tpu as pltpu
from jax.sharding import PartitionSpec as P

VMEM_LIMIT = 56 * 1024 * 1024
VMEM = pltpu.MemorySpace.VMEM
SMEM = pltpu.MemorySpace.SMEM
LANES = 128


def sine_table(length):
    steps = np.arange(1, length + 1)
    product = steps[:, None] * steps[None, :] % (2 * (length + 1))
    return math.sqrt(2.0 / (length + 1)) * np.sin(product * (math.pi / (length + 1)))


def wave_numbers(length):
    return 4.0 * np.sin(np.arange(1, length + 1) * (math.pi / (2 * (length + 1)))) ** 2


def bf16(table):
    return jnp.asarray(table.astype(ml_dtypes.bfloat16))


def contract(left, right, left_dim, right_dim):
    return lax.dot_general(
        left, right, (((left_dim,), (right_dim,)), ((), ())), preferred_element_type=jnp.float32
    )


def forward_y_kernel(table_ref, grid_ref, out_ref, scratch):
    _, x_chunk, rows, layers = grid_ref.shape
    count, part = out_ref.shape[:2]
    group = table_ref.shape[0] // rows
    for start in range(0, x_chunk, group):
        block = grid_ref[0, start : start + group].reshape(group * rows, layers)
        result = contract(table_ref[...], block, 1, 0)
        for at in range(group):
            scratch[pl.ds(start + at, rows, stride=x_chunk), :] = result[
                at * rows : (at + 1) * rows
            ]
    out_ref[:, :, 0] = scratch[...].reshape(count, part, x_chunk, layers).astype(jnp.bfloat16)


def inverse_y_kernel(table_ref, in_ref, out_ref, scratch):
    _, x_chunk, rows, layers = out_ref.shape
    group = table_ref.shape[0] // rows
    scratch[...] = in_ref[:, :, 0].astype(jnp.float32).reshape(rows * x_chunk, layers)
    for start in range(0, x_chunk, group):
        block = jnp.concatenate(
            [scratch[pl.ds(start + at, rows, stride=x_chunk), :] for at in range(group)], axis=0
        ).astype(jnp.bfloat16)
        result = contract(table_ref[...], block, 1, 0)
        out_ref[0, start : start + group] = result.reshape(group, rows, layers).astype(
            jnp.bfloat16
        )


def y_table(rows):
    group = max(1, 256 // rows)
    return bf16(np.kron(np.eye(group), sine_table(rows)))


def forward_y(carried, count):
    modes, x_local, rows, layers = carried.shape
    chunk = 16
    part = rows // count
    table = y_table(rows)
    return pl.pallas_call(
        forward_y_kernel,
        grid=(modes, x_local // chunk),
        in_specs=[
            pl.BlockSpec(table.shape, lambda m, i: (0, 0)),
            pl.BlockSpec((1, chunk, rows, layers), lambda m, i: (m, i, 0, 0)),
        ],
        out_specs=pl.BlockSpec((count, part, 1, chunk, layers), lambda m, i: (0, 0, m, i, 0)),
        out_shape=jax.ShapeDtypeStruct((count, part, modes, x_local, layers), jnp.bfloat16),
        scratch_shapes=[pltpu.VMEM((rows * chunk, layers), jnp.float32)],
        compiler_params=pltpu.CompilerParams(vmem_limit_bytes=VMEM_LIMIT),
        name="forward_y",
    )(table, carried)


def inverse_y(spectra, rows):
    count, part, modes, x_local, layers = spectra.shape
    chunk = 16
    table = y_table(rows)
    return pl.pallas_call(
        inverse_y_kernel,
        grid=(modes, x_local // chunk),
        in_specs=[
            pl.BlockSpec(table.shape, lambda m, i: (0, 0)),
            pl.BlockSpec((count, part, 1, chunk, layers), lambda m, i: (0, 0, m, i, 0)),
        ],
        out_specs=pl.BlockSpec((1, chunk, rows, layers), lambda m, i: (m, i, 0, 0)),
        out_shape=jax.ShapeDtypeStruct((modes, x_local, rows, layers), jnp.bfloat16),
        scratch_shapes=[pltpu.VMEM((rows * chunk, layers), jnp.float32)],
        compiler_params=pltpu.CompilerParams(vmem_limit_bytes=VMEM_LIMIT),
        name="inverse_y",
    )(table, spectra)


def eliminate(thick_ref, gap_ref, wave_ref, modes, right_side, lower_ref, half_ref):
    layers = thick_ref.shape[0]
    group = wave_ref.shape[1]
    nothing = jnp.zeros(wave_ref.shape, jnp.float32)

    def step(k, carry):
        excess, sums = carry
        thick, inv_gap = thick_ref[k], gap_ref[k]
        spare = wave_ref[...] * thick + excess
        inverse = 1.0 / (spare + inv_gap)
        lower = inverse * inv_gap
        rows = pl.ds(pl.multiple_of(k * group, group), group)
        lower_ref[:, rows, :] = lower
        following = []
        for mode in range(modes):
            total = right_side(mode, k, rows) * thick + sums[mode]
            half_ref[mode, :, rows, :] = total * inverse
            following.append(total * lower)
        return (lower * spare, tuple(following))

    lax.fori_loop(0, layers, step, (nothing, (nothing,) * modes))


def substitute(layers, modes, lower_ref, half_ref, use):
    tiles, all_rows, lanes = lower_ref.shape
    group = all_rows // layers
    nothing = jnp.zeros((tiles, group, lanes), jnp.float32)

    def step(back, values):
        k = layers - 1 - back
        rows = pl.ds(pl.multiple_of(k * group, group), group)
        lower = lower_ref[:, rows, :]
        found = []
        for mode in range(modes):
            value = half_ref[mode, :, rows, :] + lower * values[mode]
            use(mode, k, rows, value)
            found.append(value)
        return tuple(found)

    lax.fori_loop(0, layers, step, (nothing,) * modes)


def put_rows(ref, mode, start, group, result):
    layers = result.shape[0]
    for tile in range(ref.shape[1]):
        ref[mode, tile, pl.ds(start, layers, stride=group), :] = result[
            :, tile * LANES : (tile + 1) * LANES
        ]


def take_rows(ref, mode, start, group, layers):
    return jnp.concatenate(
        [
            ref[mode, tile, pl.ds(start, layers, stride=group), :].astype(jnp.bfloat16)
            for tile in range(ref.shape[1])
        ],
        axis=1,
    )


def block_ends_kernel(
    thick_ref, gap_ref, wave_ref, ends_ref, table_ref, rows_ref, strips_ref,
    spectrum_ref, out_ref, lower_ref, half_ref, end_ref,
):
    count, part, modes, _, layers = rows_ref.shape
    tiles, group, _ = wave_ref.shape
    if group > part:
        spectrum_ref[...] = jnp.zeros_like(spectrum_ref)

    def transform(b, carry):
        for mode in range(modes):
            left = jnp.concatenate(
                [rows_ref[c, b, mode] for c in range(count)] + [strips_ref[b, mode]], axis=0
            )
            put_rows(spectrum_ref, mode, b, group, contract(left, table_ref[...], 0, 0))
        return carry

    lax.fori_loop(0, part, transform, 0)
    eliminate(
        thick_ref, gap_ref, wave_ref, modes,
        lambda mode, k, rows: spectrum_ref[mode, :, rows, :], lower_ref, half_ref,
    )

    def use(mode, k, rows, value):
        for end in range(2):
            end_ref[end * modes + mode, :, pl.ds(k, 1), :] = jnp.sum(
                value * ends_ref[end], axis=1, keepdims=True
            )

    substitute(layers, modes, lower_ref, half_ref, use)
    for at in range(2 * modes):
        for tile in range(tiles):
            out_ref[tile * LANES : (tile + 1) * LANES, at * layers : (at + 1) * layers] = (
                end_ref[at, tile].T.astype(jnp.bfloat16)
            )


def interface_kernel(
    thick_ref, gap_ref, wave_ref, spread_ref, in_ref,
    out_ref, sum_ref, next_ref, spectrum_ref, lower_ref, half_ref,
):
    group = wave_ref.shape[1]
    layers = thick_ref.shape[0]
    blocks = spread_ref.shape[0] // 2
    modes = in_ref.shape[2] // (2 * layers)
    here = in_ref.shape[1] // blocks
    if group > here:
        spectrum_ref[...] = jnp.zeros_like(spectrum_ref)
    total = jnp.sum(in_ref[...].astype(jnp.float32), axis=0)
    for at in range(2 * modes):
        sum_ref[at] = total[:, at * layers : (at + 1) * layers]

    for a in range(here):
        picked = pl.ds(a, blocks, stride=here)
        for mode in range(modes):
            left = jnp.concatenate(
                [sum_ref[end * modes + mode, picked, :] for end in range(2)], axis=0
            ).astype(jnp.bfloat16)
            put_rows(spectrum_ref, mode, a, group, contract(left, spread_ref[...], 0, 0))
    eliminate(
        thick_ref, gap_ref, wave_ref, modes,
        lambda mode, k, rows: spectrum_ref[mode, :, rows, :], lower_ref, half_ref,
    )

    def use(mode, k, rows, value):
        half_ref[mode, :, rows, :] = value

    substitute(layers, modes, lower_ref, half_ref, use)
    for a in range(here):
        picked = pl.ds(a, blocks, stride=here)
        for mode in range(modes):
            solved = take_rows(half_ref, mode, a, group, layers)
            found = contract(spread_ref[...], solved, 1, 1)
            for end in range(2):
                next_ref[end * modes + mode, picked, :] = found[
                    end * blocks : (end + 1) * blocks
                ]
    inner = (blocks - 1) * here
    for mode in range(modes):
        first, last = mode, modes + mode
        next_ref[first, here:] = next_ref[first, here:] + sum_ref[last, :inner]
        next_ref[last, :inner] = next_ref[last, :inner] + sum_ref[first, here:]
    for copy in range(out_ref.shape[0]):
        for at in range(2 * modes):
            out_ref[copy, :, at * layers : (at + 1) * layers] = next_ref[at].astype(
                jnp.bfloat16
            )


def block_solve_kernel(
    thick_ref, gap_ref, wave_ref, ends_ref, table_ref, spectrum_ref, bound_ref, strips_ref,
    out_ref, mass_ref, lower_ref, half_ref, edge_ref,
):
    count, part, modes, x_local, layers = out_ref.shape
    tiles, group, _ = wave_ref.shape
    for at in range(2 * modes):
        for tile in range(tiles):
            edge_ref[at, tile] = (
                bound_ref[tile * LANES : (tile + 1) * LANES, at * layers : (at + 1) * layers]
                .astype(jnp.float32)
                .T
            )

    def right_side(mode, k, rows):
        total = spectrum_ref[mode, :, rows, :]
        for end in range(2):
            total = total + ends_ref[end] * edge_ref[end * modes + mode, :, pl.ds(k, 1), :]
        return total

    eliminate(thick_ref, gap_ref, wave_ref, modes, right_side, lower_ref, half_ref)

    def use(mode, k, rows, value):
        half_ref[mode, :, rows, :] = value

    substitute(layers, modes, lower_ref, half_ref, use)

    def transform(b, sums):
        found = []
        for mode in range(modes):
            solved = take_rows(half_ref, mode, b, group, layers)
            result = contract(table_ref[...], solved, 1, 1)
            for c in range(count):
                out_ref[c, b, mode] = result[c * x_local : (c + 1) * x_local].astype(
                    jnp.bfloat16
                )
            found.append(result[count * x_local :])
        weights = [strips_ref[b, mode].astype(jnp.float32) for mode in range(modes)]
        return tuple(
            sums[i * modes + j] + jnp.sum(found[i] * weights[j], axis=0, keepdims=True)
            for i in range(modes)
            for j in range(modes)
        )

    nothing = jnp.zeros((1, layers), jnp.float32)
    sums = lax.fori_loop(0, part, transform, (nothing,) * (modes * modes))
    for at in range(modes * modes):
        mass_ref[at : at + 1, :] = sums[at]


def shards(carried, velocity, strip_column, thick):
    modes, x_local, y_local, layers = carried.shape
    count_px = lax.axis_size("px")
    count_py = lax.axis_size("py")
    index_px = lax.axis_index("px")
    index_py = lax.axis_index("py")
    devices = count_px * count_py
    width_x = x_local * count_px
    width_y = y_local * count_py
    part = y_local // count_px
    group = -(-part // 8) * 8
    here = width_x // devices
    group_a = -(-here // 8) * 8
    strip_count = velocity.shape[1] * devices
    both = ("px", "py")

    code = jnp.stack([strip_column // 65536, strip_column // 256 % 256, strip_column % 256])
    code = jnp.pad(code.T, ((0, 0), (0, layers - 3))).astype(jnp.bfloat16)
    packed = jnp.concatenate([velocity, code[None]], axis=0).transpose(1, 0, 2)
    packed = jnp.broadcast_to(packed[None], (devices,) + packed.shape)
    gathered = lax.all_to_all(packed, both, split_axis=0, concat_axis=0, tiled=True)
    gathered = gathered.reshape(strip_count, modes + 1, layers)
    code = gathered[:, modes, :3].astype(jnp.int32)
    column = code[:, 0] * 65536 + code[:, 1] * 256 + code[:, 2]
    all_velocity = gathered[:, :modes].astype(jnp.float32)

    table_x = bf16(sine_table(width_x))
    table_y = jnp.asarray(sine_table(y_local).astype(np.float32))
    local_y = column % width_y - index_py * y_local
    inside = (local_y >= 0) & (local_y < y_local)
    factor = jnp.where(inside[:, None], table_y[jnp.clip(local_y, 0, y_local - 1)], 0.0)
    factor = lax.dynamic_slice_in_dim(factor, index_px * part, part, axis=1)
    strips = (factor.T[:, None, :, None] * all_velocity.transpose(1, 0, 2)[None]).astype(
        jnp.bfloat16
    )
    table_strips = jnp.concatenate([table_x, table_x[column // width_y]], axis=0)

    gap = jnp.concatenate([2.0 / (thick[:-1] + thick[1:]), 2.0 / thick[-1:]])
    wave_x = jnp.asarray(wave_numbers(width_x).astype(np.float32))
    wave_y = jnp.asarray(wave_numbers(width_y).astype(np.float32))
    wave_block = jnp.asarray(wave_numbers(y_local).astype(np.float32))
    wave_b = lax.dynamic_slice_in_dim(wave_block, index_px * part, part)
    wave_b = jnp.pad(wave_b, (0, group - part))[:, None] + wave_x.reshape(-1, 1, LANES)
    wave_a = lax.dynamic_slice_in_dim(wave_x, (index_px * count_py + index_py) * here, here)
    wave_a = jnp.pad(wave_a, (0, group_a - here))[:, None] + wave_y.reshape(-1, 1, LANES)
    ends = lax.dynamic_slice_in_dim(table_y[:, (0, y_local - 1)], index_px * part, part)
    ends = jnp.pad(ends.T, ((0, 0), (0, group - part)))[:, :, None]
    ends = jnp.broadcast_to(ends, (2, group, LANES))

    block_index = np.arange(count_py)
    full = sine_table(width_y)
    not_first = (block_index > 0)[:, None]
    not_last = (block_index < count_py - 1)[:, None]
    before = np.maximum(block_index * y_local - 1, 0)
    after = np.minimum((block_index + 1) * y_local, width_y - 1)
    spread = np.concatenate([full[before] * not_first, full[after] * not_last])

    params = pltpu.CompilerParams(vmem_limit_bytes=VMEM_LIMIT)
    vmem = pl.BlockSpec(memory_space=VMEM)
    smem = pl.BlockSpec(memory_space=SMEM)
    float32 = jnp.float32
    tiles_x, tiles_y = width_x // LANES, width_y // LANES

    spectra = forward_y(carried, count_px)
    rows = lax.all_to_all(spectra, "px", split_axis=0, concat_axis=0, tiled=True)
    spectrum, block_ends = pl.pallas_call(
        block_ends_kernel,
        in_specs=[smem, smem] + [vmem] * 5,
        out_specs=[vmem, vmem],
        out_shape=[
            jax.ShapeDtypeStruct((modes, tiles_x, layers * group, LANES), float32),
            jax.ShapeDtypeStruct((width_x, 2 * modes * layers), jnp.bfloat16),
        ],
        scratch_shapes=[
            pltpu.VMEM((tiles_x, layers * group, LANES), float32),
            pltpu.VMEM((modes, tiles_x, layers * group, LANES), float32),
            pltpu.VMEM((2 * modes, tiles_x, layers, LANES), float32),
        ],
        compiler_params=params,
        name="block_ends",
    )(thick, gap, wave_b, ends, table_strips, rows, strips)

    arrived = lax.all_to_all(block_ends, both, split_axis=0, concat_axis=0, tiled=True)
    outgoing = pl.pallas_call(
        interface_kernel,
        in_specs=[smem, smem] + [vmem] * 3,
        out_specs=vmem,
        out_shape=jax.ShapeDtypeStruct(
            (count_px, count_py * here, 2 * modes * layers), jnp.bfloat16
        ),
        scratch_shapes=[
            pltpu.VMEM((2 * modes, count_py * here, layers), float32),
            pltpu.VMEM((2 * modes, count_py * here, layers), float32),
            pltpu.VMEM((modes, tiles_y, layers * group_a, LANES), float32),
            pltpu.VMEM((tiles_y, layers * group_a, LANES), float32),
            pltpu.VMEM((modes, tiles_y, layers * group_a, LANES), float32),
        ],
        compiler_params=params,
        name="interface",
    )(
        thick, gap, wave_a, bf16(spread),
        arrived.reshape(count_px, count_py * here, 2 * modes * layers),
    )
    bounds = lax.all_to_all(
        outgoing.reshape(width_x, 2 * modes * layers), both, split_axis=0, concat_axis=0, tiled=True
    )

    returned, mass = pl.pallas_call(
        block_solve_kernel,
        in_specs=[smem, smem] + [vmem] * 6,
        out_specs=[vmem, vmem],
        out_shape=[
            jax.ShapeDtypeStruct((count_px, part, modes, x_local, layers), jnp.bfloat16),
            jax.ShapeDtypeStruct((modes * modes, layers), float32),
        ],
        scratch_shapes=[
            pltpu.VMEM((tiles_x, layers * group, LANES), float32),
            pltpu.VMEM((modes, tiles_x, layers * group, LANES), float32),
            pltpu.VMEM((2 * modes, tiles_x, layers, LANES), float32),
        ],
        compiler_params=params,
        name="block_solve",
    )(thick, gap, wave_b, ends, table_strips, spectrum, bounds, strips)
    back = lax.all_to_all(returned, "px", split_axis=0, concat_axis=0, tiled=True)
    pressure = inverse_y(back, y_local)
    local_mass = jnp.sum(mass * thick[None, :], axis=1).reshape(modes, modes)
    added_mass = lax.psum(local_mass, both) / (strip_count * layers)
    return (pressure, added_mass)


def solution(mesh):
    return jax.shard_map(
        shards,
        mesh=mesh,
        in_specs=(P(None, "px", "py", None), P(None, ("px", "py"), None), P(("px", "py")), P()),
        out_specs=(P(None, "px", "py", None), P()),
        check_vma=False,
    )
```

time: 900 us -> 277 us (0.31); the launches traced: 885 us -> 276 us
  local copies, waits for them, and re-layouts: 320 us -> 5.16 us
  waiting for transfers between devices: 188 us -> 39.3 us
  blocking collectives: 221 us -> 121 us
  other arithmetic: 102 us -> 6.44 us
  Pallas kernels: 0 us -> 85 us
  matrix products: 37.6 us -> 0 us
    slice x78 -> x1, local copies, waits for them, and re-layouts: 202 us -> 0.58 us  [shards(): gap = jnp.concatenate([2.0 / (thick[:-1] + thick[1:]), 2.0 / thick[-1:]])]
    all_to_all x3, waiting for transfers between devices: 188 us -> 39.3 us  [the longest x1 39.3 us: shards(): lax.all_to_all(spectra, 'px', split_axis=0, concat_axis=0, tiled=True)]
    pallas_call x0 -> x5, Pallas kernels: none -> 85 us  [the longest x1 22.4 us: shards(): pl.pallas_call(block_solve_kernel, in_specs=[smem, smem] + [vmem] * 6, ou...]
    all_to_all x1 -> x2, blocking collectives: 101 us -> 40.9 us  [the longest x1 21.2 us: shards(): lax.all_to_all(block_ends, both, split_axis=0, concat_axis=0, tiled=True)]
    reshape x3 -> x1, local copies, waits for them, and re-layouts: 51.2 us -> 0.08 us  [shards(): local_mass = jnp.sum(mass * thick[None, :], axis=1).reshape(modes, modes)]
    psum x1, blocking collectives: 36.9 us -> 79.8 us  [shards(): added_mass = lax.psum(local_mass, both) / (strip_count * layers)]
    unnamed x1 -> x0, blocking collectives: 42 us -> none
    all_gather x1 -> x0, blocking collectives: 40.7 us -> none  [shards(): lax.all_gather(velocity, ('px', 'py'), axis=1, tiled=True)]
  transfers between devices with their start and end apart: 3 -> 3, of which waited for: 2 -> 1; matrix products, arithmetic and copies ran while one was open for 16% -> 3% of each run, Pallas kernels for 0% -> 5%
where the time goes in v1:
time: 277 us; the launch traced here: 276 us
  blocking collectives  121 us (44%)
  Pallas kernels  85 us (31%)
  waiting for transfers between devices  39.3 us (14%)
  starting transfers between devices  17.3 us (6%)
  other arithmetic  6.44 us (2%)
  local copies, waits for them, and re-layouts  5.16 us (2%)
    psum x1, blocking collectives, shards(): added_mass = lax.psum(local_mass, both) / (strip_count * layers)  79.8 us
    all_to_all x1, waiting for transfers between devices, shards(): lax.all_to_all(spectra, 'px', split_axis=0, concat_axis=0, tiled=True)  39.3 us
    pallas_call x1, Pallas kernels, shards(): pl.pallas_call(block_solve_kernel, in_specs=[smem, smem] + [vmem] * 6, ou...  22.4 us
    pallas_call x1, Pallas kernels, shards(): pl.pallas_call(block_ends_kernel, in_specs=[smem, smem] + [vmem] * 5, out...  21.7 us
    all_to_all x1, blocking collectives, shards(): lax.all_to_all(block_ends, both, split_axis=0, concat_axis=0, tiled=True)  21.2 us
    all_to_all x1, blocking collectives, shards(): lax.all_to_all(outgoing.reshape(width_x, 2 * modes * layers), both, split...  19.7 us
    pallas_call x1, Pallas kernels, shards(): pl.pallas_call(interface_kernel, in_specs=[smem, smem] + [vmem] * 3, out_...  15.1 us
    pallas_call x1, Pallas kernels, inverse_y(): pl.pallas_call(inverse_y_kernel, grid=(modes, x_local // chunk), in_specs...  13 us
  transfers between devices with their start and end apart: 3, of which 1 were waited for; matrix products, arithmetic and copies ran while one was open for 3% of the time, Pallas kernels for 5%

profile of v1, /device:TPU:0, one launch (start us, length us, event | category | flops | bytes accessed | tf_op | source)
XLA Modules:
  0.0 275.5 jit_solution(16999934522953061923)
XLA Ops:
  0.6 0.7 convert_bitcast_fusion.1
  1.4 0.7 maximum_bitcast_fusion
  2.1 0.7 broadcast_in_dim.41
  2.8 7.3 %all-to-all-start = ((bf16[32,4,3,128]{3,1,2,0:T(4,128)(2,1)}), bf16[32,4,3,128]{3,1,2,0:T(4,128)(2,1)S(1)}, u32[]{:S(2)}, u32[]{:S(2)}) async-start(bf16[32,4,3,128]{3,1,2,0:T(4,128)(2,1)} %broadcast_in_dim.41), calls=%async_computation | async-start | bytes 196608 | tf_op jit(solution)/shard_map/all_to_all | solution.py:330
  10.1 12.8 %forward_y.1 = bf16[4,16,2,128,128]{4,3,2,1,0:T(8,128)(2,1)} custom-call(bf16[256,256]{1,0:T(8,128)(2,1)} %constant.123.clone.table_ref, bf16[2,128,64,128]{3,2,1,0:T(8,128)(2,1)} %grid_ref.1), custom_call_target="tpu_custom_call" | custom-call | tf_op jit(solution)/shard_map/forward_y/pallas_call | solution.py:77
  23.0 5.1 %all-to-all-start.1 = ((bf16[4,16,2,128,128]{4,3,2,1,0:T(8,128)(2,1)}), bf16[4,16,2,128,128]{4,3,2,1,0:T(8,128)(2,1)}, u32[]{:S(2)}, u32[]{:S(2)}) async-start(bf16[4,16,2,128,128]{4,3,2,1,0:T(8,128)(2,1)} %forward_y.1), calls=%async_computation.1 | async-start | bytes 8388608 | tf_op jit(solution)/shard_map/all_to_all | solution.py:374
  28.1 0.6 slice.26
  29.3 0.8 dynamic_slice.15
  30.8 0.6 pad_maximum_fusion.1.gap_ref
  31.5 0.7 broadcast_add_fusion
  32.6 0.6 gather_fusion.2
  33.7 0.8 gather_fusion.1
  34.5 0.9 pad_maximum_fusion.table_ref
  35.4 1.4 multiply_convert_fusion.strips_ref
  36.8 39.3 %all-to-all-done.1.rows_ref = bf16[4,16,2,128,128]{4,3,2,1,0:T(8,128)(2,1)} async-done(((bf16[4,16,2,128,128]{4,3,2,1,0:T(8,128)(2,1)}), bf16[4,16,2,128,128]{4,3,2,1,0:T(8,128)(2,1)}, u32[]{:S(2)}, u32[]{:S(2)}) %all-to-all-start.1) | async-done | bytes 4194336 | tf_op jit(solution)/shard_map/all_to_all | solution.py:374
  76.1 0.7 broadcast_in_dim.23.ends_ref
  76.8 21.7 %block_ends.1 = (f32[2,4,2048,128]{3,2,1,0:T(8,128)}, bf16[512,512]{1,0:T(8,128)(2,1)}) custom-call(f32[128]{0:T(128)} %thick_ref.5, f32[128]{0:T(128)} %pad_maximum_fusion.1.gap_ref, f32[4,16,128]{2,1,0:T(8,128)} %get-tuple-element.13.wave_ref, f32[2,16,128]{2,1,0:T(8,128)} %broadcast_in_dim.23.ends_ref, bf16[640,512]{1,0:T(8,128)(2,1)} %pad_maximum_fusion.table_ref, ...), custom_call_target="tpu_custom_call" | custom-call | tf_op jit(solution)/shard_map/block_ends/pallas_call | solution.py:375
  98.5 21.2 %all_to_all.35 = bf16[32,16,512]{2,1,0:T(8,128)(2,1)} all-to-all(bf16[32,16,512]{2,1,0:T(8,128)(2,1)} %bitcast.29), channel_id=1, replica_groups=mesh['px'=4,'py'=8] {'px','py'}, dimensions={0} | all-to-all | bytes 1048576 | tf_op jit(solution)/shard_map/all_to_all | solution.py:392
  119.7 15.1 %interface.1 = bf16[4,128,512]{2,1,0:T(8,128)(2,1)} custom-call(f32[128]{0:T(128)} %thick_ref.5, f32[128]{0:T(128)} %pad_maximum_fusion.1.gap_ref, f32[4,16,128]{2,1,0:T(8,128)} %get-tuple-element.12.wave_ref, bf16[16,512]{1,0:T(8,128)(2,1)} %constant.124.clone.spread_ref, bf16[4,128,512]{2,1,0:T(8,128)(2,1)} %bitcast.27), custom_call_target="tpu_custom_call" | custom-call | tf_op jit(solution)/shard_map/interface/pallas_call | solution.py:393
  134.9 19.7 %all_to_all.36 = bf16[32,16,512]{2,1,0:T(8,128)(2,1)} all-to-all(bf16[32,16,512]{2,1,0:T(8,128)(2,1)} %bitcast.28), channel_id=1, replica_groups=mesh['px'=4,'py'=8] {'px','py'}, dimensions={0} | all-to-all | bytes 1048576 | tf_op jit(solution)/shard_map/all_to_all | solution.py:413
  154.5 22.4 %block_solve.1 = (bf16[4,16,2,128,128]{4,3,2,1,0:T(8,128)(2,1)}, f32[4,128]{1,0:T(4,128)}) custom-call(f32[128]{0:T(128)} %thick_ref.5, f32[128]{0:T(128)} %pad_maximum_fusion.1.gap_ref, f32[4,16,128]{2,1,0:T(8,128)} %get-tuple-element.13.wave_ref, f32[2,16,128]{2,1,0:T(8,128)} %broadcast_in_dim.23.ends_ref, bf16[640,512]{1,0:T(8,128)(2,1)} %pad_maximum_fusion.table_ref, ...), custom_call_target="tpu_custom_call" | custom-call | tf_op jit(solution)/shard_map/block_solve/pallas_call | solution.py:417
  177.0 5.0 %all-to-all-start.4 = ((bf16[4,16,2,128,128]{4,3,2,1,0:T(8,128)(2,1)}), bf16[4,16,2,128,128]{4,3,2,1,0:T(8,128)(2,1)}, u32[]{:S(2)}, u32[]{:S(2)}) async-start(bf16[4,16,2,128,128]{4,3,2,1,0:T(8,128)(2,1)} %get-tuple-element.8), calls=%async_computation.4 | async-start | bytes 8388608 | tf_op jit(solution)/shard_map/all_to_all | solution.py:433
  182.2 79.8 %psum.7 = f32[2,2]{1,0:T(2,128)S(1)} all-reduce(f32[2,2]{1,0:T(2,128)S(1)} %reshape.35), channel_id=1, replica_groups=mesh['px'=4,'py'=8] {'px','py'}, use_global_device_ids=true, to_apply=%region_1.2 | all-reduce | flops 4 | bytes 32 | tf_op jit(solution)/shard_map/psum | solution.py:436
  262.6 13.0 %inverse_y.1 = bf16[2,128,64,128]{3,2,1,0:T(8,128)(2,1)} custom-call(bf16[256,256]{1,0:T(8,128)(2,1)} %constant.123.clone.table_ref, bf16[4,16,2,128,128]{4,3,2,1,0:T(8,128)(2,1)} %all-to-all-done.4.in_ref), custom_call_target="tpu_custom_call" | custom-call | tf_op jit(solution)/shard_map/inverse_y/pallas_call | solution.py:96
  (40 shorter events, 2.5 us)
Async XLA Ops:
  2.8 20.2 %all-to-all-start = ((bf16[32,4,3,128]{3,1,2,0:T(4,128)(2,1)}), bf16[32,4,3,128]{3,1,2,0:T(4,128)(2,1)S(1)}, u32[]{:S(2)}, u32[]{:S(2)}) async-start(bf16[32,4,3,128]{3,1,2,0:T(4,128)(2,1)} %broadcast_in_dim.41), calls=%async_computation | async-start | bytes 196608 | tf_op jit(solution)/shard_map/all_to_all | solution.py:330
  22.9 5.1 %copy-start.3 = (f32[128]{0:T(128)S(1)}, f32[128]{0:T(128)}, u32[]{:S(2)}) copy-start(f32[128]{0:T(128)} %thick_ref.5) | copy-start | bytes 1540
  22.9 7.2 %copy-start.7 = (f32[64]{0:T(128)S(1)}, f32[64]{0:T(128)}, u32[]{:S(2)}) copy-start(f32[64]{0:T(128)} %constant.121.clone) | copy-start | bytes 772
  22.9 7.3 %copy-start.2 = (f32[64,64]{0,1:T(8,128)S(1)}, f32[64,64]{0,1:T(8,128)}, u32[]{:S(2)}) copy-start(f32[64,64]{0,1:T(8,128)} %constant.119.clone) | copy-start | bytes 49156
  22.9 8.6 %copy-start.5 = (f32[4,128]{1,0:T(4,128)S(1)}, f32[4,128]{1,0:T(4,128)}, u32[]{:S(2)}) copy-start(f32[4,128]{1,0:T(4,128)} %constant.129) | copy-start | bytes 6148
  23.0 9.7 %copy-start = (f32[64,64]{1,0:T(8,128)S(1)}, f32[64,64]{1,0:T(8,128)}, u32[]{:S(2)}) copy-start(f32[64,64]{1,0:T(8,128)} %constant.130) | copy-start | bytes 49156
  23.0 10.7 %copy-start.1 = (bf16[512,512]{1,0:T(8,128)(2,1)S(1)}, bf16[512,512]{1,0:T(8,128)(2,1)}, u32[]{:S(2)}) copy-start(bf16[512,512]{1,0:T(8,128)(2,1)} %constant.118.clone) | copy-start | bytes 1572868
  23.0 53.2 %all-to-all-start.1 = ((bf16[4,16,2,128,128]{4,3,2,1,0:T(8,128)(2,1)}), bf16[4,16,2,128,128]{4,3,2,1,0:T(8,128)(2,1)}, u32[]{:S(2)}, u32[]{:S(2)}) async-start(bf16[4,16,2,128,128]{4,3,2,1,0:T(8,128)(2,1)} %forward_y.1), calls=%async_computation.1 | async-start | bytes 8388608 | tf_op jit(solution)/shard_map/all_to_all | solution.py:374
  176.9 5.0 %copy-start.4 = (f32[128]{0:T(128)S(1)}, f32[128]{0:T(128)}, u32[]{:S(2)}) copy-start(f32[128]{0:T(128)} %thick_ref.5) | copy-start | bytes 1540
  177.0 5.0 %copy-start.6 = (f32[4,128]{1,0:T(4,128)S(1)}, f32[4,128]{1,0:T(4,128)}, u32[]{:S(2)}) copy-start(f32[4,128]{1,0:T(4,128)} %get-tuple-element.9) | copy-start | bytes 6148
  177.0 85.6 %all-to-all-start.4 = ((bf16[4,16,2,128,128]{4,3,2,1,0:T(8,128)(2,1)}), bf16[4,16,2,128,128]{4,3,2,1,0:T(8,128)(2,1)}, u32[]{:S(2)}, u32[]{:S(2)}) async-start(bf16[4,16,2,128,128]{4,3,2,1,0:T(8,128)(2,1)} %get-tuple-element.8), calls=%async_computation.4 | async-start | bytes 8388608 | tf_op jit(solution)/shard_map/all_to_all | solution.py:433

commit v2 on v1

--- a/solution.py
+++ b/solution.py
@@ -10,7 +10,7 @@
 from jax.experimental.pallas import tpu as pltpu
 from jax.sharding import PartitionSpec as P
 
-VMEM_LIMIT = 56 * 1024 * 1024
+VMEM_LIMIT = 36 * 1024 * 1024
 VMEM = pltpu.MemorySpace.VMEM
 SMEM = pltpu.MemorySpace.SMEM
 LANES = 128
@@ -91,7 +91,7 @@
 
 def inverse_y(spectra, rows):
     count, part, modes, x_local, layers = spectra.shape
-    chunk = 16
+    chunk = min(64, x_local)
     table = y_table(rows)
     return pl.pallas_call(
         inverse_y_kernel,
@@ -327,6 +327,7 @@
     code = jnp.pad(code.T, ((0, 0), (0, layers - 3))).astype(jnp.bfloat16)
     packed = jnp.concatenate([velocity, code[None]], axis=0).transpose(1, 0, 2)
     packed = jnp.broadcast_to(packed[None], (devices,) + packed.shape)
+    spectra, packed = lax.optimization_barrier((forward_y(carried, count_px), packed))
     gathered = lax.all_to_all(packed, both, split_axis=0, concat_axis=0, tiled=True)
     gathered = gathered.reshape(strip_count, modes + 1, layers)
     code = gathered[:, modes, :3].astype(jnp.int32)
@@ -370,7 +371,6 @@
     float32 = jnp.float32
     tiles_x, tiles_y = width_x // LANES, width_y // LANES
 
-    spectra = forward_y(carried, count_px)
     rows = lax.all_to_all(spectra, "px", split_axis=0, concat_axis=0, tiled=True)
     spectrum, block_ends = pl.pallas_call(
         block_ends_kernel,
@@ -433,7 +433,9 @@
     back = lax.all_to_all(returned, "px", split_axis=0, concat_axis=0, tiled=True)
     pressure = inverse_y(back, y_local)
     local_mass = jnp.sum(mass * thick[None, :], axis=1).reshape(modes, modes)
-    added_mass = lax.psum(local_mass, both) / (strip_count * layers)
+    every_mass = jnp.broadcast_to(local_mass[None], (devices, modes, modes))
+    every_mass = lax.all_to_all(every_mass, both, split_axis=0, concat_axis=0, tiled=True)
+    added_mass = jnp.sum(every_mass, axis=0) / (strip_count * layers)
     return (pressure, added_mass)
 
 

time: 277 us -> 242 us (0.87)
  blocking collectives: 121 us -> 60.8 us
  waiting for transfers between devices: 39.3 us -> 89.6 us
  Pallas kernels: 85 us -> 64.7 us
  starting transfers between devices: 17.3 us -> 9.96 us
  local copies, waits for them, and re-layouts: 5.16 us -> 11 us
  other arithmetic: 6.44 us -> 3.45 us
    psum x1 -> x0, blocking collectives: 79.8 us -> none  [shards(): added_mass = lax.psum(local_mass, both) / (strip_count * layers)]
    all_to_all x1, waiting for transfers between devices: 0.01 us -> 47.3 us  [shards(): lax.all_to_all(returned, 'px', split_axis=0, concat_axis=0, tiled=True)]
    all_to_all x0 -> x2, blocking collectives: none -> 24.1 us  [the longest x1 14.9 us: shards(): lax.all_to_all(packed, both, split_axis=0, concat_axis=0, tiled=True)]
    all_to_all x1 -> x0, starting transfers between devices: 7.3 us -> none  [shards(): lax.all_to_all(packed, both, split_axis=0, concat_axis=0, tiled=True)]
    unnamed x16 -> x24, local copies, waits for them, and re-layouts: 0.04 us -> 7.15 us
    pallas_call x1, Pallas kernels: 12.8 us -> 6.61 us  [forward_y(): pl.pallas_call(forward_y_kernel, grid=(modes, x_local // chunk), in_specs...]
    pallas_call x1, Pallas kernels: 22.4 us -> 17 us  [shards(): pl.pallas_call(block_solve_kernel, in_specs=[smem, smem] + [vmem] * 6, ou...]
    pallas_call x1, Pallas kernels: 21.7 us -> 17.8 us  [shards(): pl.pallas_call(block_ends_kernel, in_specs=[smem, smem] + [vmem] * 5, out...]
  transfers between devices with their start and end apart: 3 -> 2, of which waited for: 1 -> 2; matrix products, arithmetic and copies ran while one was open for 3% -> 2% of each run, Pallas kernels for 5% -> 0%
where the time goes in v2:
time: 242 us; the launch traced here: 241 us
  waiting for transfers between devices  89.6 us (37%)
  Pallas kernels  64.7 us (27%)
  blocking collectives  60.8 us (25%)
  local copies, waits for them, and re-layouts  11 us (5%)
  starting transfers between devices  9.96 us (4%)
  other arithmetic  3.45 us (1%)
    all_to_all x1, waiting for transfers between devices, shards(): lax.all_to_all(returned, 'px', split_axis=0, concat_axis=0, tiled=True)  47.3 us
    all_to_all x1, waiting for transfers between devices, shards(): lax.all_to_all(spectra, 'px', split_axis=0, concat_axis=0, tiled=True)  42.2 us
    all_to_all x1, blocking collectives, shards(): lax.all_to_all(outgoing.reshape(width_x, 2 * modes * layers), both, split...  18.4 us
    all_to_all x1, blocking collectives, shards(): lax.all_to_all(block_ends, both, split_axis=0, concat_axis=0, tiled=True)  18.3 us
    pallas_call x1, Pallas kernels, shards(): pl.pallas_call(block_ends_kernel, in_specs=[smem, smem] + [vmem] * 5, out...  17.8 us
    pallas_call x1, Pallas kernels, shards(): pl.pallas_call(block_solve_kernel, in_specs=[smem, smem] + [vmem] * 6, ou...  17 us
    all_to_all x1, blocking collectives, shards(): lax.all_to_all(packed, both, split_axis=0, concat_axis=0, tiled=True)  14.9 us
    pallas_call x1, Pallas kernels, shards(): pl.pallas_call(interface_kernel, in_specs=[smem, smem] + [vmem] * 3, out_...  13.8 us
  transfers between devices with their start and end apart: 2, of which 2 were waited for; matrix products, arithmetic and copies ran while one was open for 2% of the time, Pallas kernels for 0%

profile of v2, /device:TPU:0, one launch (start us, length us, event | category | flops | bytes accessed | tf_op | source)
XLA Modules:
  0.0 241.1 jit_solution(6237118304328175586)
XLA Ops:
  0.6 0.7 convert_bitcast_fusion.1
  1.4 0.7 maximum_bitcast_fusion
  2.1 2.2 copy-done.1
  4.3 0.9 copy-done.3
  5.2 6.6 %forward_y.1 = bf16[4,16,2,128,128]{4,3,2,1,0:T(8,128)(2,1)S(1)} custom-call(bf16[256,256]{1,0:T(8,128)(2,1)S(1)} %copy-done.3, bf16[2,128,64,128]{3,2,1,0:T(8,128)(2,1)S(1)} %copy-done.1), custom_call_target="tpu_custom_call" | custom-call | tf_op jit(solution)/shard_map/forward_y/pallas_call | solution.py:77
  11.8 2.0 copy-done
  13.9 14.9 %all_to_all.40 = bf16[32,4,3,128]{3,1,2,0:T(4,128)(2,1)S(1)} all-to-all(bf16[32,4,3,128]{3,1,2,0:T(4,128)(2,1)S(1)} %broadcast_in_dim.48), channel_id=1, replica_groups=mesh['px'=4,'py'=8] {'px','py'}, dimensions={0} | all-to-all | bytes 196608 | tf_op jit(solution)/shard_map/all_to_all | solution.py:331
  28.8 5.0 %all-to-all-start.1 = ((bf16[4,16,2,128,128]{4,3,2,1,0:T(8,128)(2,1)}), bf16[4,16,2,128,128]{4,3,2,1,0:T(8,128)(2,1)}, u32[]{:S(2)}, u32[]{:S(2)}) async-start(bf16[4,16,2,128,128]{4,3,2,1,0:T(8,128)(2,1)} %copy-done), calls=%async_computation.1 | async-start | bytes 8388608 | tf_op jit(solution)/shard_map/all_to_all | solution.py:374
  33.8 0.6 slice.26
  35.1 0.8 dynamic_slice.15
  37.2 0.6 gather_fusion.2
  38.3 0.8 gather_fusion.1
  39.6 42.2 %all-to-all-done.1.rows_ref = bf16[4,16,2,128,128]{4,3,2,1,0:T(8,128)(2,1)} async-done(((bf16[4,16,2,128,128]{4,3,2,1,0:T(8,128)(2,1)}), bf16[4,16,2,128,128]{4,3,2,1,0:T(8,128)(2,1)}, u32[]{:S(2)}, u32[]{:S(2)}) %all-to-all-start.1) | async-done | bytes 4194336 | tf_op jit(solution)/shard_map/all_to_all | solution.py:374
  81.9 17.8 %block_ends.1 = (f32[2,4,2048,128]{3,2,1,0:T(8,128)S(1)}, bf16[512,512]{1,0:T(8,128)(2,1)S(1)}) custom-call(f32[128]{0:T(128)S(1)} %copy-done.6, f32[128]{0:T(128)S(1)} %pad_maximum_fusion.1.gap_ref, f32[4,16,128]{2,1,0:T(8,128)S(1)} %get-tuple-element.17.wave_ref, f32[2,16,128]{2,1,0:T(8,128)S(1)} %broadcast_in_dim.46.ends_ref, ...), custom_call_target="tpu_custom_call" | custom-call | tf_op jit(solution)/shard_map/block_ends/pallas_call | solution.py:375
  99.6 18.3 %all_to_all.41 = bf16[32,16,512]{2,1,0:T(8,128)(2,1)S(1)} all-to-all(bf16[32,16,512]{2,1,0:T(8,128)(2,1)S(1)} %bitcast.29), channel_id=1, replica_groups=mesh['px'=4,'py'=8] {'px','py'}, dimensions={0} | all-to-all | bytes 1048576 | tf_op jit(solution)/shard_map/all_to_all | solution.py:392
  118.0 13.8 %interface.1 = bf16[4,128,512]{2,1,0:T(8,128)(2,1)S(1)} custom-call(f32[128]{0:T(128)S(1)} %copy-done.6, f32[128]{0:T(128)S(1)} %pad_maximum_fusion.1.gap_ref, f32[4,16,128]{2,1,0:T(8,128)S(1)} %get-tuple-element.16.wave_ref, bf16[16,512]{1,0:T(8,128)(2,1)S(1)} %copy-done.5, bf16[4,128,512]{2,1,0:T(8,128)(2,1)S(1)} %bitcast.27), custom_call_target="tpu_custom_call" | custom-call | tf_op jit(solution)/shard_map/interface/pallas_call | solution.py:393
  131.8 18.4 %all_to_all.42 = bf16[32,16,512]{2,1,0:T(8,128)(2,1)S(1)} all-to-all(bf16[32,16,512]{2,1,0:T(8,128)(2,1)S(1)} %bitcast.28), channel_id=1, replica_groups=mesh['px'=4,'py'=8] {'px','py'}, dimensions={0} | all-to-all | bytes 1048576 | tf_op jit(solution)/shard_map/all_to_all | solution.py:413
  150.1 17.0 %block_solve.1 = (bf16[4,16,2,128,128]{4,3,2,1,0:T(8,128)(2,1)S(1)}, f32[4,128]{1,0:T(4,128)S(1)}) custom-call(f32[128]{0:T(128)S(1)} %copy-done.6, f32[128]{0:T(128)S(1)} %pad_maximum_fusion.1.gap_ref, f32[4,16,128]{2,1,0:T(8,128)S(1)} %get-tuple-element.17.wave_ref, f32[2,16,128]{2,1,0:T(8,128)S(1)} %broadcast_in_dim.46.ends_ref, ...), custom_call_target="tpu_custom_call" | custom-call | tf_op jit(solution)/shard_map/block_solve/pallas_call | solution.py:417
  167.1 2.0 copy-done.2
  169.4 9.3 %all_to_all.43 = f32[32,2,2]{2,1,0:T(2,128)S(1)} all-to-all(f32[32,2,2]{2,1,0:T(2,128)S(1)} %broadcast_in_dim.53), channel_id=1, replica_groups=mesh['px'=4,'py'=8] {'px','py'}, dimensions={0} | all-to-all | bytes 1024 | tf_op jit(solution)/shard_map/all_to_all | solution.py:437
  178.6 5.0 %all-to-all-start.4 = ((bf16[4,16,2,128,128]{4,3,2,1,0:T(8,128)(2,1)}), bf16[4,16,2,128,128]{4,3,2,1,0:T(8,128)(2,1)}, u32[]{:S(2)}, u32[]{:S(2)}) async-start(bf16[4,16,2,128,128]{4,3,2,1,0:T(8,128)(2,1)} %copy-done.2), calls=%async_computation.4 | async-start | bytes 8388608 | tf_op jit(solution)/shard_map/all_to_all | solution.py:433
  183.6 0.6 broadcast_multiply_fusion
  184.2 47.3 %all-to-all-done.4.in_ref = bf16[4,16,2,128,128]{4,3,2,1,0:T(8,128)(2,1)} async-done(((bf16[4,16,2,128,128]{4,3,2,1,0:T(8,128)(2,1)}), bf16[4,16,2,128,128]{4,3,2,1,0:T(8,128)(2,1)}, u32[]{:S(2)}, u32[]{:S(2)}) %all-to-all-start.4) | async-done | bytes 4194336 | tf_op jit(solution)/shard_map/all_to_all | solution.py:433
  231.6 9.5 %inverse_y.1 = bf16[2,128,64,128]{3,2,1,0:T(8,128)(2,1)} custom-call(bf16[256,256]{1,0:T(8,128)(2,1)S(1)} %copy-done.4, bf16[4,16,2,128,128]{4,3,2,1,0:T(8,128)(2,1)} %all-to-all-done.4.in_ref), custom_call_target="tpu_custom_call" | custom-call | tf_op jit(solution)/shard_map/inverse_y/pallas_call | solution.py:96
  (49 shorter events, 2.6 us)
Async XLA Ops:
  2.1 2.2 copy-start.1
  4.3 0.9 copy-start.3
  11.8 2.0 copy-start
  28.8 5.0 %copy-start.6 = (f32[128]{0:T(128)S(1)}, f32[128]{0:T(128)}, u32[]{:S(2)}) copy-start(f32[128]{0:T(128)} %thick_ref.5) | copy-start | bytes 1540
  28.8 7.1 %copy-start.11 = (f32[64]{0:T(128)S(1)}, f32[64]{0:T(128)}, u32[]{:S(2)}) copy-start(f32[64]{0:T(128)} %constant.122.clone) | copy-start | bytes 772
  28.8 7.2 %copy-start.9 = (f32[64,64]{0,1:T(8,128)S(1)}, f32[64,64]{0,1:T(8,128)}, u32[]{:S(2)}) copy-start(f32[64,64]{0,1:T(8,128)} %constant.120.clone) | copy-start | bytes 49156
  28.8 8.0 %copy-start.10 = (f32[4,128]{1,0:T(4,128)S(1)}, f32[4,128]{1,0:T(4,128)}, u32[]{:S(2)}) copy-start(f32[4,128]{1,0:T(4,128)} %constant.129) | copy-start | bytes 6148
  28.8 8.4 %copy-start.7 = (f32[64,64]{1,0:T(8,128)S(1)}, f32[64,64]{1,0:T(8,128)}, u32[]{:S(2)}) copy-start(f32[64,64]{1,0:T(8,128)} %constant.130) | copy-start | bytes 49156
  28.8 9.5 %copy-start.8 = (bf16[512,512]{1,0:T(8,128)(2,1)S(1)}, bf16[512,512]{1,0:T(8,128)(2,1)}, u32[]{:S(2)}) copy-start(bf16[512,512]{1,0:T(8,128)(2,1)} %constant.119.clone) | copy-start | bytes 1572868
  28.8 53.0 %all-to-all-start.1 = ((bf16[4,16,2,128,128]{4,3,2,1,0:T(8,128)(2,1)}), bf16[4,16,2,128,128]{4,3,2,1,0:T(8,128)(2,1)}, u32[]{:S(2)}, u32[]{:S(2)}) async-start(bf16[4,16,2,128,128]{4,3,2,1,0:T(8,128)(2,1)} %copy-done), calls=%async_computation.1 | async-start | bytes 8388608 | tf_op jit(solution)/shard_map/all_to_all | solution.py:374
  39.2 78.8 %copy-start.5 = (bf16[16,512]{1,0:T(8,128)(2,1)S(1)}, bf16[16,512]{1,0:T(8,128)(2,1)}, u32[]{:S(2)}) copy-start(bf16[16,512]{1,0:T(8,128)(2,1)} %constant.124.clone.spread_ref) | copy-start | bytes 49156
  167.1 2.0 copy-start.2
  178.6 52.9 %copy-start.4 = (bf16[256,256]{1,0:T(8,128)(2,1)S(1)}, bf16[256,256]{1,0:T(8,128)(2,1)}, u32[]{:S(2)}) copy-start(bf16[256,256]{1,0:T(8,128)(2,1)} %constant.118.clone.table_ref) | copy-start | bytes 393220
  178.6 52.9 %all-to-all-start.4 = ((bf16[4,16,2,128,128]{4,3,2,1,0:T(8,128)(2,1)}), bf16[4,16,2,128,128]{4,3,2,1,0:T(8,128)(2,1)}, u32[]{:S(2)}, u32[]{:S(2)}) async-start(bf16[4,16,2,128,128]{4,3,2,1,0:T(8,128)(2,1)} %copy-done.2), calls=%async_computation.4 | async-start | bytes 8388608 | tf_op jit(solution)/shard_map/all_to_all | solution.py:433

commit v3 on v1

v3 whole, which is shorter than its diff:
```python
import functools
import math

import jax
import jax.numpy as jnp
import ml_dtypes
import numpy as np
from jax import lax
from jax.experimental import pallas as pl
from jax.experimental.pallas import tpu as pltpu
from jax.sharding import PartitionSpec as P

VMEM_LIMIT = 58 * 1024 * 1024
VMEM = pltpu.MemorySpace.VMEM
SMEM = pltpu.MemorySpace.SMEM
LANES = 128
CHUNK = 64


def sine_table(length):
    steps = np.arange(1, length + 1)
    product = steps[:, None] * steps[None, :] % (2 * (length + 1))
    return math.sqrt(2.0 / (length + 1)) * np.sin(product * (math.pi / (length + 1)))


def wave_numbers(length):
    return 4.0 * np.sin(np.arange(1, length + 1) * (math.pi / (2 * (length + 1)))) ** 2


def bf16(table):
    return jnp.asarray(table.astype(ml_dtypes.bfloat16))


def contract(left, right, left_dim, right_dim):
    return lax.dot_general(
        left, right, (((left_dim,), (right_dim,)), ((), ())), preferred_element_type=jnp.float32
    )


def pitch_of(group):
    return group if group // 8 % 2 else group + 8


def forward_y_kernel(table_ref, grid_ref, out_ref, scratch):
    _, x_chunk, rows, layers = grid_ref.shape
    pieces, part = out_ref.shape[:2]
    group = table_ref.shape[0] // rows
    for start in range(0, x_chunk, group):
        block = grid_ref[0, start : start + group].reshape(group * rows, layers)
        result = contract(table_ref[...], block, 1, 0)
        for at in range(group):
            scratch[pl.ds(start + at, rows, stride=pitch_of(x_chunk)), :] = result[
                at * rows : (at + 1) * rows
            ]
    for b in range(rows):
        begin = b * pitch_of(x_chunk)
        out_ref[b // part, b % part] = scratch[begin : begin + x_chunk, :].astype(jnp.bfloat16)


def inverse_y_kernel(table_ref, in_ref, out_ref, scratch):
    _, x_chunk, rows, layers = out_ref.shape
    group = table_ref.shape[0] // rows
    part = in_ref.shape[1]
    for b in range(rows):
        begin = b * pitch_of(x_chunk)
        scratch[begin : begin + x_chunk, :] = in_ref[b // part, b % part].astype(jnp.float32)
    for start in range(0, x_chunk, group):
        block = jnp.concatenate(
            [
                scratch[pl.ds(start + at, rows, stride=pitch_of(x_chunk)), :]
                for at in range(group)
            ],
            axis=0,
        ).astype(jnp.bfloat16)
        result = contract(table_ref[...], block, 1, 0)
        out_ref[0, start : start + group] = result.reshape(group, rows, layers).astype(
            jnp.bfloat16
        )


def y_table(rows):
    group = max(1, 256 // rows)
    return bf16(np.kron(np.eye(group), sine_table(rows)))


def forward_y(carried, count):
    modes, x_local, rows, layers = carried.shape
    chunk = min(CHUNK, x_local)
    pieces = count // modes
    part = rows // pieces
    table = y_table(rows)
    return pl.pallas_call(
        forward_y_kernel,
        grid=(modes, x_local // chunk),
        in_specs=[
            pl.BlockSpec(table.shape, lambda m, i: (0, 0)),
            pl.BlockSpec((1, chunk, rows, layers), lambda m, i: (m, i, 0, 0)),
        ],
        out_specs=pl.BlockSpec((pieces, part, chunk, layers), lambda m, i: (m, 0, i, 0)),
        out_shape=jax.ShapeDtypeStruct((count, part, x_local, layers), jnp.bfloat16),
        scratch_shapes=[pltpu.VMEM((rows * pitch_of(chunk), layers), jnp.float32)],
        compiler_params=pltpu.CompilerParams(vmem_limit_bytes=VMEM_LIMIT),
        name="forward_y",
    )(table, carried)


def inverse_y(spectra, rows):
    count, part, x_local, layers = spectra.shape
    pieces = rows // part
    modes = count // pieces
    chunk = min(CHUNK, x_local)
    table = y_table(rows)
    return pl.pallas_call(
        inverse_y_kernel,
        grid=(modes, x_local // chunk),
        in_specs=[
            pl.BlockSpec(table.shape, lambda m, i: (0, 0)),
            pl.BlockSpec((pieces, part, chunk, layers), lambda m, i: (m, 0, i, 0)),
        ],
        out_specs=pl.BlockSpec((1, chunk, rows, layers), lambda m, i: (m, i, 0, 0)),
        out_shape=jax.ShapeDtypeStruct((modes, x_local, rows, layers), jnp.bfloat16),
        scratch_shapes=[pltpu.VMEM((rows * pitch_of(chunk), layers), jnp.float32)],
        compiler_params=pltpu.CompilerParams(vmem_limit_bytes=VMEM_LIMIT),
        name="inverse_y",
    )(table, spectra)


def at_layer(k, group, pitch):
    return pl.ds(pl.multiple_of(k * pitch, 8), group)


def eliminate(
    thick_ref, gap_ref, wave_ref, modes, right_side, lower_ref, half_ref, ready=(None,)
):
    layers = thick_ref.shape[0]
    group = wave_ref.shape[1]
    nothing = jnp.zeros(wave_ref.shape, jnp.float32)

    def step(k, carry):
        excess, sums = carry
        thick, inv_gap = thick_ref[k], gap_ref[k]
        spare = wave_ref[...] * thick + excess
        inverse = 1.0 / (spare + inv_gap)
        lower = inverse * inv_gap
        rows = at_layer(k, group, pitch_of(group))
        lower_ref[:, at_layer(k, group, group), :] = lower
        following = []
        for mode in range(modes):
            total = right_side(mode, k, rows) * thick + sums[mode]
            half_ref[mode, :, rows, :] = total * inverse
            following.append(total * lower)
        return (lower * spare, tuple(following))

    carry = (nothing, (nothing,) * modes)
    each = layers // len(ready)
    for at, wait in enumerate(ready):
        if wait is not None:
            wait()
        carry = lax.fori_loop(at * each, (at + 1) * each, step, carry)


def substitute(layers, modes, lower_ref, half_ref, use):
    tiles, all_rows, lanes = lower_ref.shape
    group = all_rows // layers
    nothing = jnp.zeros((tiles, group, lanes), jnp.float32)

    def step(back, values):
        k = layers - 1 - back
        rows = at_layer(k, group, pitch_of(group))
        lower = lower_ref[:, at_layer(k, group, group), :]
        found = []
        for mode in range(modes):
            value = half_ref[mode, :, rows, :] + lower * values[mode]
            use(mode, k, rows, value)
            found.append(value)
        return tuple(found)

    lax.fori_loop(0, layers, step, (nothing,) * modes)


def put_rows(ref, mode, start, group, result):
    layers = result.shape[0]
    for tile in range(ref.shape[1]):
        ref[mode, tile, pl.ds(start, layers, stride=pitch_of(group)), :] = result[
            :, tile * LANES : (tile + 1) * LANES
        ]


def take_rows(ref, mode, start, group, layers):
    return jnp.concatenate(
        [
            ref[mode, tile, pl.ds(start, layers, stride=pitch_of(group)), :].astype(jnp.bfloat16)
            for tile in range(ref.shape[1])
        ],
        axis=1,
    )


def block_ends_kernel(
    thick_ref, gap_ref, wave_ref, ends_ref, table_ref, factor_ref, velocity_ref, rows_ref,
    saved_ref, out_ref, spectrum_ref, lower_ref, half_ref, end_ref, buffer, arrived, done,
):
    count, part, _, layers = rows_ref.shape
    tiles, group, _ = wave_ref.shape
    if group > part:
        spectrum_ref[...] = jnp.zeros_like(spectrum_ref)

    def fetch(b):
        return pltpu.make_async_copy(rows_ref.at[:, b], buffer.at[b], arrived.at[b])

    for b in range(part):
        fetch(b).start()

    def transform(b, carry):
        fetch(b).wait()
        strips = (factor_ref[b].astype(jnp.float32) * velocity_ref[...]).astype(jnp.bfloat16)
        left = jnp.concatenate([buffer[b, c] for c in range(count)] + [strips], axis=0)
        put_rows(spectrum_ref, 0, b, group, contract(left, table_ref[...], 0, 0))
        return carry

    lax.fori_loop(0, part, transform, 0)
    saving = pltpu.make_async_copy(spectrum_ref, saved_ref, done)
    saving.start()
    eliminate(
        thick_ref, gap_ref, wave_ref, 1,
        lambda mode, k, rows: spectrum_ref[mode, :, rows, :], lower_ref, half_ref,
    )

    def use(mode, k, rows, value):
        for end in range(2):
            end_ref[end, :, pl.ds(k, 1), :] = jnp.sum(
                value * ends_ref[end], axis=1, keepdims=True
            )

    substitute(layers, 1, lower_ref, half_ref, use)
    for end in range(2):
        for tile in range(tiles):
            out_ref[tile * LANES : (tile + 1) * LANES, end * layers : (end + 1) * layers] = (
                end_ref[end, tile].T.astype(jnp.bfloat16)
            )
    saving.wait()


def interface_kernel(
    thick_ref, gap_ref, wave_ref, spread_ref, in_ref,
    out_ref, sum_ref, next_ref, spectrum_ref, lower_ref,
):
    group = wave_ref.shape[1]
    layers = thick_ref.shape[0]
    blocks = spread_ref.shape[0] // 2
    modes = in_ref.shape[0]
    here = in_ref.shape[2] // blocks
    if group > here:
        spectrum_ref[...] = jnp.zeros_like(spectrum_ref)
    for mode in range(modes):
        total = jnp.sum(in_ref[mode].astype(jnp.float32), axis=0)
        for end in range(2):
            sum_ref[end * modes + mode] = total[:, end * layers : (end + 1) * layers]

    for a in range(here):
        picked = pl.ds(a, blocks, stride=here)
        for mode in range(modes):
            left = jnp.concatenate(
                [sum_ref[end * modes + mode, picked, :] for end in range(2)], axis=0
            ).astype(jnp.bfloat16)
            put_rows(spectrum_ref, mode, a, group, contract(left, spread_ref[...], 0, 0))
    eliminate(
        thick_ref, gap_ref, wave_ref, modes,
        lambda mode, k, rows: spectrum_ref[mode, :, rows, :], lower_ref, spectrum_ref,
    )

    def use(mode, k, rows, value):
        spectrum_ref[mode, :, rows, :] = value

    substitute(layers, modes, lower_ref, spectrum_ref, use)
    for a in range(here):
        picked = pl.ds(a, blocks, stride=here)
        for mode in range(modes):
            solved = take_rows(spectrum_ref, mode, a, group, layers)
            found = contract(spread_ref[...], solved, 1, 1)
            for end in range(2):
                next_ref[end * modes + mode, picked, :] = found[
                    end * blocks : (end + 1) * blocks
                ]
    inner = (blocks - 1) * here
    for mode in range(modes):
        first, last = mode, modes + mode
        next_ref[first, here:] = next_ref[first, here:] + sum_ref[last, :inner]
        next_ref[last, :inner] = next_ref[last, :inner] + sum_ref[first, here:]
    for mode in range(modes):
        for end in range(2):
            outgoing = next_ref[end * modes + mode].astype(jnp.bfloat16)
            for copy in range(out_ref.shape[1]):
                out_ref[mode, copy, :, end * layers : (end + 1) * layers] = outgoing


def block_solve_kernel(
    thick_ref, gap_ref, wave_ref, ends_ref, table_ref, factor_ref, velocity_ref, bound_ref,
    saved_ref, out_ref, mass_ref, lower_ref, spectrum_ref, edge_ref, outgoing, arrived, sent,
):
    count, part, x_local, layers = out_ref.shape
    tiles, group, _ = wave_ref.shape
    pieces = arrived.shape[0]
    size = saved_ref.shape[2] // pieces
    loads = []
    for at in range(pieces):
        rows = pl.ds(at * size, size)
        loads.append(
            pltpu.make_async_copy(
                saved_ref.at[:, :, rows], spectrum_ref.at[:, :, rows], arrived.at[at]
            )
        )
        loads[-1].start()
    for end in range(2):
        for tile in range(tiles):
            edge_ref[end, tile] = (
                bound_ref[tile * LANES : (tile + 1) * LANES, end * layers : (end + 1) * layers]
                .astype(jnp.float32)
                .T
            )

    def right_side(mode, k, rows):
        total = spectrum_ref[mode, :, rows, :]
        for end in range(2):
            total = total + ends_ref[end] * edge_ref[end, :, pl.ds(k, 1), :]
        return total

    eliminate(
        thick_ref, gap_ref, wave_ref, 1, right_side, lower_ref, spectrum_ref,
        [load.wait for load in loads],
    )

    def use(mode, k, rows, value):
        spectrum_ref[mode, :, rows, :] = value

    substitute(layers, 1, lower_ref, spectrum_ref, use)

    def send(b):
        return pltpu.make_async_copy(outgoing.at[b], out_ref.at[:, b], sent.at[b])

    def transform(b, at_strips):
        solved = take_rows(spectrum_ref, 0, b, group, layers)
        result = contract(table_ref[...], solved, 1, 1)
        for c in range(count):
            outgoing[b, c] = result[c * x_local : (c + 1) * x_local].astype(jnp.bfloat16)
        send(b).start()
        return at_strips + result[count * x_local :] * factor_ref[b].astype(jnp.float32)

    nothing = jnp.zeros(velocity_ref.shape[1:], jnp.float32)
    at_strips = lax.fori_loop(0, part, transform, nothing)
    for mode in range(velocity_ref.shape[0]):
        mass_ref[mode : mode + 1, :] = jnp.sum(
            at_strips * velocity_ref[mode], axis=0, keepdims=True
        )
    for b in range(part):
        send(b).wait()


def shards(carried, velocity, strip_column, thick):
    modes, x_local, y_local, layers = carried.shape
    count_px = lax.axis_size("px")
    count_py = lax.axis_size("py")
    index_px = lax.axis_index("px")
    index_py = lax.axis_index("py")
    devices = count_px * count_py
    width_x = x_local * count_px
    width_y = y_local * count_py
    pieces = count_px // modes
    part = y_local // pieces
    own_mode, own_piece = index_px // pieces, index_px % pieces
    group = -(-part // 8) * 8
    here = width_x // devices
    group_a = -(-here // 8) * 8
    strip_count = velocity.shape[1] * devices
    both = ("px", "py")

    code = jnp.stack([strip_column // 65536, strip_column // 256 % 256, strip_column % 256])
    code = jnp.pad(code.T, ((0, 0), (0, layers - 3))).astype(jnp.bfloat16)
    packed = jnp.concatenate([velocity, code[None]], axis=0).transpose(1, 0, 2)
    packed = jnp.broadcast_to(packed[None], (devices,) + packed.shape)
    gathered = lax.all_to_all(packed, both, split_axis=0, concat_axis=0, tiled=True)
    gathered = gathered.reshape(strip_count, modes + 1, layers)
    spectra = forward_y(carried, count_px)
    code = gathered[:, modes, :3].astype(jnp.int32)
    column = code[:, 0] * 65536 + code[:, 1] * 256 + code[:, 2]
    all_velocity = gathered[:, :modes].astype(jnp.float32).transpose(1, 0, 2)
    own_velocity = lax.dynamic_index_in_dim(all_velocity, own_mode, 0, False)

    table_x = bf16(sine_table(width_x))
    table_y = jnp.asarray(sine_table(y_local).astype(np.float32))
    local_y = column % width_y - index_py * y_local
    inside = (local_y >= 0) & (local_y < y_local)
    factor = jnp.where(inside[:, None], table_y[jnp.clip(local_y, 0, y_local - 1)], 0.0)
    factor = lax.dynamic_slice_in_dim(factor, own_piece * part, part, axis=1)
    factor = jnp.broadcast_to(factor.T[:, :, None], (part, strip_count, layers))
    factor = factor.astype(jnp.bfloat16)
    table_strips = jnp.concatenate([table_x, table_x[column // width_y]], axis=0)

    gap = jnp.concatenate([2.0 / (thick[:-1] + thick[1:]), 2.0 / thick[-1:]])
    wave_x = jnp.asarray(wave_numbers(width_x).astype(np.float32))
    wave_y = jnp.asarray(wave_numbers(width_y).astype(np.float32))
    wave_block = jnp.asarray(wave_numbers(y_local).astype(np.float32))
    wave_b = lax.dynamic_slice_in_dim(wave_block, own_piece * part, part)
    wave_b = jnp.pad(wave_b, (0, group - part))[:, None] + wave_x.reshape(-1, 1, LANES)
    wave_a = lax.dynamic_slice_in_dim(wave_x, (index_px * count_py + index_py) * here, here)
    wave_a = jnp.pad(wave_a, (0, group_a - here))[:, None] + wave_y.reshape(-1, 1, LANES)
    ends = lax.dynamic_slice_in_dim(table_y[:, (0, y_local - 1)], own_piece * part, part)
    ends = jnp.pad(ends.T, ((0, 0), (0, group - part)))[:, :, None]
    ends = jnp.broadcast_to(ends, (2, group, LANES))

    block_index = np.arange(count_py)
    full = sine_table(width_y)
    not_first = (block_index > 0)[:, None]
    not_last = (block_index < count_py - 1)[:, None]
    before = np.maximum(block_index * y_local - 1, 0)
    after = np.minimum((block_index + 1) * y_local, width_y - 1)
    spread = np.concatenate([full[before] * not_first, full[after] * not_last])

    params = pltpu.CompilerParams(vmem_limit_bytes=VMEM_LIMIT)
    vmem = pl.BlockSpec(memory_space=VMEM)
    smem = pl.BlockSpec(memory_space=SMEM)
    anywhere = pl.BlockSpec(memory_space=pl.ANY)
    float32 = jnp.float32
    tiles_x, tiles_y = width_x // LANES, width_y // LANES

    rows = lax.all_to_all(spectra, "px", split_axis=0, concat_axis=0, tiled=True)
    spectrum, block_ends = pl.pallas_call(
        block_ends_kernel,
        in_specs=[smem, smem] + [vmem] * 5 + [anywhere],
        out_specs=[anywhere, vmem],
        out_shape=[
            jax.ShapeDtypeStruct((1, tiles_x, layers * pitch_of(group), LANES), float32),
            jax.ShapeDtypeStruct((width_x, 2 * layers), jnp.bfloat16),
        ],
        scratch_shapes=[
            pltpu.VMEM((1, tiles_x, layers * pitch_of(group), LANES), float32),
            pltpu.VMEM((tiles_x, layers * group, LANES), float32),
            pltpu.VMEM((1, tiles_x, layers * pitch_of(group), LANES), float32),
            pltpu.VMEM((2, tiles_x, layers, LANES), float32),
            pltpu.VMEM((part, count_px, x_local, layers), jnp.bfloat16),
            pltpu.SemaphoreType.DMA((part,)),
            pltpu.SemaphoreType.DMA(()),
        ],
        compiler_params=params,
        name="block_ends",
    )(thick, gap, wave_b, ends, table_strips, factor, own_velocity, rows)

    arrived = lax.all_to_all(block_ends, both, split_axis=0, concat_axis=0, tiled=True)
    outgoing = pl.pallas_call(
        interface_kernel,
        in_specs=[smem, smem] + [vmem] * 3,
        out_specs=vmem,
        out_shape=jax.ShapeDtypeStruct(
            (modes, pieces, count_py * here, 2 * layers), jnp.bfloat16
        ),
        scratch_shapes=[
            pltpu.VMEM((2 * modes, count_py * here, layers), float32),
            pltpu.VMEM((2 * modes, count_py * here, layers), float32),
            pltpu.VMEM((modes, tiles_y, layers * pitch_of(group_a), LANES), float32),
            pltpu.VMEM((tiles_y, layers * group_a, LANES), float32),
        ],
        compiler_params=pltpu.CompilerParams(vmem_limit_bytes=24 * 1024 * 1024),
        name="interface",
    )(
        thick, gap, wave_a, bf16(spread),
        arrived.reshape(modes, pieces, count_py * here, 2 * layers),
    )
    bounds = lax.all_to_all(
        outgoing.reshape(width_x, 2 * layers), both, split_axis=0, concat_axis=0, tiled=True
    )

    returned, mass = pl.pallas_call(
        block_solve_kernel,
        in_specs=[smem, smem] + [vmem] * 6 + [anywhere],
        out_specs=[anywhere, vmem],
        out_shape=[
            jax.ShapeDtypeStruct((count_px, part, x_local, layers), jnp.bfloat16),
            jax.ShapeDtypeStruct((modes, layers), float32),
        ],
        scratch_shapes=[
            pltpu.VMEM((tiles_x, layers * group, LANES), float32),
            pltpu.VMEM((1, tiles_x, layers * pitch_of(group), LANES), float32),
            pltpu.VMEM((2, tiles_x, layers, LANES), float32),
            pltpu.VMEM((part, count_px, x_local, layers), jnp.bfloat16),
            pltpu.SemaphoreType.DMA((8,)),
            pltpu.SemaphoreType.DMA((part,)),
        ],
        compiler_params=params,
        name="block_solve",
    )(thick, gap, wave_b, ends, table_strips, factor, all_velocity, bounds, spectrum)
    back = lax.all_to_all(returned, "px", split_axis=0, concat_axis=0, tiled=True)
    pressure = inverse_y(back, y_local)
    own_row = (jnp.arange(modes) == own_mode)[:, None]
    local_mass = jnp.where(own_row, jnp.sum(mass * thick[None, :], axis=1)[None, :], 0.0)
    added_mass = lax.psum(lax.psum(local_mass, "py"), "px") / (strip_count * layers)
    return (pressure, added_mass)


def solution(mesh):
    return jax.shard_map(
        shards,
        mesh=mesh,
        in_specs=(P(None, "px", "py", None), P(None, ("px", "py"), None), P(("px", "py")), P()),
        out_specs=(P(None, "px", "py", None), P()),
        check_vma=False,
    )
```

time: 277 us -> 218 us (0.79)
  blocking collectives: 121 us -> 63.9 us
  Pallas kernels: 85 us -> 67.1 us
  waiting for transfers between devices: 39.3 us -> 50.7 us
  starting transfers between devices: 17.3 us -> 20.8 us
    psum x1 -> x2, blocking collectives: 79.8 us -> 51.1 us  [the longest x1 36.2 us: shards(): lax.psum(lax.psum(local_mass, 'py'), 'px') / (strip_count * layers)]
    all_to_all x2 -> x1, blocking collectives: 40.9 us -> 12.8 us  [shards(): lax.all_to_all(outgoing.reshape(width_x, 2 * layers), both, split_axis=0,...]
    all_to_all x0 -> x1, waiting for transfers between devices: none -> 9.54 us  [shards(): lax.all_to_all(block_ends, both, split_axis=0, concat_axis=0, tiled=True)]
    pallas_call x1, Pallas kernels: 13 us -> 6.52 us  [inverse_y(): pl.pallas_call(inverse_y_kernel, grid=(modes, x_local // chunk), in_specs...]
    pallas_call x1, Pallas kernels: 12.8 us -> 6.53 us  [forward_y(): pl.pallas_call(forward_y_kernel, grid=(modes, x_local // chunk), in_specs...]
    pallas_call x1, Pallas kernels: 15.1 us -> 9.36 us  [shards(): pl.pallas_call(interface_kernel, in_specs=[smem, smem] + [vmem] * 3, out_...]
    all_to_all x0 -> x1, starting transfers between devices: none -> 3.8 us  [shards(): lax.all_to_all(block_ends, both, split_axis=0, concat_axis=0, tiled=True)]
  transfers between devices with their start and end apart: 3 -> 4, of which waited for: 1 -> 3; matrix products, arithmetic and copies ran while one was open for 3% -> 4% of each run, Pallas kernels for 5% -> 3%
where the time goes in v3:
time: 218 us; the launch traced here: 217 us
  Pallas kernels  67.1 us (31%)
  blocking collectives  63.9 us (29%)
  waiting for transfers between devices  50.7 us (23%)
  starting transfers between devices  20.8 us (10%)
  local copies, waits for them, and re-layouts  7.45 us (3%)
  other arithmetic  5.94 us (3%)
    all_to_all x1, waiting for transfers between devices, shards(): lax.all_to_all(spectra, 'px', split_axis=0, concat_axis=0, tiled=True)  39.9 us
    psum x1, blocking collectives, shards(): lax.psum(lax.psum(local_mass, 'py'), 'px') / (strip_count * layers)  36.2 us
    pallas_call x1, Pallas kernels, shards(): pl.pallas_call(block_solve_kernel, in_specs=[smem, smem] + [vmem] * 6 + [...  23.4 us
    pallas_call x1, Pallas kernels, shards(): pl.pallas_call(block_ends_kernel, in_specs=[smem, smem] + [vmem] * 5 + [a...  21.2 us
    psum x1, blocking collectives, shards(): lax.psum(local_mass, 'py')  14.8 us
    all_to_all x1, blocking collectives, shards(): lax.all_to_all(outgoing.reshape(width_x, 2 * layers), both, split_axis=0,...  12.8 us
    all_to_all x1, waiting for transfers between devices, shards(): lax.all_to_all(block_ends, both, split_axis=0, concat_axis=0, tiled=True)  9.54 us
    pallas_call x1, Pallas kernels, shards(): pl.pallas_call(interface_kernel, in_specs=[smem, smem] + [vmem] * 3, out_...  9.36 us
  transfers between devices with their start and end apart: 4, of which 3 were waited for; matrix products, arithmetic and copies ran while one was open for 4% of the time, Pallas kernels for 3%

profile of v3, /device:TPU:0, one launch (start us, length us, event | category | flops | bytes accessed | tf_op | source)
XLA Modules:
  0.0 217.3 jit_solution(1323092258327401122)
XLA Ops:
  0.6 0.7 convert_bitcast_fusion
  1.4 0.7 maximum_bitcast_fusion
  2.8 7.3 %all-to-all-start = ((bf16[32,4,3,128]{3,1,2,0:T(4,128)(2,1)}), bf16[32,4,3,128]{3,1,2,0:T(4,128)(2,1)S(1)}, u32[]{:S(2)}, u32[]{:S(2)}) async-start(bf16[32,4,3,128]{3,1,2,0:T(4,128)(2,1)} %broadcast_in_dim.67), calls=%async_computation | async-start | bytes 196608 | tf_op jit(solution)/shard_map/all_to_all | solution.py:381
  10.1 6.5 %forward_y.1 = bf16[4,32,128,128]{3,2,1,0:T(8,128)(2,1)} custom-call(bf16[256,256]{1,0:T(8,128)(2,1)} %constant.145.clone.table_ref, bf16[2,128,64,128]{3,2,1,0:T(8,128)(2,1)} %grid_ref.1), custom_call_target="tpu_custom_call" | custom-call | tf_op jit(solution)/shard_map/forward_y/pallas_call | solution.py:92
  16.7 1.2 all-to-all-done
  17.9 4.8 %all-to-all-start.1 = ((bf16[4,32,128,128]{3,2,1,0:T(8,128)(2,1)}), bf16[4,32,128,128]{3,2,1,0:T(8,128)(2,1)}, u32[]{:S(2)}, u32[]{:S(2)}) async-start(bf16[4,32,128,128]{3,2,1,0:T(8,128)(2,1)} %forward_y.1), calls=%async_computation.1 | async-start | bytes 8388608 | tf_op jit(solution)/shard_map/all_to_all | solution.py:426
  25.5 0.7 broadcast_add_fusion.wave_ref
  26.6 0.7 gather_fusion.2
  27.8 0.8 gather_fusion.1
  29.9 0.9 pad_maximum_fusion.table_ref
  30.8 39.9 %all-to-all-done.1.rows_ref = bf16[4,32,128,128]{3,2,1,0:T(8,128)(2,1)} async-done(((bf16[4,32,128,128]{3,2,1,0:T(8,128)(2,1)}), bf16[4,32,128,128]{3,2,1,0:T(8,128)(2,1)}, u32[]{:S(2)}, u32[]{:S(2)}) %all-to-all-start.1) | async-done | bytes 4194336 | tf_op jit(solution)/shard_map/all_to_all | solution.py:426
  70.7 1.6 broadcast_in_dim.71.factor_ref
  72.4 0.7 broadcast_in_dim.65.ends_ref
  73.0 21.2 %block_ends.1 = (f32[1,4,5120,128]{3,2,1,0:T(8,128)}, bf16[512,256]{1,0:T(8,128)(2,1)}) custom-call(f32[128]{0:T(128)} %thick_ref.5, f32[128]{0:T(128)} %pad_maximum_fusion.1.gap_ref, f32[4,32,128]{2,1,0:T(8,128)} %broadcast_add_fusion.wave_ref, f32[2,32,128]{2,1,0:T(8,128)} %broadcast_in_dim.65.ends_ref, bf16[640,512]{1,0:T(8,128)(2,1)} %pad_maximum_fusion.table_ref, ...), custom_call_target="tpu_custom_call" | custom-call | tf_op jit(solution)/shard_map/block_ends/pallas_call | solution.py:427
  94.3 3.8 %all-to-all-start.2 = ((bf16[32,16,256]{2,1,0:T(8,128)(2,1)}), bf16[32,16,256]{2,1,0:T(8,128)(2,1)S(1)}, u32[]{:S(2)}, u32[]{:S(2)}) async-start(bf16[32,16,256]{2,1,0:T(8,128)(2,1)} %bitcast.33), calls=%async_computation.2 | async-start | bytes 524288 | tf_op jit(solution)/shard_map/all_to_all | solution.py:448
  98.1 0.8 dynamic_slice.17
  98.9 9.5 %all-to-all-done.2 = bf16[32,16,256]{2,1,0:T(8,128)(2,1)S(1)} async-done(((bf16[32,16,256]{2,1,0:T(8,128)(2,1)}), bf16[32,16,256]{2,1,0:T(8,128)(2,1)S(1)}, u32[]{:S(2)}, u32[]{:S(2)}) %all-to-all-start.2) | async-done | bytes 262176 | tf_op jit(solution)/shard_map/all_to_all | solution.py:448
  108.5 9.4 %interface.1 = bf16[2,2,128,256]{3,2,1,0:T(8,128)(2,1)S(1)} custom-call(f32[128]{0:T(128)S(1)} %copy-done.2, f32[128]{0:T(128)S(1)} %copy-done.4, f32[4,16,128]{2,1,0:T(8,128)S(1)} %broadcast_add_fusion.1.wave_ref, bf16[16,512]{1,0:T(8,128)(2,1)S(1)} %copy-done, bf16[2,2,128,256]{3,2,1,0:T(8,128)(2,1)S(1)} %bitcast.28), custom_call_target="tpu_custom_call" | custom-call | tf_op jit(solution)/shard_map/interface/pallas_call | solution.py:449
  117.9 12.8 %all_to_all.35 = bf16[32,16,256]{2,1,0:T(8,128)(2,1)} all-to-all(bf16[32,16,256]{2,1,0:T(8,128)(2,1)S(1)} %bitcast.29), channel_id=1, replica_groups=mesh['px'=4,'py'=8] {'px','py'}, dimensions={0} | all-to-all | bytes 524288 | tf_op jit(solution)/shard_map/all_to_all | solution.py:468
  130.7 23.4 %block_solve.1 = (bf16[4,32,128,128]{3,2,1,0:T(8,128)(2,1)}, f32[2,128]{1,0:T(2,128)}) custom-call(f32[128]{0:T(128)} %thick_ref.5, f32[128]{0:T(128)} %pad_maximum_fusion.1.gap_ref, f32[4,32,128]{2,1,0:T(8,128)} %broadcast_add_fusion.wave_ref, f32[2,32,128]{2,1,0:T(8,128)} %broadcast_in_dim.65.ends_ref, bf16[640,512]{1,0:T(8,128)(2,1)} %pad_maximum_fusion.table_ref, ...), custom_call_target="tpu_custom_call" | custom-call | tf_op jit(solution)/shard_map/block_solve/pallas_call | solution.py:472
  154.1 4.9 %all-to-all-start.4 = ((bf16[4,32,128,128]{3,2,1,0:T(8,128)(2,1)}), bf16[4,32,128,128]{3,2,1,0:T(8,128)(2,1)}, u32[]{:S(2)}, u32[]{:S(2)}) async-start(bf16[4,32,128,128]{3,2,1,0:T(8,128)(2,1)} %get-tuple-element.8), calls=%async_computation.4 | async-start | bytes 8388608 | tf_op jit(solution)/shard_map/all_to_all | solution.py:491
  159.2 14.8 %psum.14 = f32[2,2]{1,0:T(2,128)S(1)} all-reduce(f32[2,2]{1,0:T(2,128)S(1)} %broadcast_select_fusion), channel_id=1, replica_groups=mesh['px'=4,'py'=8] {'py'}, use_global_device_ids=true, to_apply=%region_1.2 | all-reduce | flops 4 | bytes 32 | tf_op jit(solution)/shard_map/psum | solution.py:495
  174.0 36.2 %psum.15 = f32[2,2]{1,0:T(2,128)S(1)} all-reduce(f32[2,2]{1,0:T(2,128)S(1)} %psum.14), channel_id=1, replica_groups=mesh['px'=4,'py'=8] {'px'}, use_global_device_ids=true, to_apply=%region_2.3 | all-reduce | flops 4 | bytes 32 | tf_op jit(solution)/shard_map/psum | solution.py:495
  210.8 6.5 %inverse_y.1 = bf16[2,128,64,128]{3,2,1,0:T(8,128)(2,1)} custom-call(bf16[256,256]{1,0:T(8,128)(2,1)} %constant.145.clone.table_ref, bf16[4,32,128,128]{3,2,1,0:T(8,128)(2,1)} %all-to-all-done.4.in_ref), custom_call_target="tpu_custom_call" | custom-call | tf_op jit(solution)/shard_map/inverse_y/pallas_call | solution.py:113
  (51 shorter events, 5.8 us)
Async XLA Ops:
  2.8 15.1 %all-to-all-start = ((bf16[32,4,3,128]{3,1,2,0:T(4,128)(2,1)}), bf16[32,4,3,128]{3,1,2,0:T(4,128)(2,1)S(1)}, u32[]{:S(2)}, u32[]{:S(2)}) async-start(bf16[32,4,3,128]{3,1,2,0:T(4,128)(2,1)} %broadcast_in_dim.67), calls=%async_computation | async-start | bytes 196608 | tf_op jit(solution)/shard_map/all_to_all | solution.py:381
  16.6 6.1 %copy-start.1 = (f32[128]{0:T(128)S(1)}, f32[128]{0:T(128)}, u32[]{:S(2)}) copy-start(f32[128]{0:T(128)} %thick_ref.5) | copy-start | bytes 1540
  16.6 6.7 %copy-start.10 = (f32[64]{0:T(128)S(1)}, f32[64]{0:T(128)}, u32[]{:S(2)}) copy-start(f32[64]{0:T(128)} %constant.149.clone) | copy-start | bytes 772
  16.6 6.8 %copy-start.7 = (f32[64,64]{0,1:T(8,128)S(1)}, f32[64,64]{0,1:T(8,128)}, u32[]{:S(2)}) copy-start(f32[64,64]{0,1:T(8,128)} %constant.147.clone) | copy-start | bytes 49156
  16.6 8.9 %copy-start.8 = (f32[4,128]{1,0:T(4,128)S(1)}, f32[4,128]{1,0:T(4,128)}, u32[]{:S(2)}) copy-start(f32[4,128]{1,0:T(4,128)} %constant.156) | copy-start | bytes 6148
  16.6 10.0 %copy-start.6 = (bf16[64,64]{1,0:T(8,128)(2,1)S(1)}, bf16[64,64]{1,0:T(8,128)(2,1)}, u32[]{:S(2)}) copy-start(bf16[64,64]{1,0:T(8,128)(2,1)} %constant.231) | copy-start | bytes 24580
  16.7 11.1 %copy-start.5 = (bf16[512,512]{1,0:T(8,128)(2,1)S(1)}, bf16[512,512]{1,0:T(8,128)(2,1)}, u32[]{:S(2)}) copy-start(bf16[512,512]{1,0:T(8,128)(2,1)} %constant.146.clone) | copy-start | bytes 1572868
  17.9 52.9 %all-to-all-start.1 = ((bf16[4,32,128,128]{3,2,1,0:T(8,128)(2,1)}), bf16[4,32,128,128]{3,2,1,0:T(8,128)(2,1)}, u32[]{:S(2)}, u32[]{:S(2)}) async-start(bf16[4,32,128,128]{3,2,1,0:T(8,128)(2,1)} %forward_y.1), calls=%async_computation.1 | async-start | bytes 8388608 | tf_op jit(solution)/shard_map/all_to_all | solution.py:426
  29.9 78.6 %copy-start = (bf16[16,512]{1,0:T(8,128)(2,1)S(1)}, bf16[16,512]{1,0:T(8,128)(2,1)}, u32[]{:S(2)}) copy-start(bf16[16,512]{1,0:T(8,128)(2,1)} %constant.151.clone.spread_ref) | copy-start | bytes 49156
  29.9 78.6 %copy-start.2 = (f32[128]{0:T(128)S(1)}, f32[128]{0:T(128)}, u32[]{:S(2)}) copy-start(f32[128]{0:T(128)} %thick_ref.5) | copy-start | bytes 1540
  29.9 78.6 %copy-start.4 = (f32[128]{0:T(128)S(1)}, f32[128]{0:T(128)}, u32[]{:S(2)}) copy-start(f32[128]{0:T(128)} %pad_maximum_fusion.1.gap_ref) | copy-start | bytes 1540
  94.3 14.2 %all-to-all-start.2 = ((bf16[32,16,256]{2,1,0:T(8,128)(2,1)}), bf16[32,16,256]{2,1,0:T(8,128)(2,1)S(1)}, u32[]{:S(2)}, u32[]{:S(2)}) async-start(bf16[32,16,256]{2,1,0:T(8,128)(2,1)} %bitcast.33), calls=%async_computation.2 | async-start | bytes 524288 | tf_op jit(solution)/shard_map/all_to_all | solution.py:448
  154.1 4.9 %copy-start.3 = (f32[128]{0:T(128)S(1)}, f32[128]{0:T(128)}, u32[]{:S(2)}) copy-start(f32[128]{0:T(128)} %thick_ref.5) | copy-start | bytes 1540
  154.1 4.9 %copy-start.9 = (f32[2,128]{1,0:T(2,128)S(1)}, f32[2,128]{1,0:T(2,128)}, u32[]{:S(2)}) copy-start(f32[2,128]{1,0:T(2,128)} %get-tuple-element.9) | copy-start | bytes 3076
  154.1 56.7 %all-to-all-start.4 = ((bf16[4,32,128,128]{3,2,1,0:T(8,128)(2,1)}), bf16[4,32,128,128]{3,2,1,0:T(8,128)(2,1)}, u32[]{:S(2)}, u32[]{:S(2)}) async-start(bf16[4,32,128,128]{3,2,1,0:T(8,128)(2,1)} %get-tuple-element.8), calls=%async_computation.4 | async-start | bytes 8388608 | tf_op jit(solution)/shard_map/all_to_all | solution.py:491

commit v4 on v3

--- a/solution.py
+++ b/solution.py
@@ -98,7 +98,7 @@
         ],
         out_specs=pl.BlockSpec((pieces, part, chunk, layers), lambda m, i: (m, 0, i, 0)),
         out_shape=jax.ShapeDtypeStruct((count, part, x_local, layers), jnp.bfloat16),
-        scratch_shapes=[pltpu.VMEM((rows * pitch_of(chunk), layers), jnp.float32)],
+        scratch_shapes=[pltpu.VMEM(((rows + 1) * pitch_of(chunk), layers), jnp.float32)],
         compiler_params=pltpu.CompilerParams(vmem_limit_bytes=VMEM_LIMIT),
         name="forward_y",
     )(table, carried)
@@ -119,7 +119,7 @@
         ],
         out_specs=pl.BlockSpec((1, chunk, rows, layers), lambda m, i: (m, i, 0, 0)),
         out_shape=jax.ShapeDtypeStruct((modes, x_local, rows, layers), jnp.bfloat16),
-        scratch_shapes=[pltpu.VMEM((rows * pitch_of(chunk), layers), jnp.float32)],
+        scratch_shapes=[pltpu.VMEM(((rows + 1) * pitch_of(chunk), layers), jnp.float32)],
         compiler_params=pltpu.CompilerParams(vmem_limit_bytes=VMEM_LIMIT),
         name="inverse_y",
     )(table, spectra)
@@ -156,7 +156,7 @@
     for at, wait in enumerate(ready):
         if wait is not None:
             wait()
-        carry = lax.fori_loop(at * each, (at + 1) * each, step, carry)
+        carry = lax.fori_loop(at * each, (at + 1) * each, step, carry, unroll=4)
 
 
 def substitute(layers, modes, lower_ref, half_ref, use):
@@ -175,7 +175,7 @@
             found.append(value)
         return tuple(found)
 
-    lax.fori_loop(0, layers, step, (nothing,) * modes)
+    lax.fori_loop(0, layers, step, (nothing,) * modes, unroll=4)
 
 
 def put_rows(ref, mode, start, group, result):
@@ -197,7 +197,8 @@
 
 
 def block_ends_kernel(
-    thick_ref, gap_ref, wave_ref, ends_ref, table_ref, factor_ref, velocity_ref, rows_ref,
+    thick_ref, gap_ref, wave_ref, ends_ref, table_ref, strip_table_ref, factor_ref, velocity_ref,
+    rows_ref,
     saved_ref, out_ref, spectrum_ref, lower_ref, half_ref, end_ref, buffer, arrived, done,
 ):
     count, part, _, layers = rows_ref.shape
@@ -213,12 +214,15 @@
 
     def transform(b, carry):
         fetch(b).wait()
-        strips = (factor_ref[b].astype(jnp.float32) * velocity_ref[...]).astype(jnp.bfloat16)
-        left = jnp.concatenate([buffer[b, c] for c in range(count)] + [strips], axis=0)
-        put_rows(spectrum_ref, 0, b, group, contract(left, table_ref[...], 0, 0))
+        strips = (factor_ref[b] * velocity_ref[...]).astype(jnp.bfloat16)
+        left = jnp.concatenate([buffer[b, c] for c in range(count)], axis=0)
+        result = contract(left, table_ref[...], 0, 0) + contract(
+            strips, strip_table_ref[...], 1, 0
+        )
+        put_rows(spectrum_ref, 0, b, group, result)
         return carry
 
-    lax.fori_loop(0, part, transform, 0)
+    lax.fori_loop(0, part, transform, 0, unroll=2)
     saving = pltpu.make_async_copy(spectrum_ref, saved_ref, done)
     saving.start()
     eliminate(
@@ -255,7 +259,7 @@
     for mode in range(modes):
         total = jnp.sum(in_ref[mode].astype(jnp.float32), axis=0)
         for end in range(2):
-            sum_ref[end * modes + mode] = total[:, end * layers : (end + 1) * layers]
+            sum_ref[end * modes + mode, : total.shape[0]] = total[:, end * layers : (end + 1) * layers]
 
     for a in range(here):
         picked = pl.ds(a, blocks, stride=here)
@@ -282,26 +286,27 @@
                 next_ref[end * modes + mode, picked, :] = found[
                     end * blocks : (end + 1) * blocks
                 ]
-    inner = (blocks - 1) * here
+    inner, every = (blocks - 1) * here, blocks * here
     for mode in range(modes):
         first, last = mode, modes + mode
-        next_ref[first, here:] = next_ref[first, here:] + sum_ref[last, :inner]
-        next_ref[last, :inner] = next_ref[last, :inner] + sum_ref[first, here:]
+        next_ref[first, here:every] = next_ref[first, here:every] + sum_ref[last, :inner]
+        next_ref[last, :inner] = next_ref[last, :inner] + sum_ref[first, here:every]
     for mode in range(modes):
         for end in range(2):
-            outgoing = next_ref[end * modes + mode].astype(jnp.bfloat16)
+            outgoing = next_ref[end * modes + mode, :every].astype(jnp.bfloat16)
             for copy in range(out_ref.shape[1]):
                 out_ref[mode, copy, :, end * layers : (end + 1) * layers] = outgoing
 
 
 def block_solve_kernel(
-    thick_ref, gap_ref, wave_ref, ends_ref, table_ref, factor_ref, velocity_ref, bound_ref,
+    thick_ref, gap_ref, wave_ref, ends_ref, table_ref, strip_table_ref, factor_ref, velocity_ref,
+    bound_ref,
     saved_ref, out_ref, mass_ref, lower_ref, spectrum_ref, edge_ref, outgoing, arrived, sent,
 ):
     count, part, x_local, layers = out_ref.shape
     tiles, group, _ = wave_ref.shape
     pieces = arrived.shape[0]
-    size = saved_ref.shape[2] // pieces
+    size = layers * pitch_of(group) // pieces
     loads = []
     for at in range(pieces):
         rows = pl.ds(at * size, size)
@@ -338,20 +343,27 @@
     def send(b):
         return pltpu.make_async_copy(outgoing.at[b], out_ref.at[:, b], sent.at[b])
 
-    def transform(b, at_strips):
-        solved = take_rows(spectrum_ref, 0, b, group, layers)
+    def transform(pair, at_strips):
+        first = pair * 2
+        solved = jnp.concatenate(
+            [take_rows(spectrum_ref, 0, first + at, group, layers) for at in range(2)], axis=0
+        )
         result = contract(table_ref[...], solved, 1, 1)
-        for c in range(count):
-            outgoing[b, c] = result[c * x_local : (c + 1) * x_local].astype(jnp.bfloat16)
-        send(b).start()
-        return at_strips + result[count * x_local :] * factor_ref[b].astype(jnp.float32)
+        for at in range(2):
+            b = first + at
+            found = result[:, at * layers : (at + 1) * layers]
+            for c in range(count):
+                outgoing[b, c] = found[c * x_local : (c + 1) * x_local].astype(jnp.bfloat16)
+            send(b).start()
+        found = contract(solved, strip_table_ref[...], 1, 1)
+        for at in range(2):
+            at_strips += found[at * layers : (at + 1) * layers] * factor_ref[first + at]
+        return at_strips
 
     nothing = jnp.zeros(velocity_ref.shape[1:], jnp.float32)
-    at_strips = lax.fori_loop(0, part, transform, nothing)
+    at_strips = lax.fori_loop(0, part // 2, transform, nothing, unroll=4)
     for mode in range(velocity_ref.shape[0]):
-        mass_ref[mode : mode + 1, :] = jnp.sum(
-            at_strips * velocity_ref[mode], axis=0, keepdims=True
-        )
+        mass_ref[mode] = at_strips * velocity_ref[mode]
     for b in range(part):
         send(b).wait()
 
@@ -383,7 +395,7 @@
     spectra = forward_y(carried, count_px)
     code = gathered[:, modes, :3].astype(jnp.int32)
     column = code[:, 0] * 65536 + code[:, 1] * 256 + code[:, 2]
-    all_velocity = gathered[:, :modes].astype(jnp.float32).transpose(1, 0, 2)
+    all_velocity = gathered[:, :modes].astype(jnp.float32).transpose(1, 2, 0)
     own_velocity = lax.dynamic_index_in_dim(all_velocity, own_mode, 0, False)
 
     table_x = bf16(sine_table(width_x))
@@ -392,9 +404,8 @@
     inside = (local_y >= 0) & (local_y < y_local)
     factor = jnp.where(inside[:, None], table_y[jnp.clip(local_y, 0, y_local - 1)], 0.0)
     factor = lax.dynamic_slice_in_dim(factor, own_piece * part, part, axis=1)
-    factor = jnp.broadcast_to(factor.T[:, :, None], (part, strip_count, layers))
-    factor = factor.astype(jnp.bfloat16)
-    table_strips = jnp.concatenate([table_x, table_x[column // width_y]], axis=0)
+    factor = factor.T[:, None, :]
+    table_strips = table_x[column // width_y]
 
     gap = jnp.concatenate([2.0 / (thick[:-1] + thick[1:]), 2.0 / thick[-1:]])
     wave_x = jnp.asarray(wave_numbers(width_x).astype(np.float32))
@@ -426,16 +437,16 @@
     rows = lax.all_to_all(spectra, "px", split_axis=0, concat_axis=0, tiled=True)
     spectrum, block_ends = pl.pallas_call(
         block_ends_kernel,
-        in_specs=[smem, smem] + [vmem] * 5 + [anywhere],
+        in_specs=[smem, smem] + [vmem] * 6 + [anywhere],
         out_specs=[anywhere, vmem],
         out_shape=[
-            jax.ShapeDtypeStruct((1, tiles_x, layers * pitch_of(group), LANES), float32),
+            jax.ShapeDtypeStruct((1, tiles_x, (layers + 1) * pitch_of(group), LANES), float32),
             jax.ShapeDtypeStruct((width_x, 2 * layers), jnp.bfloat16),
         ],
         scratch_shapes=[
-            pltpu.VMEM((1, tiles_x, layers * pitch_of(group), LANES), float32),
+            pltpu.VMEM((1, tiles_x, (layers + 1) * pitch_of(group), LANES), float32),
             pltpu.VMEM((tiles_x, layers * group, LANES), float32),
-            pltpu.VMEM((1, tiles_x, layers * pitch_of(group), LANES), float32),
+            pltpu.VMEM((1, tiles_x, (layers + 1) * pitch_of(group), LANES), float32),
             pltpu.VMEM((2, tiles_x, layers, LANES), float32),
             pltpu.VMEM((part, count_px, x_local, layers), jnp.bfloat16),
             pltpu.SemaphoreType.DMA((part,)),
@@ -443,7 +454,7 @@
         ],
         compiler_params=params,
         name="block_ends",
-    )(thick, gap, wave_b, ends, table_strips, factor, own_velocity, rows)
+    )(thick, gap, wave_b, ends, table_x, table_strips, factor, own_velocity, rows)
 
     arrived = lax.all_to_all(block_ends, both, split_axis=0, concat_axis=0, tiled=True)
     outgoing = pl.pallas_call(
@@ -454,9 +465,9 @@
             (modes, pieces, count_py * here, 2 * layers), jnp.bfloat16
         ),
         scratch_shapes=[
-            pltpu.VMEM((2 * modes, count_py * here, layers), float32),
-            pltpu.VMEM((2 * modes, count_py * here, layers), float32),
-            pltpu.VMEM((modes, tiles_y, layers * pitch_of(group_a), LANES), float32),
+            pltpu.VMEM((2 * modes, (count_py + 1) * here, layers), float32),
+            pltpu.VMEM((2 * modes, (count_py + 1) * here, layers), float32),
+            pltpu.VMEM((modes, tiles_y, (layers + 1) * pitch_of(group_a), LANES), float32),
             pltpu.VMEM((tiles_y, layers * group_a, LANES), float32),
         ],
         compiler_params=pltpu.CompilerParams(vmem_limit_bytes=24 * 1024 * 1024),
@@ -471,15 +482,15 @@
 
     returned, mass = pl.pallas_call(
         block_solve_kernel,
-        in_specs=[smem, smem] + [vmem] * 6 + [anywhere],
+        in_specs=[smem, smem] + [vmem] * 7 + [anywhere],
         out_specs=[anywhere, vmem],
         out_shape=[
             jax.ShapeDtypeStruct((count_px, part, x_local, layers), jnp.bfloat16),
-            jax.ShapeDtypeStruct((modes, layers), float32),
+            jax.ShapeDtypeStruct((modes, layers, strip_count), float32),
         ],
         scratch_shapes=[
             pltpu.VMEM((tiles_x, layers * group, LANES), float32),
-            pltpu.VMEM((1, tiles_x, layers * pitch_of(group), LANES), float32),
+            pltpu.VMEM((1, tiles_x, (layers + 1) * pitch_of(group), LANES), float32),
             pltpu.VMEM((2, tiles_x, layers, LANES), float32),
             pltpu.VMEM((part, count_px, x_local, layers), jnp.bfloat16),
             pltpu.SemaphoreType.DMA((8,)),
@@ -487,11 +498,14 @@
         ],
         compiler_params=params,
         name="block_solve",
-    )(thick, gap, wave_b, ends, table_strips, factor, all_velocity, bounds, spectrum)
+    )(
+        thick, gap, wave_b, ends, table_x, table_strips, factor, all_velocity, bounds, spectrum
+    )
     back = lax.all_to_all(returned, "px", split_axis=0, concat_axis=0, tiled=True)
     pressure = inverse_y(back, y_local)
     own_row = (jnp.arange(modes) == own_mode)[:, None]
-    local_mass = jnp.where(own_row, jnp.sum(mass * thick[None, :], axis=1)[None, :], 0.0)
+    local_mass = jnp.sum(mass * thick[None, :, None], axis=(1, 2))
+    local_mass = jnp.where(own_row, local_mass[None, :], 0.0)
     added_mass = lax.psum(lax.psum(local_mass, "py"), "px") / (strip_count * layers)
     return (pressure, added_mass)
 

time: 218 us -> 204 us (0.936)
  Pallas kernels: 67.1 us -> 54.1 us
    pallas_call x2, Pallas kernels: 44.6 us -> 32.8 us  [the longest x1 18.6 us: shards(): pl.pallas_call(block_ends_kernel, in_specs=[smem, smem] + [vmem] * 6 + [a...]
  transfers between devices with their start and end apart: 4 -> 4, of which waited for: 3 -> 3; matrix products, arithmetic and copies ran while one was open for 4% -> 5% of each run, Pallas kernels for 3% -> 3%
where the time goes in v4:
time: 204 us; the launch traced here: 203 us
  blocking collectives  63.8 us (31%)
  Pallas kernels  54.1 us (27%)
  waiting for transfers between devices  50.4 us (25%)
  starting transfers between devices  20.9 us (10%)
  local copies, waits for them, and re-layouts  6.6 us (3%)
  other arithmetic  5.51 us (3%)
    all_to_all x1, waiting for transfers between devices, shards(): lax.all_to_all(spectra, 'px', split_axis=0, concat_axis=0, tiled=True)  39.6 us
    psum x1, blocking collectives, shards(): lax.psum(lax.psum(local_mass, 'py'), 'px') / (strip_count * layers)  36.2 us
    pallas_call x1, Pallas kernels, shards(): pl.pallas_call(block_ends_kernel, in_specs=[smem, smem] + [vmem] * 6 + [a...  18.6 us
    psum x1, blocking collectives, shards(): lax.psum(local_mass, 'py')  14.8 us
    pallas_call x1, Pallas kernels, shards(): pl.pallas_call(block_solve_kernel, in_specs=[smem, smem] + [vmem] * 7 + [...  14.2 us
    all_to_all x1, blocking collectives, shards(): lax.all_to_all(outgoing.reshape(width_x, 2 * layers), both, split_axis=0,...  12.8 us
    all_to_all x1, waiting for transfers between devices, shards(): lax.all_to_all(block_ends, both, split_axis=0, concat_axis=0, tiled=True)  9.54 us
    pallas_call x1, Pallas kernels, shards(): pl.pallas_call(interface_kernel, in_specs=[smem, smem] + [vmem] * 3, out_...  8.31 us
  transfers between devices with their start and end apart: 4, of which 3 were waited for; matrix products, arithmetic and copies ran while one was open for 5% of the time, Pallas kernels for 3%

profile of v4, /device:TPU:0, one launch (start us, length us, event | category | flops | bytes accessed | tf_op | source)
XLA Modules:
  0.0 203.0 jit_solution(4696415348077308790)
XLA Ops:
  0.6 0.7 convert_bitcast_fusion.1
  1.4 0.7 maximum_bitcast_fusion
  2.1 0.7 broadcast_in_dim.64
  2.8 7.3 %all-to-all-start = ((bf16[32,4,3,128]{3,1,2,0:T(4,128)(2,1)}), bf16[32,4,3,128]{3,1,2,0:T(4,128)(2,1)S(1)}, u32[]{:S(2)}, u32[]{:S(2)}) async-start(bf16[32,4,3,128]{3,1,2,0:T(4,128)(2,1)} %broadcast_in_dim.64), calls=%async_computation | async-start | bytes 196608 | tf_op jit(solution)/shard_map/all_to_all | solution.py:393
  10.1 6.5 %forward_y.1 = bf16[4,32,128,128]{3,2,1,0:T(8,128)(2,1)} custom-call(bf16[256,256]{1,0:T(8,128)(2,1)} %constant.145.clone.table_ref, bf16[2,128,64,128]{3,2,1,0:T(8,128)(2,1)} %grid_ref.1), custom_call_target="tpu_custom_call" | custom-call | tf_op jit(solution)/shard_map/forward_y/pallas_call | solution.py:92
  16.6 1.2 all-to-all-done
  17.9 4.9 %all-to-all-start.1 = ((bf16[4,32,128,128]{3,2,1,0:T(8,128)(2,1)}), bf16[4,32,128,128]{3,2,1,0:T(8,128)(2,1)}, u32[]{:S(2)}, u32[]{:S(2)}) async-start(bf16[4,32,128,128]{3,2,1,0:T(8,128)(2,1)} %forward_y.1), calls=%async_computation.1 | async-start | bytes 8388608 | tf_op jit(solution)/shard_map/all_to_all | solution.py:437
  25.5 0.7 broadcast_add_fusion.wave_ref
  26.7 0.6 gather_fusion.2
  27.8 1.5 gather_fusion.1
  29.3 0.7 fusion.13
  31.2 39.6 %all-to-all-done.1.rows_ref = bf16[4,32,128,128]{3,2,1,0:T(8,128)(2,1)} async-done(((bf16[4,32,128,128]{3,2,1,0:T(8,128)(2,1)}), bf16[4,32,128,128]{3,2,1,0:T(8,128)(2,1)}, u32[]{:S(2)}, u32[]{:S(2)}) %all-to-all-start.1) | async-done | bytes 4194336 | tf_op jit(solution)/shard_map/all_to_all | solution.py:437
  70.8 0.7 broadcast_in_dim.62.ends_ref
  71.4 18.6 %block_ends.1 = (f32[1,4,5160,128]{3,2,1,0:T(8,128)}, bf16[512,256]{1,0:T(8,128)(2,1)}) custom-call(f32[128]{0:T(128)} %thick_ref.5, f32[128]{0:T(128)} %pad_maximum_fusion.gap_ref, f32[4,32,128]{2,1,0:T(8,128)} %broadcast_add_fusion.wave_ref, f32[2,32,128]{2,1,0:T(8,128)} %broadcast_in_dim.62.ends_ref, bf16[512,512]{1,0:T(8,128)(2,1)} %constant.146.clone.table_ref, ...), custom_call_target="tpu_custom_call" | custom-call | tf_op jit(solution)/shard_map/block_ends/pallas_call | solution.py:438
  90.0 3.8 %all-to-all-start.2 = ((bf16[32,16,256]{2,1,0:T(8,128)(2,1)}), bf16[32,16,256]{2,1,0:T(8,128)(2,1)S(1)}, u32[]{:S(2)}, u32[]{:S(2)}) async-start(bf16[32,16,256]{2,1,0:T(8,128)(2,1)} %bitcast.36), calls=%async_computation.2 | async-start | bytes 524288 | tf_op jit(solution)/shard_map/all_to_all | solution.py:459
  93.8 0.8 dynamic_slice.19
  94.6 9.5 %all-to-all-done.2 = bf16[32,16,256]{2,1,0:T(8,128)(2,1)S(1)} async-done(((bf16[32,16,256]{2,1,0:T(8,128)(2,1)}), bf16[32,16,256]{2,1,0:T(8,128)(2,1)S(1)}, u32[]{:S(2)}, u32[]{:S(2)}) %all-to-all-start.2) | async-done | bytes 262176 | tf_op jit(solution)/shard_map/all_to_all | solution.py:459
  104.2 8.3 %interface.1 = bf16[2,2,128,256]{3,2,1,0:T(8,128)(2,1)S(1)} custom-call(f32[128]{0:T(128)S(1)} %copy-done.2, f32[128]{0:T(128)S(1)} %copy-done.4, f32[4,16,128]{2,1,0:T(8,128)S(1)} %broadcast_add_fusion.1.wave_ref, bf16[16,512]{1,0:T(8,128)(2,1)S(1)} %copy-done, bf16[2,2,128,256]{3,2,1,0:T(8,128)(2,1)S(1)} %bitcast.31), custom_call_target="tpu_custom_call" | custom-call | tf_op jit(solution)/shard_map/interface/pallas_call | solution.py:460
  112.5 12.8 %all_to_all.35 = bf16[32,16,256]{2,1,0:T(8,128)(2,1)} all-to-all(bf16[32,16,256]{2,1,0:T(8,128)(2,1)S(1)} %bitcast.32), channel_id=1, replica_groups=mesh['px'=4,'py'=8] {'px','py'}, dimensions={0} | all-to-all | bytes 524288 | tf_op jit(solution)/shard_map/all_to_all | solution.py:479
  125.3 14.2 %block_solve.1 = (bf16[4,32,128,128]{3,2,1,0:T(8,128)(2,1)}, f32[2,128,128]{2,1,0:T(8,128)}) custom-call(f32[128]{0:T(128)} %thick_ref.5, f32[128]{0:T(128)} %pad_maximum_fusion.gap_ref, f32[4,32,128]{2,1,0:T(8,128)} %broadcast_add_fusion.wave_ref, f32[2,32,128]{2,1,0:T(8,128)} %broadcast_in_dim.62.ends_ref, bf16[512,512]{1,0:T(8,128)(2,1)} %constant.146.clone.table_ref, ...), custom_call_target="tpu_custom_call" | custom-call | tf_op jit(solution)/shard_map/block_solve/pallas_call | solution.py:483
  139.6 5.0 %all-to-all-start.4 = ((bf16[4,32,128,128]{3,2,1,0:T(8,128)(2,1)}), bf16[4,32,128,128]{3,2,1,0:T(8,128)(2,1)}, u32[]{:S(2)}, u32[]{:S(2)}) async-start(bf16[4,32,128,128]{3,2,1,0:T(8,128)(2,1)} %get-tuple-element.8), calls=%async_computation.4 | async-start | bytes 8388608 | tf_op jit(solution)/shard_map/all_to_all | solution.py:504
  144.9 14.8 %psum.14 = f32[2,2]{1,0:T(2,128)S(1)} all-reduce(f32[2,2]{1,0:T(2,128)S(1)} %broadcast_select_fusion.1), channel_id=1, replica_groups=mesh['px'=4,'py'=8] {'py'}, use_global_device_ids=true, to_apply=%region_1.2 | all-reduce | flops 4 | bytes 32 | tf_op jit(solution)/shard_map/psum | solution.py:509
  159.7 36.2 %psum.15 = f32[2,2]{1,0:T(2,128)S(1)} all-reduce(f32[2,2]{1,0:T(2,128)S(1)} %psum.14), channel_id=1, replica_groups=mesh['px'=4,'py'=8] {'px'}, use_global_device_ids=true, to_apply=%region_2.3 | all-reduce | flops 4 | bytes 32 | tf_op jit(solution)/shard_map/psum | solution.py:509
  196.4 6.5 %inverse_y.1 = bf16[2,128,64,128]{3,2,1,0:T(8,128)(2,1)} custom-call(bf16[256,256]{1,0:T(8,128)(2,1)} %constant.145.clone.table_ref, bf16[4,32,128,128]{3,2,1,0:T(8,128)(2,1)} %all-to-all-done.4.in_ref), custom_call_target="tpu_custom_call" | custom-call | tf_op jit(solution)/shard_map/inverse_y/pallas_call | solution.py:113
  (52 shorter events, 5.1 us)
Async XLA Ops:
  2.8 15.1 %all-to-all-start = ((bf16[32,4,3,128]{3,1,2,0:T(4,128)(2,1)}), bf16[32,4,3,128]{3,1,2,0:T(4,128)(2,1)S(1)}, u32[]{:S(2)}, u32[]{:S(2)}) async-start(bf16[32,4,3,128]{3,1,2,0:T(4,128)(2,1)} %broadcast_in_dim.64), calls=%async_computation | async-start | bytes 196608 | tf_op jit(solution)/shard_map/all_to_all | solution.py:393
  16.6 6.2 %copy-start.1 = (f32[128]{0:T(128)S(1)}, f32[128]{0:T(128)}, u32[]{:S(2)}) copy-start(f32[128]{0:T(128)} %thick_ref.5) | copy-start | bytes 1540
  16.6 7.5 %copy-start.10 = (f32[64]{0:T(128)S(1)}, f32[64]{0:T(128)}, u32[]{:S(2)}) copy-start(f32[64]{0:T(128)} %constant.149.clone) | copy-start | bytes 772
  16.6 7.6 %copy-start.7 = (f32[64,64]{0,1:T(8,128)S(1)}, f32[64,64]{0,1:T(8,128)}, u32[]{:S(2)}) copy-start(f32[64,64]{0,1:T(8,128)} %constant.147.clone) | copy-start | bytes 49156
  16.6 8.9 %copy-start.9 = (f32[4,128]{1,0:T(4,128)S(1)}, f32[4,128]{1,0:T(4,128)}, u32[]{:S(2)}) copy-start(f32[4,128]{1,0:T(4,128)} %constant.156) | copy-start | bytes 6148
  16.6 10.1 %copy-start.5 = (f32[64,64]{1,0:T(8,128)S(1)}, f32[64,64]{1,0:T(8,128)}, u32[]{:S(2)}) copy-start(f32[64,64]{1,0:T(8,128)} %constant.157) | copy-start | bytes 49156
  16.6 11.1 %copy-start.6 = (bf16[512,512]{1,0:T(8,128)(2,1)S(1)}, bf16[512,512]{1,0:T(8,128)(2,1)}, u32[]{:S(2)}) copy-start(bf16[512,512]{1,0:T(8,128)(2,1)} %constant.146.clone.table_ref) | copy-start | bytes 1572868
  17.9 52.9 %all-to-all-start.1 = ((bf16[4,32,128,128]{3,2,1,0:T(8,128)(2,1)}), bf16[4,32,128,128]{3,2,1,0:T(8,128)(2,1)}, u32[]{:S(2)}, u32[]{:S(2)}) async-start(bf16[4,32,128,128]{3,2,1,0:T(8,128)(2,1)} %forward_y.1), calls=%async_computation.1 | async-start | bytes 8388608 | tf_op jit(solution)/shard_map/all_to_all | solution.py:437
  26.5 77.6 %copy-start = (bf16[16,512]{1,0:T(8,128)(2,1)S(1)}, bf16[16,512]{1,0:T(8,128)(2,1)}, u32[]{:S(2)}) copy-start(bf16[16,512]{1,0:T(8,128)(2,1)} %constant.151.clone.spread_ref) | copy-start | bytes 49156
  26.6 77.6 %copy-start.2 = (f32[128]{0:T(128)S(1)}, f32[128]{0:T(128)}, u32[]{:S(2)}) copy-start(f32[128]{0:T(128)} %thick_ref.5) | copy-start | bytes 1540
  26.6 77.6 %copy-start.4 = (f32[128]{0:T(128)S(1)}, f32[128]{0:T(128)}, u32[]{:S(2)}) copy-start(f32[128]{0:T(128)} %pad_maximum_fusion.gap_ref) | copy-start | bytes 1540
  90.0 14.2 %all-to-all-start.2 = ((bf16[32,16,256]{2,1,0:T(8,128)(2,1)}), bf16[32,16,256]{2,1,0:T(8,128)(2,1)S(1)}, u32[]{:S(2)}, u32[]{:S(2)}) async-start(bf16[32,16,256]{2,1,0:T(8,128)(2,1)} %bitcast.36), calls=%async_computation.2 | async-start | bytes 524288 | tf_op jit(solution)/shard_map/all_to_all | solution.py:459
  139.6 5.0 %copy-start.3 = (f32[128]{0:T(128)S(1)}, f32[128]{0:T(128)}, u32[]{:S(2)}) copy-start(f32[128]{0:T(128)} %thick_ref.5) | copy-start | bytes 1540
  139.6 5.0 %copy-start.8 = (f32[2,128,128]{2,1,0:T(8,128)S(1)}, f32[2,128,128]{2,1,0:T(8,128)}, u32[]{:S(2)}) copy-start(f32[2,128,128]{2,1,0:T(8,128)} %get-tuple-element.9) | copy-start | bytes 393220
  139.6 56.8 %all-to-all-start.4 = ((bf16[4,32,128,128]{3,2,1,0:T(8,128)(2,1)}), bf16[4,32,128,128]{3,2,1,0:T(8,128)(2,1)}, u32[]{:S(2)}, u32[]{:S(2)}) async-start(bf16[4,32,128,128]{3,2,1,0:T(8,128)(2,1)} %get-tuple-element.8), calls=%async_computation.4 | async-start | bytes 8388608 | tf_op jit(solution)/shard_map/all_to_all | solution.py:504

commit v5 on v4

--- a/solution.py
+++ b/solution.py
@@ -15,6 +15,7 @@
 SMEM = pltpu.MemorySpace.SMEM
 LANES = 128
 CHUNK = 64
+BATCH = 8
 
 
 def sine_table(length):
@@ -41,36 +42,40 @@
     return group if group // 8 % 2 else group + 8
 
 
-def forward_y_kernel(table_ref, grid_ref, out_ref, scratch):
+def forward_y_kernel(me_ref, table_ref, grid_ref, *refs):
+    outs, scratch = refs[:-1], refs[-1]
     _, x_chunk, rows, layers = grid_ref.shape
-    pieces, part = out_ref.shape[:2]
+    part = outs[0].shape[0]
     group = table_ref.shape[0] // rows
+    pitch = pitch_of(x_chunk)
     for start in range(0, x_chunk, group):
         block = grid_ref[0, start : start + group].reshape(group * rows, layers)
         result = contract(table_ref[...], block, 1, 0)
         for at in range(group):
-            scratch[pl.ds(start + at, rows, stride=pitch_of(x_chunk)), :] = result[
+            scratch[pl.ds(start + at, rows, stride=pitch), :] = result[
                 at * rows : (at + 1) * rows
             ]
-    for b in range(rows):
-        begin = b * pitch_of(x_chunk)
-        out_ref[b // part, b % part] = scratch[begin : begin + x_chunk, :].astype(jnp.bfloat16)
-
-
-def inverse_y_kernel(table_ref, in_ref, out_ref, scratch):
+    for f, out in enumerate(outs):
+        first = (me_ref[1] ^ f) * part
+        for b in range(part):
+            begin = pl.multiple_of((first + b) * pitch, 8)
+            out[b] = scratch[pl.ds(begin, x_chunk), :].astype(jnp.bfloat16)
+
+
+def inverse_y_kernel(pieces, me_ref, table_ref, *refs):
+    ins, out_ref, scratch = refs[:pieces], refs[-2], refs[-1]
     _, x_chunk, rows, layers = out_ref.shape
+    part = ins[0].shape[0]
     group = table_ref.shape[0] // rows
-    part = in_ref.shape[1]
-    for b in range(rows):
-        begin = b * pitch_of(x_chunk)
-        scratch[begin : begin + x_chunk, :] = in_ref[b // part, b % part].astype(jnp.float32)
+    pitch = pitch_of(x_chunk)
+    for f, value in enumerate(ins):
+        first = (me_ref[1] ^ f) * part
+        for b in range(part):
+            begin = pl.multiple_of((first + b) * pitch, 8)
+            scratch[pl.ds(begin, x_chunk), :] = value[b].astype(jnp.float32)
     for start in range(0, x_chunk, group):
         block = jnp.concatenate(
-            [
-                scratch[pl.ds(start + at, rows, stride=pitch_of(x_chunk)), :]
-                for at in range(group)
-            ],
-            axis=0,
+            [scratch[pl.ds(start + at, rows, stride=pitch), :] for at in range(group)], axis=0
         ).astype(jnp.bfloat16)
         result = contract(table_ref[...], block, 1, 0)
         out_ref[0, start : start + group] = result.reshape(group, rows, layers).astype(
@@ -83,46 +88,59 @@
     return bf16(np.kron(np.eye(group), sine_table(rows)))
 
 
-def forward_y(carried, count):
+def forward_y(me, carried, pieces, step):
     modes, x_local, rows, layers = carried.shape
     chunk = min(CHUNK, x_local)
-    pieces = count // modes
     part = rows // pieces
     table = y_table(rows)
     return pl.pallas_call(
         forward_y_kernel,
-        grid=(modes, x_local // chunk),
-        in_specs=[
-            pl.BlockSpec(table.shape, lambda m, i: (0, 0)),
-            pl.BlockSpec((1, chunk, rows, layers), lambda m, i: (m, i, 0, 0)),
-        ],
-        out_specs=pl.BlockSpec((pieces, part, chunk, layers), lambda m, i: (m, 0, i, 0)),
-        out_shape=jax.ShapeDtypeStruct((count, part, x_local, layers), jnp.bfloat16),
-        scratch_shapes=[pltpu.VMEM(((rows + 1) * pitch_of(chunk), layers), jnp.float32)],
+        grid_spec=pltpu.PrefetchScalarGridSpec(
+            num_scalar_prefetch=1,
+            grid=(x_local // chunk,),
+            in_specs=[
+                pl.BlockSpec(table.shape, lambda i, own: (0, 0)),
+                pl.BlockSpec((1, chunk, rows, layers), lambda i, own: (own[0] ^ step, i, 0, 0)),
+            ],
+            out_specs=[pl.BlockSpec((part, chunk, layers), lambda i, own: (0, i, 0))] * pieces,
+            scratch_shapes=[pltpu.VMEM(((rows + 1) * pitch_of(chunk), layers), jnp.float32)],
+        ),
+        out_shape=[jax.ShapeDtypeStruct((part, x_local, layers), jnp.bfloat16)] * pieces,
         compiler_params=pltpu.CompilerParams(vmem_limit_bytes=VMEM_LIMIT),
         name="forward_y",
-    )(table, carried)
-
-
-def inverse_y(spectra, rows):
-    count, part, x_local, layers = spectra.shape
-    pieces = rows // part
-    modes = count // pieces
+    )(me, table, carried)
+
+
+def inverse_y(me, spectra, rows, modes, step, pressure):
+    pieces = len(spectra)
+    part, x_local, layers = spectra[0].shape
     chunk = min(CHUNK, x_local)
     table = y_table(rows)
+    earlier = [] if pressure is None else [pressure]
     return pl.pallas_call(
-        inverse_y_kernel,
-        grid=(modes, x_local // chunk),
-        in_specs=[
-            pl.BlockSpec(table.shape, lambda m, i: (0, 0)),
-            pl.BlockSpec((pieces, part, chunk, layers), lambda m, i: (m, 0, i, 0)),
-        ],
-        out_specs=pl.BlockSpec((1, chunk, rows, layers), lambda m, i: (m, i, 0, 0)),
+        functools.partial(inverse_y_kernel, pieces),
+        grid_spec=pltpu.PrefetchScalarGridSpec(
+            num_scalar_prefetch=1,
+            grid=(x_local // chunk,),
+            in_specs=[pl.BlockSpec(table.shape, lambda i, own: (0, 0))]
+            + [pl.BlockSpec((part, chunk, layers), lambda i, own: (0, i, 0))] * pieces
+            + [pl.BlockSpec(memory_space=pl.ANY)] * len(earlier),
+            out_specs=pl.BlockSpec(
+                (1, chunk, rows, layers), lambda i, own: (own[0] ^ step, i, 0, 0)
+            ),
+            scratch_shapes=[pltpu.VMEM(((rows + 1) * pitch_of(chunk), layers), jnp.float32)],
+        ),
         out_shape=jax.ShapeDtypeStruct((modes, x_local, rows, layers), jnp.bfloat16),
-        scratch_shapes=[pltpu.VMEM(((rows + 1) * pitch_of(chunk), layers), jnp.float32)],
+        input_output_aliases={2 + pieces: 0} if earlier else {},
         compiler_params=pltpu.CompilerParams(vmem_limit_bytes=VMEM_LIMIT),
         name="inverse_y",
-    )(table, spectra)
+    )(me, table, *spectra, *earlier)
+
+
+def swap(values, distance):
+    return lax.ppermute(
+        values, "px", [(k, k ^ distance) for k in range(lax.axis_size("px"))]
+    )
 
 
 def at_layer(k, group, pitch):
@@ -197,32 +215,41 @@
 
 
 def block_ends_kernel(
-    thick_ref, gap_ref, wave_ref, ends_ref, table_ref, strip_table_ref, factor_ref, velocity_ref,
-    rows_ref,
-    saved_ref, out_ref, spectrum_ref, lower_ref, half_ref, end_ref, buffer, arrived, done,
+    count, me_ref, thick_ref, gap_ref, wave_ref, ends_ref, table_ref, strip_table_ref, factor_ref, velocity_ref,
+    *refs,
 ):
-    count, part, _, layers = rows_ref.shape
+    rows_refs, (saved_ref, out_ref, spectrum_ref, lower_ref, half_ref) = refs[:count], refs[count : count + 5]
+    end_ref, buffer, arrived, done = refs[count + 5 :]
+    part, _, layers = rows_refs[0].shape
+    each = min(BATCH, part)
+    me = me_ref[0]
     tiles, group, _ = wave_ref.shape
     if group > part:
         spectrum_ref[...] = jnp.zeros_like(spectrum_ref)
 
-    def fetch(b):
-        return pltpu.make_async_copy(rows_ref.at[:, b], buffer.at[b], arrived.at[b])
-
-    for b in range(part):
-        fetch(b).start()
+    def fetch(at, d):
+        some = pl.ds(at * each, each)
+        return pltpu.make_async_copy(
+            rows_refs[d].at[some], buffer.at[me ^ d, some], arrived.at[at, d]
+        )
+
+    for at in range(part // each):
+        for d in range(count):
+            fetch(at, d).start()
 
     def transform(b, carry):
-        fetch(b).wait()
         strips = (factor_ref[b] * velocity_ref[...]).astype(jnp.bfloat16)
-        left = jnp.concatenate([buffer[b, c] for c in range(count)], axis=0)
+        left = jnp.concatenate([buffer[c, b] for c in range(count)], axis=0)
         result = contract(left, table_ref[...], 0, 0) + contract(
             strips, strip_table_ref[...], 1, 0
         )
         put_rows(spectrum_ref, 0, b, group, result)
         return carry
 
-    lax.fori_loop(0, part, transform, 0, unroll=2)
+    for at in range(part // each):
+        for d in range(count):
+            fetch(at, d).wait()
+        lax.fori_loop(at * each, (at + 1) * each, transform, 0, unroll=2)
     saving = pltpu.make_async_copy(spectrum_ref, saved_ref, done)
     saving.start()
     eliminate(
@@ -299,11 +326,15 @@
 
 
 def block_solve_kernel(
-    thick_ref, gap_ref, wave_ref, ends_ref, table_ref, strip_table_ref, factor_ref, velocity_ref,
+    count, me_ref, thick_ref, gap_ref, wave_ref, ends_ref, table_ref, strip_table_ref, factor_ref, velocity_ref,
     bound_ref,
-    saved_ref, out_ref, mass_ref, lower_ref, spectrum_ref, edge_ref, outgoing, arrived, sent,
+    saved_ref, *refs,
 ):
-    count, part, x_local, layers = out_ref.shape
+    outs, (mass_ref, lower_ref, spectrum_ref, edge_ref) = refs[:count], refs[count : count + 4]
+    outgoing, arrived, sent = refs[count + 4 :]
+    part, x_local, layers = outs[0].shape
+    each = min(BATCH, part)
+    me = me_ref[0]
     tiles, group, _ = wave_ref.shape
     pieces = arrived.shape[0]
     size = layers * pitch_of(group) // pieces
@@ -340,8 +371,9 @@
 
     substitute(layers, 1, lower_ref, spectrum_ref, use)
 
-    def send(b):
-        return pltpu.make_async_copy(outgoing.at[b], out_ref.at[:, b], sent.at[b])
+    def send(at, d):
+        some = pl.ds(at * each, each)
+        return pltpu.make_async_copy(outgoing.at[me ^ d, some], outs[d].at[some], sent.at[at, d])
 
     def transform(pair, at_strips):
         first = pair * 2
@@ -353,19 +385,25 @@
             b = first + at
             found = result[:, at * layers : (at + 1) * layers]
             for c in range(count):
-                outgoing[b, c] = found[c * x_local : (c + 1) * x_local].astype(jnp.bfloat16)
-            send(b).start()
+                outgoing[c, b] = found[c * x_local : (c + 1) * x_local].astype(jnp.bfloat16)
         found = contract(solved, strip_table_ref[...], 1, 1)
         for at in range(2):
             at_strips += found[at * layers : (at + 1) * layers] * factor_ref[first + at]
         return at_strips
 
     nothing = jnp.zeros(velocity_ref.shape[1:], jnp.float32)
-    at_strips = lax.fori_loop(0, part // 2, transform, nothing, unroll=4)
+    at_strips = nothing
+    for at in range(part // each):
+        at_strips = lax.fori_loop(
+            at * each // 2, (at + 1) * each // 2, transform, at_strips, unroll=True
+        )
+        for d in range(count):
+            send(at, d).start()
     for mode in range(velocity_ref.shape[0]):
         mass_ref[mode] = at_strips * velocity_ref[mode]
-    for b in range(part):
-        send(b).wait()
+    for at in range(part // each):
+        for d in range(count):
+            send(at, d).wait()
 
 
 def shards(carried, velocity, strip_column, thick):
@@ -392,7 +430,14 @@
     packed = jnp.broadcast_to(packed[None], (devices,) + packed.shape)
     gathered = lax.all_to_all(packed, both, split_axis=0, concat_axis=0, tiled=True)
     gathered = gathered.reshape(strip_count, modes + 1, layers)
-    spectra = forward_y(carried, count_px)
+    own = index_px.astype(jnp.int32).reshape(1)
+    place = jnp.stack([own_mode, own_piece]).astype(jnp.int32)
+    rows = [None] * count_px
+    for step in reversed(range(modes)):
+        chunks = forward_y(place, carried, pieces, step)
+        for f, chunk in enumerate(chunks):
+            d = step * pieces + f
+            rows[d] = swap(chunk, d) if d else chunk
     code = gathered[:, modes, :3].astype(jnp.int32)
     column = code[:, 0] * 65536 + code[:, 1] * 256 + code[:, 2]
     all_velocity = gathered[:, :modes].astype(jnp.float32).transpose(1, 2, 0)
@@ -434,10 +479,9 @@
     float32 = jnp.float32
     tiles_x, tiles_y = width_x // LANES, width_y // LANES
 
-    rows = lax.all_to_all(spectra, "px", split_axis=0, concat_axis=0, tiled=True)
     spectrum, block_ends = pl.pallas_call(
-        block_ends_kernel,
-        in_specs=[smem, smem] + [vmem] * 6 + [anywhere],
+        functools.partial(block_ends_kernel, count_px),
+        in_specs=[smem] * 3 + [vmem] * 6 + [anywhere] * count_px,
         out_specs=[anywhere, vmem],
         out_shape=[
             jax.ShapeDtypeStruct((1, tiles_x, (layers + 1) * pitch_of(group), LANES), float32),
@@ -448,13 +492,13 @@
             pltpu.VMEM((tiles_x, layers * group, LANES), float32),
             pltpu.VMEM((1, tiles_x, (layers + 1) * pitch_of(group), LANES), float32),
             pltpu.VMEM((2, tiles_x, layers, LANES), float32),
-            pltpu.VMEM((part, count_px, x_local, layers), jnp.bfloat16),
-            pltpu.SemaphoreType.DMA((part,)),
+            pltpu.VMEM((count_px, part, x_local, layers), jnp.bfloat16),
+            pltpu.SemaphoreType.DMA((part // min(BATCH, part), count_px)),
             pltpu.SemaphoreType.DMA(()),
         ],
         compiler_params=params,
         name="block_ends",
-    )(thick, gap, wave_b, ends, table_x, table_strips, factor, own_velocity, rows)
+    )(own, thick, gap, wave_b, ends, table_x, table_strips, factor, own_velocity, *rows)
 
     arrived = lax.all_to_all(block_ends, both, split_axis=0, concat_axis=0, tiled=True)
     outgoing = pl.pallas_call(
@@ -480,33 +524,41 @@
         outgoing.reshape(width_x, 2 * layers), both, split_axis=0, concat_axis=0, tiled=True
     )
 
-    returned, mass = pl.pallas_call(
-        block_solve_kernel,
-        in_specs=[smem, smem] + [vmem] * 7 + [anywhere],
-        out_specs=[anywhere, vmem],
-        out_shape=[
-            jax.ShapeDtypeStruct((count_px, part, x_local, layers), jnp.bfloat16),
+    *returned, mass = pl.pallas_call(
+        functools.partial(block_solve_kernel, count_px),
+        in_specs=[smem] * 3 + [vmem] * 7 + [anywhere],
+        out_specs=[anywhere] * count_px + [vmem],
+        out_shape=[jax.ShapeDtypeStruct((part, x_local, layers), jnp.bfloat16)] * count_px
+        + [
             jax.ShapeDtypeStruct((modes, layers, strip_count), float32),
         ],
         scratch_shapes=[
             pltpu.VMEM((tiles_x, layers * group, LANES), float32),
             pltpu.VMEM((1, tiles_x, (layers + 1) * pitch_of(group), LANES), float32),
             pltpu.VMEM((2, tiles_x, layers, LANES), float32),
-            pltpu.VMEM((part, count_px, x_local, layers), jnp.bfloat16),
+            pltpu.VMEM((count_px, part, x_local, layers), jnp.bfloat16),
             pltpu.SemaphoreType.DMA((8,)),
-            pltpu.SemaphoreType.DMA((part,)),
+            pltpu.SemaphoreType.DMA((part // min(BATCH, part), count_px)),
         ],
         compiler_params=params,
         name="block_solve",
     )(
-        thick, gap, wave_b, ends, table_x, table_strips, factor, all_velocity, bounds, spectrum
-    )
-    back = lax.all_to_all(returned, "px", split_axis=0, concat_axis=0, tiled=True)
-    pressure = inverse_y(back, y_local)
+        own, thick, gap, wave_b, ends, table_x, table_strips, factor, all_velocity, bounds,
+        spectrum,
+    )
+    back = [swap(chunk, d) if d else chunk for d, chunk in enumerate(returned)]
     own_row = (jnp.arange(modes) == own_mode)[:, None]
     local_mass = jnp.sum(mass * thick[None, :, None], axis=(1, 2))
     local_mass = jnp.where(own_row, local_mass[None, :], 0.0)
-    added_mass = lax.psum(lax.psum(local_mass, "py"), "px") / (strip_count * layers)
+    local_mass = lax.psum(local_mass, "py")
+    pressure = None
+    for step in range(modes):
+        chunks = back[step * pieces : (step + 1) * pieces]
+        pressure = inverse_y(place, chunks, y_local, modes, step, pressure)
+        if step == 0:
+            pressure, local_mass = lax.optimization_barrier((pressure, local_mass))
+            every_mass = lax.all_gather(local_mass, "px", axis=0, tiled=False)
+    added_mass = jnp.sum(every_mass, axis=0) / (strip_count * layers)
     return (pressure, added_mass)
 
 

time: 204 us -> 192 us (0.941)
  blocking collectives: 63.8 us -> 46.5 us
  local copies, waits for them, and re-layouts: 6.6 us -> 9.58 us
  Pallas kernels: 54.1 us -> 56.4 us
    ppermute x0 -> x6, waiting for transfers between devices: none -> 40.4 us  [swap(): lax.ppermute(values, 'px', [(k, k ^ distance) for k in range(lax.axis_siz...]
    all_to_all x2 -> x0, waiting for transfers between devices: 39.6 us -> none  [the longest x1 39.6 us: shards(): lax.all_to_all(spectra, 'px', split_axis=0, concat_axis=0, tiled=True)]
    psum x2 -> x1, blocking collectives: 51 us -> 14 us  [shards(): local_mass = lax.psum(local_mass, 'py')]
    all_gather x0 -> x1, blocking collectives: none -> 19.7 us  [shards(): every_mass = lax.all_gather(local_mass, 'px', axis=0, tiled=False)]
    all_to_all x2 -> x0, starting transfers between devices: 9.84 us -> none  [the longest x1 4.99 us: shards(): lax.all_to_all(returned, 'px', split_axis=0, concat_axis=0, tiled=True)]
    ppermute x0 -> x6, starting transfers between devices: none -> 7.07 us  [swap(): lax.ppermute(values, 'px', [(k, k ^ distance) for k in range(lax.axis_siz...]
    unnamed x24 -> x32, local copies, waits for them, and re-layouts: 0.24 us -> 3.18 us
    pallas_call x4 -> x6, Pallas kernels: 45.8 us -> 48.1 us  [the longest x1 15.8 us: shards(): pl.pallas_call(functools.partial(block_ends_kernel, count_px), in_specs=[...]
  transfers between devices with their start and end apart: 4 -> 8, of which waited for: 3 -> 4; matrix products, arithmetic and copies ran while one was open for 5% -> 6% of each run, Pallas kernels for 3% -> 7%
where the time goes in v5:
time: 192 us; the launch traced here: 191 us
  Pallas kernels  56.4 us (29%)
  waiting for transfers between devices  50 us (26%)
  blocking collectives  46.5 us (24%)
  starting transfers between devices  20.1 us (10%)
  local copies, waits for them, and re-layouts  9.58 us (5%)
  other arithmetic  7.15 us (4%)
    ppermute x6, waiting for transfers between devices, swap(): lax.ppermute(values, 'px', [(k, k ^ distance) for k in range(lax.axis_siz...  40.4 us
    all_gather x1, blocking collectives, shards(): every_mass = lax.all_gather(local_mass, 'px', axis=0, tiled=False)  19.7 us
    pallas_call x1, Pallas kernels, shards(): pl.pallas_call(functools.partial(block_ends_kernel, count_px), in_specs=[...  15.8 us
    psum x1, blocking collectives, shards(): local_mass = lax.psum(local_mass, 'py')  14 us
    pallas_call x1, Pallas kernels, shards(): pl.pallas_call(functools.partial(block_solve_kernel, count_px), in_specs=...  13.7 us
    all_to_all x1, blocking collectives, shards(): lax.all_to_all(outgoing.reshape(width_x, 2 * layers), both, split_axis=0,...  12.8 us
    all_to_all x1, waiting for transfers between devices, shards(): lax.all_to_all(block_ends, both, split_axis=0, concat_axis=0, tiled=True)  9.54 us
    pallas_call x2, Pallas kernels, inverse_y(): pl.pallas_call(functools.partial(inverse_y_kernel, pieces), grid_spec=plt...  9.33 us
  transfers between devices with their start and end apart: 8, of which 4 were waited for; matrix products, arithmetic and copies ran while one was open for 6% of the time, Pallas kernels for 7%

profile of v5, /device:TPU:0, one launch (start us, length us, event | category | flops | bytes accessed | tf_op | source)
XLA Modules:
  0.0 191.2 jit_solution(15648453021513124976)
XLA Ops:
  2.8 7.3 %all-to-all-start = ((bf16[32,4,3,128]{3,1,2,0:T(4,128)(2,1)}), bf16[32,4,3,128]{3,1,2,0:T(4,128)(2,1)S(1)}, u32[]{:S(2)}, u32[]{:S(2)}) async-start(bf16[32,4,3,128]{3,1,2,0:T(4,128)(2,1)} %broadcast_in_dim.64), calls=%async_computation | async-start | bytes 196608 | tf_op jit(solution)/shard_map/all_to_all | solution.py:431
  10.8 4.7 %forward_y.3 = (bf16[32,128,128]{2,1,0:T(8,128)(2,1)}, bf16[32,128,128]{2,1,0:T(8,128)(2,1)}) custom-call(s32[2]{0:T(128)} %get-tuple-element.36.me_ref, bf16[256,256]{1,0:T(8,128)(2,1)} %constant.145.clone.table_ref, bf16[2,128,64,128]{3,2,1,0:T(8,128)(2,1)} %grid_ref.3), custom_call_target="tpu_custom_call" | custom-call | tf_op jit(solution)/shard_map/forward_y/pallas_call | solution.py:96
  15.5 1.8 collective-permute-start.1
  17.3 1.5 collective-permute-start.2
  18.7 4.5 %forward_y.2 = (bf16[32,128,128]{2,1,0:T(8,128)(2,1)}, bf16[32,128,128]{2,1,0:T(8,128)(2,1)}) custom-call(s32[2]{0:T(128)} %get-tuple-element.36.me_ref, bf16[256,256]{1,0:T(8,128)(2,1)} %constant.145.clone.table_ref, bf16[2,128,64,128]{3,2,1,0:T(8,128)(2,1)} %grid_ref.3), custom_call_target="tpu_custom_call" | custom-call | tf_op jit(solution)/shard_map/forward_y/pallas_call | solution.py:96
  28.6 1.5 gather_fusion.1
  32.0 31.5 %collective-permute-done.1.refs_2_ = bf16[32,128,128]{2,1,0:T(8,128)(2,1)S(1)} collective-permute-done((bf16[32,128,128]{2,1,0:T(8,128)(2,1)}, bf16[32,128,128]{2,1,0:T(8,128)(2,1)S(1)}, u32[]{:S(2)}, u32[]{:S(2)}) %collective-permute-start.1) | collective-permute-done | bytes 1048608 | tf_op jit(solution)/shard_map/ppermute | solution.py:141
  63.5 1.3 collective-permute-done.refs_1_
  65.5 15.8 %block_ends.1 = (f32[1,4,5160,128]{3,2,1,0:T(8,128)}, bf16[512,256]{1,0:T(8,128)(2,1)}) custom-call(s32[1]{0:T(128)} %bitcast.2.me_ref, f32[128]{0:T(128)} %thick_ref.5, f32[128]{0:T(128)} %pad_maximum_fusion.gap_ref, f32[4,32,128]{2,1,0:T(8,128)} %broadcast_add_fusion.wave_ref, f32[2,32,128]{2,1,0:T(8,128)} %broadcast_in_dim.62.ends_ref, ...), custom_call_target="tpu_custom_call" | custom-call | tf_op jit(solution)/shard_map/block_ends/pallas_call | solution.py:482
  81.3 5.7 %all-to-all-start.1 = ((bf16[32,16,256]{2,1,0:T(8,128)(2,1)}), bf16[32,16,256]{2,1,0:T(8,128)(2,1)S(1)}, u32[]{:S(2)}, u32[]{:S(2)}) async-start(bf16[32,16,256]{2,1,0:T(8,128)(2,1)} %bitcast.40), calls=%async_computation.1 | async-start | bytes 524288 | tf_op jit(solution)/shard_map/all_to_all | solution.py:503
  87.9 9.5 %all-to-all-done.1 = bf16[32,16,256]{2,1,0:T(8,128)(2,1)S(1)} async-done(((bf16[32,16,256]{2,1,0:T(8,128)(2,1)}), bf16[32,16,256]{2,1,0:T(8,128)(2,1)S(1)}, u32[]{:S(2)}, u32[]{:S(2)}) %all-to-all-start.1) | async-done | bytes 262176 | tf_op jit(solution)/shard_map/all_to_all | solution.py:503
  97.5 8.3 %interface.1 = bf16[2,2,128,256]{3,2,1,0:T(8,128)(2,1)S(1)} custom-call(f32[128]{0:T(128)S(1)} %copy-done.2, f32[128]{0:T(128)S(1)} %copy-done.4, f32[4,16,128]{2,1,0:T(8,128)S(1)} %broadcast_add_fusion.1.wave_ref, bf16[16,512]{1,0:T(8,128)(2,1)S(1)} %copy-done, bf16[2,2,128,256]{3,2,1,0:T(8,128)(2,1)S(1)} %bitcast.35), custom_call_target="tpu_custom_call" | custom-call | tf_op jit(solution)/shard_map/interface/pallas_call | solution.py:504
  105.8 12.8 %all_to_all.25 = bf16[32,16,256]{2,1,0:T(8,128)(2,1)} all-to-all(bf16[32,16,256]{2,1,0:T(8,128)(2,1)S(1)} %bitcast.36), channel_id=1, replica_groups=mesh['px'=4,'py'=8] {'px','py'}, dimensions={0} | all-to-all | bytes 524288 | tf_op jit(solution)/shard_map/all_to_all | solution.py:523
  118.6 13.7 %block_solve.1 = (bf16[32,128,128]{2,1,0:T(8,128)(2,1)}, bf16[32,128,128]{2,1,0:T(8,128)(2,1)}, bf16[32,128,128]{2,1,0:T(8,128)(2,1)}, bf16[32,128,128]{2,1,0:T(8,128)(2,1)}, f32[2,128,128]{2,1,0:T(8,128)}) custom-call(s32[1]{0:T(128)} %bitcast.2.me_ref, f32[128]{0:T(128)} %thick_ref.5, f32[128]{0:T(128)} %pad_maximum_fusion.gap_ref, ...), custom_call_target="tpu_custom_call" | custom-call | tf_op jit(solution)/shard_map/block_solve/pallas_call | solution.py:527
  133.7 2.2 %collective-permute-start.4 = (bf16[32,128,128]{2,1,0:T(8,128)(2,1)}, bf16[32,128,128]{2,1,0:T(8,128)(2,1)S(1)}, u32[]{:S(2)}, u32[]{:S(2)}) collective-permute-start(bf16[32,128,128]{2,1,0:T(8,128)(2,1)} %get-tuple-element.22), channel_id=1, source_target_pairs={{0,24},{8,16},{16,8},{24,0},{1,25},{9,17},{17,9},{25,1},{2,26},{10... | collective-permute-start | bytes 3145736 | tf_op jit(solution)/shard_map/ppermute | solution.py:141
  135.9 1.1 multiply_reduce_fusion
  137.1 14.0 %psum.7 = f32[2,2]{1,0:T(2,128)S(1)} all-reduce(f32[2,2]{1,0:T(2,128)S(1)} %broadcast_select_fusion.1), channel_id=1, replica_groups=mesh['px'=4,'py'=8] {'py'}, use_global_device_ids=true, to_apply=%region_1.2 | all-reduce | flops 4 | bytes 32 | tf_op jit(solution)/shard_map/psum | solution.py:553
  151.0 7.6 %collective-permute-done.5.refs_1_ = bf16[32,128,128]{2,1,0:T(8,128)(2,1)S(1)} collective-permute-done((bf16[32,128,128]{2,1,0:T(8,128)(2,1)}, bf16[32,128,128]{2,1,0:T(8,128)(2,1)S(1)}, u32[]{:S(2)}, u32[]{:S(2)}) %collective-permute-start.5) | collective-permute-done | bytes 1048608 | tf_op jit(solution)/shard_map/ppermute | solution.py:141
  158.6 1.0 copy-done.8
  159.6 4.7 %inverse_y.2.refs_2_ = bf16[2,128,64,128]{3,2,1,0:T(8,128)(2,1)} custom-call(s32[2]{0:T(128)} %get-tuple-element.36.me_ref, bf16[256,256]{1,0:T(8,128)(2,1)} %constant.145.clone.table_ref, bf16[32,128,128]{2,1,0:T(8,128)(2,1)} %get-tuple-element.23.refs_0_, bf16[32,128,128]{2,1,0:T(8,128)(2,1)} %copy-done.8), custom_call_target="tpu_custom_call" | custom-call | tf_op jit(solution)/shard_map/inverse_y/pallas_call | solution.py:120
  164.2 19.7 %all-gather.1 = f32[4,2,2]{2,1,0:T(2,128)S(1)} all-gather(f32[1,2,2]{2,1,0:T(2,128)S(1)} %bitcast.43), channel_id=2, replica_groups=mesh['px'=4,'py'=8] {'px'}, dimensions={0}, use_global_device_ids=true | all-gather | bytes 80 | tf_op jit(solution)/shard_map/all_gather | solution.py:560
  184.5 1.0 copy-done.11
  185.5 1.0 copy-done.12
  186.5 4.7 %inverse_y.3 = bf16[2,128,64,128]{3,2,1,0:T(8,128)(2,1)} custom-call(s32[2]{0:T(128)} %get-tuple-element.36.me_ref, bf16[256,256]{1,0:T(8,128)(2,1)} %constant.145.clone.table_ref, bf16[32,128,128]{2,1,0:T(8,128)(2,1)} %copy-done.11, bf16[32,128,128]{2,1,0:T(8,128)(2,1)} %copy-done.12, ...), custom_call_target="tpu_custom_call", output_to_operand_aliasing={{}: (4, {})} | custom-call | tf_op jit(solution)/shard_map/inverse_y/pallas_call | solution.py:120
  (71 shorter events, 12.9 us)
Async XLA Ops:
  2.8 24.2 %all-to-all-start = ((bf16[32,4,3,128]{3,1,2,0:T(4,128)(2,1)}), bf16[32,4,3,128]{3,1,2,0:T(4,128)(2,1)S(1)}, u32[]{:S(2)}, u32[]{:S(2)}) async-start(bf16[32,4,3,128]{3,1,2,0:T(4,128)(2,1)} %broadcast_in_dim.64), calls=%async_computation | async-start | bytes 196608 | tf_op jit(solution)/shard_map/all_to_all | solution.py:431
  10.8 12.7 %copy-start.1 = (f32[128]{0:T(128)S(1)}, f32[128]{0:T(128)}, u32[]{:S(2)}) copy-start(f32[128]{0:T(128)} %thick_ref.5) | copy-start | bytes 1540
  10.8 13.4 %copy-start.14 = (f32[64]{0:T(128)S(1)}, f32[64]{0:T(128)}, u32[]{:S(2)}) copy-start(f32[64]{0:T(128)} %constant.149.clone) | copy-start | bytes 772
  10.8 13.5 %copy-start.7 = (f32[64,64]{0,1:T(8,128)S(1)}, f32[64,64]{0,1:T(8,128)}, u32[]{:S(2)}) copy-start(f32[64,64]{0,1:T(8,128)} %constant.147.clone) | copy-start | bytes 49156
  10.8 15.5 %copy-start.13 = (f32[4,128]{1,0:T(4,128)S(1)}, f32[4,128]{1,0:T(4,128)}, u32[]{:S(2)}) copy-start(f32[4,128]{1,0:T(4,128)} %constant.156) | copy-start | bytes 6148
  10.8 16.7 %copy-start.6 = (f32[64,64]{1,0:T(8,128)S(1)}, f32[64,64]{1,0:T(8,128)}, u32[]{:S(2)}) copy-start(f32[64,64]{1,0:T(8,128)} %constant.157) | copy-start | bytes 49156
  15.5 13.1 %copy-start.5 = (bf16[512,512]{1,0:T(8,128)(2,1)S(1)}, bf16[512,512]{1,0:T(8,128)(2,1)}, u32[]{:S(2)}) copy-start(bf16[512,512]{1,0:T(8,128)(2,1)} %constant.146.clone.table_ref) | copy-start | bytes 1572868
  15.5 48.0 %collective-permute-start.1 = (bf16[32,128,128]{2,1,0:T(8,128)(2,1)}, bf16[32,128,128]{2,1,0:T(8,128)(2,1)S(1)}, u32[]{:S(2)}, u32[]{:S(2)}) collective-permute-start(bf16[32,128,128]{2,1,0:T(8,128)(2,1)} %get-tuple-element.17), channel_id=1, source_target_pairs={{0,16},{8,24},{16,0},{24,8},{1,17},{9,25},{17,1},{25,9},{2,18},{10... | collective-permute-start | bytes 3145736 | tf_op jit(solution)/shard_map/ppermute | solution.py:141
  17.3 46.2 %collective-permute-start.2 = (bf16[32,128,128]{2,1,0:T(8,128)(2,1)}, bf16[32,128,128]{2,1,0:T(8,128)(2,1)S(1)}, u32[]{:S(2)}, u32[]{:S(2)}) collective-permute-start(bf16[32,128,128]{2,1,0:T(8,128)(2,1)} %get-tuple-element.18), channel_id=1, source_target_pairs={{0,24},{8,16},{16,8},{24,0},{1,25},{9,17},{17,9},{25,1},{2,26},{10... | collective-permute-start | bytes 3145736 | tf_op jit(solution)/shard_map/ppermute | solution.py:141
  23.2 41.6 %collective-permute-start = (bf16[32,128,128]{2,1,0:T(8,128)(2,1)}, bf16[32,128,128]{2,1,0:T(8,128)(2,1)}, u32[]{:S(2)}, u32[]{:S(2)}) collective-permute-start(bf16[32,128,128]{2,1,0:T(8,128)(2,1)} %get-tuple-element.16), channel_id=1, source_target_pairs={{0,8},{8,0},{16,24},{24,16},{1,9},{9,1},{17,25},{25,17},{2,10},{10... | collective-permute-start | bytes 3145736 | tf_op jit(solution)/shard_map/ppermute | solution.py:141
  27.5 70.0 %copy-start = (bf16[16,512]{1,0:T(8,128)(2,1)S(1)}, bf16[16,512]{1,0:T(8,128)(2,1)}, u32[]{:S(2)}) copy-start(bf16[16,512]{1,0:T(8,128)(2,1)} %constant.151.clone.spread_ref) | copy-start | bytes 49156
  27.5 70.0 %copy-start.2 = (f32[128]{0:T(128)S(1)}, f32[128]{0:T(128)}, u32[]{:S(2)}) copy-start(f32[128]{0:T(128)} %thick_ref.5) | copy-start | bytes 1540
  27.5 70.0 %copy-start.4 = (f32[128]{0:T(128)S(1)}, f32[128]{0:T(128)}, u32[]{:S(2)}) copy-start(f32[128]{0:T(128)} %pad_maximum_fusion.gap_ref) | copy-start | bytes 1540
  63.5 2.0 %copy-start.9 = (bf16[32,128,128]{2,1,0:T(8,128)(2,1)}, bf16[32,128,128]{2,1,0:T(8,128)(2,1)S(1)}, u32[]{:S(2)}) copy-start(bf16[32,128,128]{2,1,0:T(8,128)(2,1)S(1)} %collective-permute-done.1.refs_2_) | copy-start | bytes 3145732
  63.5 2.0 %copy-start.10 = (bf16[32,128,128]{2,1,0:T(8,128)(2,1)}, bf16[32,128,128]{2,1,0:T(8,128)(2,1)S(1)}, u32[]{:S(2)}) copy-start(bf16[32,128,128]{2,1,0:T(8,128)(2,1)S(1)} %collective-permute-done.2.refs_3_) | copy-start | bytes 3145732
  81.3 16.1 %all-to-all-start.1 = ((bf16[32,16,256]{2,1,0:T(8,128)(2,1)}), bf16[32,16,256]{2,1,0:T(8,128)(2,1)S(1)}, u32[]{:S(2)}, u32[]{:S(2)}) async-start(bf16[32,16,256]{2,1,0:T(8,128)(2,1)} %bitcast.40), calls=%async_computation.1 | async-start | bytes 524288 | tf_op jit(solution)/shard_map/all_to_all | solution.py:503
  118.6 17.3 %copy-start.3 = (f32[128]{0:T(128)S(1)}, f32[128]{0:T(128)}, u32[]{:S(2)}) copy-start(f32[128]{0:T(128)} %thick_ref.5) | copy-start | bytes 1540
  132.3 26.3 %collective-permute-start.5 = (bf16[32,128,128]{2,1,0:T(8,128)(2,1)}, bf16[32,128,128]{2,1,0:T(8,128)(2,1)S(1)}, u32[]{:S(2)}, u32[]{:S(2)}) collective-permute-start(bf16[32,128,128]{2,1,0:T(8,128)(2,1)} %get-tuple-element.24), channel_id=1, source_target_pairs={{0,8},{8,0},{16,24},{24,16},{1,9},{9,1},{17,25},{25,17},{2,10},{10... | collective-permute-start | bytes 3145736 | tf_op jit(solution)/shard_map/ppermute | solution.py:141
  132.9 51.6 %collective-permute-start.3 = (bf16[32,128,128]{2,1,0:T(8,128)(2,1)}, bf16[32,128,128]{2,1,0:T(8,128)(2,1)S(1)}, u32[]{:S(2)}, u32[]{:S(2)}) collective-permute-start(bf16[32,128,128]{2,1,0:T(8,128)(2,1)} %get-tuple-element.21), channel_id=1, source_target_pairs={{0,16},{8,24},{16,0},{24,8},{1,17},{9,25},{17,1},{25,9},{2,18},{10... | collective-permute-start | bytes 3145736 | tf_op jit(solution)/shard_map/ppermute | solution.py:141
  133.7 50.8 %collective-permute-start.4 = (bf16[32,128,128]{2,1,0:T(8,128)(2,1)}, bf16[32,128,128]{2,1,0:T(8,128)(2,1)S(1)}, u32[]{:S(2)}, u32[]{:S(2)}) collective-permute-start(bf16[32,128,128]{2,1,0:T(8,128)(2,1)} %get-tuple-element.22), channel_id=1, source_target_pairs={{0,24},{8,16},{16,8},{24,0},{1,25},{9,17},{17,9},{25,1},{2,26},{10... | collective-permute-start | bytes 3145736 | tf_op jit(solution)/shard_map/ppermute | solution.py:141
  158.6 1.0 copy-start.8
  184.5 1.0 copy-start.11
  185.5 1.0 copy-start.12

commit v6 on v5

--- a/solution.py
+++ b/solution.py
@@ -14,6 +14,7 @@
 VMEM = pltpu.MemorySpace.VMEM
 SMEM = pltpu.MemorySpace.SMEM
 LANES = 128
+INVERSE_LIMIT = 16 * 1024 * 1024
 CHUNK = 64
 BATCH = 8
 
@@ -132,7 +133,7 @@
         ),
         out_shape=jax.ShapeDtypeStruct((modes, x_local, rows, layers), jnp.bfloat16),
         input_output_aliases={2 + pieces: 0} if earlier else {},
-        compiler_params=pltpu.CompilerParams(vmem_limit_bytes=VMEM_LIMIT),
+        compiler_params=pltpu.CompilerParams(vmem_limit_bytes=INVERSE_LIMIT),
         name="inverse_y",
     )(me, table, *spectra, *earlier)
 
@@ -427,17 +428,19 @@
     code = jnp.stack([strip_column // 65536, strip_column // 256 % 256, strip_column % 256])
     code = jnp.pad(code.T, ((0, 0), (0, layers - 3))).astype(jnp.bfloat16)
     packed = jnp.concatenate([velocity, code[None]], axis=0).transpose(1, 0, 2)
-    packed = jnp.broadcast_to(packed[None], (devices,) + packed.shape)
-    gathered = lax.all_to_all(packed, both, split_axis=0, concat_axis=0, tiled=True)
-    gathered = gathered.reshape(strip_count, modes + 1, layers)
     own = index_px.astype(jnp.int32).reshape(1)
     place = jnp.stack([own_mode, own_piece]).astype(jnp.int32)
     rows = [None] * count_px
     for step in reversed(range(modes)):
-        chunks = forward_y(place, carried, pieces, step)
+        chunks = list(forward_y(place, carried, pieces, step))
+        if step == 0:
+            packed, chunks[0] = lax.optimization_barrier((packed, chunks[0]))
         for f, chunk in enumerate(chunks):
             d = step * pieces + f
             rows[d] = swap(chunk, d) if d else chunk
+    packed = jnp.broadcast_to(packed[None], (devices,) + packed.shape)
+    gathered = lax.all_to_all(packed, both, split_axis=0, concat_axis=0, tiled=True)
+    gathered = gathered.reshape(strip_count, modes + 1, layers)
     code = gathered[:, modes, :3].astype(jnp.int32)
     column = code[:, 0] * 65536 + code[:, 1] * 256 + code[:, 2]
     all_velocity = gathered[:, :modes].astype(jnp.float32).transpose(1, 2, 0)

time: 192 us -> 186 us (0.969)
  waiting for transfers between devices: 50 us -> 47 us
  Pallas kernels: 56.4 us -> 54 us
    ppermute x6, waiting for transfers between devices: 40.4 us -> 7.59 us  [swap(): lax.ppermute(values, 'px', [(k, k ^ distance) for k in range(lax.axis_siz...]
    all_to_all x1, waiting for transfers between devices: 0.01 us -> 29.9 us  [shards(): lax.all_to_all(packed, both, split_axis=0, concat_axis=0, tiled=True)]
    ppermute x6, starting transfers between devices: 7.07 us -> 9.82 us  [swap(): lax.ppermute(values, 'px', [(k, k ^ distance) for k in range(lax.axis_siz...]
    pallas_call x2, Pallas kernels: 9.33 us -> 6.91 us  [inverse_y(): pl.pallas_call(functools.partial(inverse_y_kernel, pieces), grid_spec=plt...]
    all_to_all x1, starting transfers between devices: 7.3 us -> 4.92 us  [shards(): lax.all_to_all(packed, both, split_axis=0, concat_axis=0, tiled=True)]
  transfers between devices with their start and end apart: 8 -> 8, of which waited for: 4 -> 3; matrix products, arithmetic and copies ran while one was open for 6% -> 6% of each run, Pallas kernels for 7% -> 4%
where the time goes in v6:
time: 186 us; the launch traced here: 185 us
  Pallas kernels  54 us (29%)
  blocking collectives  47.4 us (25%)
  waiting for transfers between devices  47 us (25%)
  starting transfers between devices  20.8 us (11%)
  local copies, waits for them, and re-layouts  8.7 us (5%)
  other arithmetic  5.75 us (3%)
    all_to_all x1, waiting for transfers between devices, shards(): lax.all_to_all(packed, both, split_axis=0, concat_axis=0, tiled=True)  29.9 us
    all_gather x1, blocking collectives, shards(): every_mass = lax.all_gather(local_mass, 'px', axis=0, tiled=False)  20.7 us
    pallas_call x1, Pallas kernels, shards(): pl.pallas_call(functools.partial(block_ends_kernel, count_px), in_specs=[...  15.8 us
    psum x1, blocking collectives, shards(): local_mass = lax.psum(local_mass, 'py')  14 us
    pallas_call x1, Pallas kernels, shards(): pl.pallas_call(functools.partial(block_solve_kernel, count_px), in_specs=...  13.7 us
    all_to_all x1, blocking collectives, shards(): lax.all_to_all(outgoing.reshape(width_x, 2 * layers), both, split_axis=0,...  12.8 us
    ppermute x6, starting transfers between devices, swap(): lax.ppermute(values, 'px', [(k, k ^ distance) for k in range(lax.axis_siz...  9.82 us
    all_to_all x1, waiting for transfers between devices, shards(): lax.all_to_all(block_ends, both, split_axis=0, concat_axis=0, tiled=True)  9.54 us
  transfers between devices with their start and end apart: 8, of which 3 were waited for; matrix products, arithmetic and copies ran while one was open for 6% of the time, Pallas kernels for 4%

profile of v6, /device:TPU:0, one launch (start us, length us, event | category | flops | bytes accessed | tf_op | source)
XLA Modules:
  0.0 185.3 jit_solution(1450190042660266068)
XLA Ops:
  1.4 4.7 %forward_y.3 = (bf16[32,128,128]{2,1,0:T(8,128)(2,1)}, bf16[32,128,128]{2,1,0:T(8,128)(2,1)}) custom-call(s32[2]{0:T(128)} %get-tuple-element.40.me_ref, bf16[256,256]{1,0:T(8,128)(2,1)} %constant.145.clone.table_ref, bf16[2,128,64,128]{3,2,1,0:T(8,128)(2,1)} %grid_ref.3), custom_call_target="tpu_custom_call" | custom-call | tf_op jit(solution)/shard_map/forward_y/pallas_call | solution.py:97
  6.1 3.0 %collective-permute-start.1 = (bf16[32,128,128]{2,1,0:T(8,128)(2,1)}, bf16[32,128,128]{2,1,0:T(8,128)(2,1)S(1)}, u32[]{:S(2)}, u32[]{:S(2)}) collective-permute-start(bf16[32,128,128]{2,1,0:T(8,128)(2,1)} %get-tuple-element.21), channel_id=1, source_target_pairs={{0,16},{8,24},{16,0},{24,8},{1,17},{9,25},{17,1},{25,9},{2,18},{10... | collective-permute-start | bytes 3145736 | tf_op jit(solution)/shard_map/ppermute | solution.py:142
  9.0 1.4 collective-permute-start.2
  10.5 4.5 %forward_y.2 = (bf16[32,128,128]{2,1,0:T(8,128)(2,1)}, bf16[32,128,128]{2,1,0:T(8,128)(2,1)}) custom-call(s32[2]{0:T(128)} %get-tuple-element.40.me_ref, bf16[256,256]{1,0:T(8,128)(2,1)} %constant.145.clone.table_ref, bf16[2,128,64,128]{3,2,1,0:T(8,128)(2,1)} %grid_ref.3), custom_call_target="tpu_custom_call" | custom-call | tf_op jit(solution)/shard_map/forward_y/pallas_call | solution.py:97
  15.8 4.9 %all-to-all-start = ((bf16[32,4,3,128]{3,1,2,0:T(4,128)(2,1)}), bf16[32,4,3,128]{3,1,2,0:T(4,128)(2,1)S(1)}, u32[]{:S(2)}, u32[]{:S(2)}) async-start(bf16[32,4,3,128]{3,1,2,0:T(4,128)(2,1)} %broadcast_in_dim.64), calls=%async_computation | async-start | bytes 196608 | tf_op jit(solution)/shard_map/all_to_all | solution.py:442
  20.7 1.8 collective-permute-start
  26.0 29.9 %all-to-all-done = bf16[32,4,3,128]{3,1,2,0:T(4,128)(2,1)S(1)} async-done(((bf16[32,4,3,128]{3,1,2,0:T(4,128)(2,1)}), bf16[32,4,3,128]{3,1,2,0:T(4,128)(2,1)S(1)}, u32[]{:S(2)}, u32[]{:S(2)}) %all-to-all-start) | async-done | bytes 98336 | tf_op jit(solution)/shard_map/all_to_all | solution.py:442
  57.5 1.5 gather_fusion.1
  61.0 0.8 broadcast_in_dim.62.ends_ref
  62.4 15.8 %block_ends.1 = (f32[1,4,5160,128]{3,2,1,0:T(8,128)}, bf16[512,256]{1,0:T(8,128)(2,1)}) custom-call(s32[1]{0:T(128)} %bitcast.2.me_ref, f32[128]{0:T(128)} %thick_ref.5, f32[128]{0:T(128)} %pad_maximum_fusion.gap_ref, f32[4,32,128]{2,1,0:T(8,128)} %broadcast_add_fusion.wave_ref, f32[2,32,128]{2,1,0:T(8,128)} %broadcast_in_dim.62.ends_ref, ...), custom_call_target="tpu_custom_call" | custom-call | tf_op jit(solution)/shard_map/block_ends/pallas_call | solution.py:485
  78.2 6.1 %all-to-all-start.1 = ((bf16[32,16,256]{2,1,0:T(8,128)(2,1)}), bf16[32,16,256]{2,1,0:T(8,128)(2,1)S(1)}, u32[]{:S(2)}, u32[]{:S(2)}) async-start(bf16[32,16,256]{2,1,0:T(8,128)(2,1)} %bitcast.40), calls=%async_computation.1 | async-start | bytes 524288 | tf_op jit(solution)/shard_map/all_to_all | solution.py:506
  85.2 9.5 %all-to-all-done.1 = bf16[32,16,256]{2,1,0:T(8,128)(2,1)S(1)} async-done(((bf16[32,16,256]{2,1,0:T(8,128)(2,1)}), bf16[32,16,256]{2,1,0:T(8,128)(2,1)S(1)}, u32[]{:S(2)}, u32[]{:S(2)}) %all-to-all-start.1) | async-done | bytes 262176 | tf_op jit(solution)/shard_map/all_to_all | solution.py:506
  94.7 8.3 %interface.1 = bf16[2,2,128,256]{3,2,1,0:T(8,128)(2,1)S(1)} custom-call(f32[128]{0:T(128)S(1)} %copy-done.5, f32[128]{0:T(128)S(1)} %copy-done.7, f32[4,16,128]{2,1,0:T(8,128)S(1)} %broadcast_add_fusion.1.wave_ref, bf16[16,512]{1,0:T(8,128)(2,1)S(1)} %copy-done.2, bf16[2,2,128,256]{3,2,1,0:T(8,128)(2,1)S(1)} %bitcast.35), custom_call_target="tpu_custom_call" | custom-call | tf_op jit(solution)/shard_map/interface/pallas_call | solution.py:507
  103.1 12.8 %all_to_all.25 = bf16[32,16,256]{2,1,0:T(8,128)(2,1)} all-to-all(bf16[32,16,256]{2,1,0:T(8,128)(2,1)S(1)} %bitcast.36), channel_id=1, replica_groups=mesh['px'=4,'py'=8] {'px','py'}, dimensions={0} | all-to-all | bytes 524288 | tf_op jit(solution)/shard_map/all_to_all | solution.py:526
  115.9 13.7 %block_solve.1 = (bf16[32,128,128]{2,1,0:T(8,128)(2,1)}, bf16[32,128,128]{2,1,0:T(8,128)(2,1)}, bf16[32,128,128]{2,1,0:T(8,128)(2,1)}, bf16[32,128,128]{2,1,0:T(8,128)(2,1)}, f32[2,128,128]{2,1,0:T(8,128)}) custom-call(s32[1]{0:T(128)} %bitcast.2.me_ref, f32[128]{0:T(128)} %thick_ref.5, f32[128]{0:T(128)} %pad_maximum_fusion.gap_ref, ...), custom_call_target="tpu_custom_call" | custom-call | tf_op jit(solution)/shard_map/block_solve/pallas_call | solution.py:530
  130.2 0.8 collective-permute-start.3
  131.0 2.2 %collective-permute-start.4 = (bf16[32,128,128]{2,1,0:T(8,128)(2,1)}, bf16[32,128,128]{2,1,0:T(8,128)(2,1)S(1)}, u32[]{:S(2)}, u32[]{:S(2)}) collective-permute-start(bf16[32,128,128]{2,1,0:T(8,128)(2,1)} %get-tuple-element.26), channel_id=1, source_target_pairs={{0,24},{8,16},{16,8},{24,0},{1,25},{9,17},{17,9},{25,1},{2,26},{10... | collective-permute-start | bytes 3145736 | tf_op jit(solution)/shard_map/ppermute | solution.py:142
  133.2 1.1 multiply_reduce_fusion
  134.4 14.0 %psum.7 = f32[2,2]{1,0:T(2,128)S(1)} all-reduce(f32[2,2]{1,0:T(2,128)S(1)} %broadcast_select_fusion.1), channel_id=1, replica_groups=mesh['px'=4,'py'=8] {'py'}, use_global_device_ids=true, to_apply=%region_1.2 | all-reduce | flops 4 | bytes 32 | tf_op jit(solution)/shard_map/psum | solution.py:556
  148.3 7.6 %collective-permute-done.5.refs_1_ = bf16[32,128,128]{2,1,0:T(8,128)(2,1)S(1)} collective-permute-done((bf16[32,128,128]{2,1,0:T(8,128)(2,1)}, bf16[32,128,128]{2,1,0:T(8,128)(2,1)S(1)}, u32[]{:S(2)}, u32[]{:S(2)}) %collective-permute-start.5) | collective-permute-done | bytes 1048608 | tf_op jit(solution)/shard_map/ppermute | solution.py:142
  155.9 1.2 copy-done.1
  157.1 3.5 %inverse_y.2.refs_2_ = bf16[2,128,64,128]{3,2,1,0:T(8,128)(2,1)} custom-call(s32[2]{0:T(128)S(1)} %copy-done.3, bf16[256,256]{1,0:T(8,128)(2,1)S(1)} %copy-done, bf16[32,128,128]{2,1,0:T(8,128)(2,1)S(1)} %copy-done.1, bf16[32,128,128]{2,1,0:T(8,128)(2,1)S(1)} %collective-permute-done.5.refs_1_), custom_call_target="tpu_custom_call" | custom-call | tf_op jit(solution)/shard_map/inverse_y/pallas_call | solution.py:121
  160.6 20.7 %all-gather.1 = f32[4,2,2]{2,1,0:T(2,128)S(1)} all-gather(f32[1,2,2]{2,1,0:T(2,128)S(1)} %bitcast.43), channel_id=2, replica_groups=mesh['px'=4,'py'=8] {'px'}, dimensions={0}, use_global_device_ids=true | all-gather | bytes 80 | tf_op jit(solution)/shard_map/all_gather | solution.py:563
  181.8 3.5 %inverse_y.3 = bf16[2,128,64,128]{3,2,1,0:T(8,128)(2,1)} custom-call(s32[2]{0:T(128)S(1)} %copy-done.3, bf16[256,256]{1,0:T(8,128)(2,1)S(1)} %copy-done, bf16[32,128,128]{2,1,0:T(8,128)(2,1)S(1)} %collective-permute-done.3.refs_0_, bf16[32,128,128]{2,1,0:T(8,128)(2,1)S(1)} %collective-permute-done.4.refs_1_, ...), custom_call_target="tpu_custom_call", output_to_operand_aliasing={{}: (4, {})} | custom-call | tf_op jit(solution)/shard_map/inverse_y/pallas_call | solution.py:121
  (75 shorter events, 10.4 us)
Async XLA Ops:
  1.3 13.7 %copy-start.15 = (s32[4]{0:T(128)S(1)}, s32[4]{0:T(128)}, u32[]{:S(2)}) copy-start(s32[4]{0:T(128)} %param.17) | copy-start | bytes 52
  1.3 13.8 %copy-start.14 = (bf16[2,4,128]{2,1,0:T(4,128)(2,1)S(1)}, bf16[2,4,128]{2,1,0:T(4,128)(2,1)}, u32[]{:S(2)}) copy-start(bf16[2,4,128]{2,1,0:T(4,128)(2,1)} %param.16) | copy-start | bytes 6148
  1.3 21.3 %copy-start.4 = (f32[128]{0:T(128)S(1)}, f32[128]{0:T(128)}, u32[]{:S(2)}) copy-start(f32[128]{0:T(128)} %thick_ref.5) | copy-start | bytes 1540
  1.3 22.0 %copy-start.16 = (f32[64]{0:T(128)S(1)}, f32[64]{0:T(128)}, u32[]{:S(2)}) copy-start(f32[64]{0:T(128)} %constant.149.clone) | copy-start | bytes 772
  1.3 22.1 %copy-start.10 = (f32[64,64]{0,1:T(8,128)S(1)}, f32[64,64]{0,1:T(8,128)}, u32[]{:S(2)}) copy-start(f32[64,64]{0,1:T(8,128)} %constant.147.clone) | copy-start | bytes 49156
  1.3 24.0 %copy-start.13 = (f32[4,128]{1,0:T(4,128)S(1)}, f32[4,128]{1,0:T(4,128)}, u32[]{:S(2)}) copy-start(f32[4,128]{1,0:T(4,128)} %constant.156) | copy-start | bytes 6148
  1.3 55.1 %copy-start.9 = (f32[64,64]{1,0:T(8,128)S(1)}, f32[64,64]{1,0:T(8,128)}, u32[]{:S(2)}) copy-start(f32[64,64]{1,0:T(8,128)} %constant.157) | copy-start | bytes 49156
  6.1 51.5 %copy-start.8 = (bf16[512,512]{1,0:T(8,128)(2,1)S(1)}, bf16[512,512]{1,0:T(8,128)(2,1)}, u32[]{:S(2)}) copy-start(bf16[512,512]{1,0:T(8,128)(2,1)} %constant.146.clone.table_ref) | copy-start | bytes 1572868
  6.1 54.9 %collective-permute-start.1 = (bf16[32,128,128]{2,1,0:T(8,128)(2,1)}, bf16[32,128,128]{2,1,0:T(8,128)(2,1)S(1)}, u32[]{:S(2)}, u32[]{:S(2)}) collective-permute-start(bf16[32,128,128]{2,1,0:T(8,128)(2,1)} %get-tuple-element.21), channel_id=1, source_target_pairs={{0,16},{8,24},{16,0},{24,8},{1,17},{9,25},{17,1},{25,9},{2,18},{10... | collective-permute-start | bytes 3145736 | tf_op jit(solution)/shard_map/ppermute | solution.py:142
  9.0 51.9 %collective-permute-start.2 = (bf16[32,128,128]{2,1,0:T(8,128)(2,1)}, bf16[32,128,128]{2,1,0:T(8,128)(2,1)S(1)}, u32[]{:S(2)}, u32[]{:S(2)}) collective-permute-start(bf16[32,128,128]{2,1,0:T(8,128)(2,1)} %get-tuple-element.22), channel_id=1, source_target_pairs={{0,24},{8,16},{16,8},{24,0},{1,25},{9,17},{17,9},{25,1},{2,26},{10... | collective-permute-start | bytes 3145736 | tf_op jit(solution)/shard_map/ppermute | solution.py:142
  15.8 40.1 %all-to-all-start = ((bf16[32,4,3,128]{3,1,2,0:T(4,128)(2,1)}), bf16[32,4,3,128]{3,1,2,0:T(4,128)(2,1)S(1)}, u32[]{:S(2)}, u32[]{:S(2)}) async-start(bf16[32,4,3,128]{3,1,2,0:T(4,128)(2,1)} %broadcast_in_dim.64), calls=%async_computation | async-start | bytes 196608 | tf_op jit(solution)/shard_map/all_to_all | solution.py:442
  20.7 40.2 %collective-permute-start = (bf16[32,128,128]{2,1,0:T(8,128)(2,1)}, bf16[32,128,128]{2,1,0:T(8,128)(2,1)}, u32[]{:S(2)}, u32[]{:S(2)}) collective-permute-start(bf16[32,128,128]{2,1,0:T(8,128)(2,1)} %get-tuple-element.20), channel_id=1, source_target_pairs={{0,8},{8,0},{16,24},{24,16},{1,9},{9,1},{17,25},{25,17},{2,10},{10... | collective-permute-start | bytes 3145736 | tf_op jit(solution)/shard_map/ppermute | solution.py:142
  56.4 38.3 %copy-start.2 = (bf16[16,512]{1,0:T(8,128)(2,1)S(1)}, bf16[16,512]{1,0:T(8,128)(2,1)}, u32[]{:S(2)}) copy-start(bf16[16,512]{1,0:T(8,128)(2,1)} %constant.151.clone.spread_ref) | copy-start | bytes 49156
  56.4 38.3 %copy-start.5 = (f32[128]{0:T(128)S(1)}, f32[128]{0:T(128)}, u32[]{:S(2)}) copy-start(f32[128]{0:T(128)} %thick_ref.5) | copy-start | bytes 1540
  56.5 38.3 %copy-start.7 = (f32[128]{0:T(128)S(1)}, f32[128]{0:T(128)}, u32[]{:S(2)}) copy-start(f32[128]{0:T(128)} %pad_maximum_fusion.gap_ref) | copy-start | bytes 1540
  61.0 1.5 copy-start.12
  78.2 16.5 %all-to-all-start.1 = ((bf16[32,16,256]{2,1,0:T(8,128)(2,1)}), bf16[32,16,256]{2,1,0:T(8,128)(2,1)S(1)}, u32[]{:S(2)}, u32[]{:S(2)}) async-start(bf16[32,16,256]{2,1,0:T(8,128)(2,1)} %bitcast.40), calls=%async_computation.1 | async-start | bytes 524288 | tf_op jit(solution)/shard_map/all_to_all | solution.py:506
  115.9 17.3 %copy-start.6 = (f32[128]{0:T(128)S(1)}, f32[128]{0:T(128)}, u32[]{:S(2)}) copy-start(f32[128]{0:T(128)} %thick_ref.5) | copy-start | bytes 1540
  115.9 40.0 %copy-start = (bf16[256,256]{1,0:T(8,128)(2,1)S(1)}, bf16[256,256]{1,0:T(8,128)(2,1)}, u32[]{:S(2)}) copy-start(bf16[256,256]{1,0:T(8,128)(2,1)} %constant.145.clone.table_ref) | copy-start | bytes 393220
  115.9 40.0 %copy-start.3 = (s32[2]{0:T(128)S(1)}, s32[2]{0:T(128)}, u32[]{:S(2)}) copy-start(s32[2]{0:T(128)} %get-tuple-element.40.me_ref) | copy-start | bytes 28
  129.6 26.3 %collective-permute-start.5 = (bf16[32,128,128]{2,1,0:T(8,128)(2,1)}, bf16[32,128,128]{2,1,0:T(8,128)(2,1)S(1)}, u32[]{:S(2)}, u32[]{:S(2)}) collective-permute-start(bf16[32,128,128]{2,1,0:T(8,128)(2,1)} %get-tuple-element.28), channel_id=1, source_target_pairs={{0,8},{8,0},{16,24},{24,16},{1,9},{9,1},{17,25},{25,17},{2,10},{10... | collective-permute-start | bytes 3145736 | tf_op jit(solution)/shard_map/ppermute | solution.py:142
  130.2 51.6 %collective-permute-start.3 = (bf16[32,128,128]{2,1,0:T(8,128)(2,1)}, bf16[32,128,128]{2,1,0:T(8,128)(2,1)S(1)}, u32[]{:S(2)}, u32[]{:S(2)}) collective-permute-start(bf16[32,128,128]{2,1,0:T(8,128)(2,1)} %get-tuple-element.25), channel_id=1, source_target_pairs={{0,16},{8,24},{16,0},{24,8},{1,17},{9,25},{17,1},{25,9},{2,18},{10... | collective-permute-start | bytes 3145736 | tf_op jit(solution)/shard_map/ppermute | solution.py:142
  131.0 50.8 %collective-permute-start.4 = (bf16[32,128,128]{2,1,0:T(8,128)(2,1)}, bf16[32,128,128]{2,1,0:T(8,128)(2,1)S(1)}, u32[]{:S(2)}, u32[]{:S(2)}) collective-permute-start(bf16[32,128,128]{2,1,0:T(8,128)(2,1)} %get-tuple-element.26), channel_id=1, source_target_pairs={{0,24},{8,16},{16,8},{24,0},{1,25},{9,17},{17,9},{25,1},{2,26},{10... | collective-permute-start | bytes 3145736 | tf_op jit(solution)/shard_map/ppermute | solution.py:142
  155.9 1.2 copy-start.1
  (1 other events, 1.0 us)

commit v7 on v6

--- a/solution.py
+++ b/solution.py
@@ -250,7 +250,7 @@
     for at in range(part // each):
         for d in range(count):
             fetch(at, d).wait()
-        lax.fori_loop(at * each, (at + 1) * each, transform, 0, unroll=2)
+        lax.fori_loop(at * each, (at + 1) * each, transform, 0, unroll=4)
     saving = pltpu.make_async_copy(spectrum_ref, saved_ref, done)
     saving.start()
     eliminate(

time: 186 us -> 185 us (level)
  no operation moved by 1% of the time
where the time goes in v7:
time: 185 us; the launch traced here: 184 us
  Pallas kernels  52.8 us (29%)
  blocking collectives  47.4 us (26%)
  waiting for transfers between devices  47.1 us (25%)
  starting transfers between devices  20.8 us (11%)
  local copies, waits for them, and re-layouts  8.7 us (5%)
  other arithmetic  5.75 us (3%)
    all_to_all x1, waiting for transfers between devices, shards(): lax.all_to_all(packed, both, split_axis=0, concat_axis=0, tiled=True)  29.9 us
    all_gather x1, blocking collectives, shards(): every_mass = lax.all_gather(local_mass, 'px', axis=0, tiled=False)  20.7 us
    pallas_call x1, Pallas kernels, shards(): pl.pallas_call(functools.partial(block_ends_kernel, count_px), in_specs=[...  14.7 us
    psum x1, blocking collectives, shards(): local_mass = lax.psum(local_mass, 'py')  14 us
    pallas_call x1, Pallas kernels, shards(): pl.pallas_call(functools.partial(block_solve_kernel, count_px), in_specs=...  13.7 us
    all_to_all x1, blocking collectives, shards(): lax.all_to_all(outgoing.reshape(width_x, 2 * layers), both, split_axis=0,...  12.8 us
    ppermute x6, starting transfers between devices, swap(): lax.ppermute(values, 'px', [(k, k ^ distance) for k in range(lax.axis_siz...  9.81 us
    all_to_all x1, waiting for transfers between devices, shards(): lax.all_to_all(block_ends, both, split_axis=0, concat_axis=0, tiled=True)  9.54 us
  transfers between devices with their start and end apart: 8, of which 3 were waited for; matrix products, arithmetic and copies ran while one was open for 6% of the time, Pallas kernels for 4%

profile of v7, /device:TPU:0, one launch (start us, length us, event | category | flops | bytes accessed | tf_op | source)
XLA Modules:
  0.0 184.1 jit_solution(5343740538925521036)
XLA Ops:
  1.4 4.7 %forward_y.3 = (bf16[32,128,128]{2,1,0:T(8,128)(2,1)}, bf16[32,128,128]{2,1,0:T(8,128)(2,1)}) custom-call(s32[2]{0:T(128)} %get-tuple-element.40.me_ref, bf16[256,256]{1,0:T(8,128)(2,1)} %constant.145.clone.table_ref, bf16[2,128,64,128]{3,2,1,0:T(8,128)(2,1)} %grid_ref.3), custom_call_target="tpu_custom_call" | custom-call | tf_op jit(solution)/shard_map/forward_y/pallas_call | solution.py:97
  6.1 3.0 %collective-permute-start.1 = (bf16[32,128,128]{2,1,0:T(8,128)(2,1)}, bf16[32,128,128]{2,1,0:T(8,128)(2,1)S(1)}, u32[]{:S(2)}, u32[]{:S(2)}) collective-permute-start(bf16[32,128,128]{2,1,0:T(8,128)(2,1)} %get-tuple-element.21), channel_id=1, source_target_pairs={{0,16},{8,24},{16,0},{24,8},{1,17},{9,25},{17,1},{25,9},{2,18},{10... | collective-permute-start | bytes 3145736 | tf_op jit(solution)/shard_map/ppermute | solution.py:142
  9.0 1.4 collective-permute-start.2
  10.5 4.5 %forward_y.2 = (bf16[32,128,128]{2,1,0:T(8,128)(2,1)}, bf16[32,128,128]{2,1,0:T(8,128)(2,1)}) custom-call(s32[2]{0:T(128)} %get-tuple-element.40.me_ref, bf16[256,256]{1,0:T(8,128)(2,1)} %constant.145.clone.table_ref, bf16[2,128,64,128]{3,2,1,0:T(8,128)(2,1)} %grid_ref.3), custom_call_target="tpu_custom_call" | custom-call | tf_op jit(solution)/shard_map/forward_y/pallas_call | solution.py:97
  15.8 4.9 %all-to-all-start = ((bf16[32,4,3,128]{3,1,2,0:T(4,128)(2,1)}), bf16[32,4,3,128]{3,1,2,0:T(4,128)(2,1)S(1)}, u32[]{:S(2)}, u32[]{:S(2)}) async-start(bf16[32,4,3,128]{3,1,2,0:T(4,128)(2,1)} %broadcast_in_dim.64), calls=%async_computation | async-start | bytes 196608 | tf_op jit(solution)/shard_map/all_to_all | solution.py:442
  20.7 1.8 collective-permute-start
  26.0 29.9 %all-to-all-done = bf16[32,4,3,128]{3,1,2,0:T(4,128)(2,1)S(1)} async-done(((bf16[32,4,3,128]{3,1,2,0:T(4,128)(2,1)}), bf16[32,4,3,128]{3,1,2,0:T(4,128)(2,1)S(1)}, u32[]{:S(2)}, u32[]{:S(2)}) %all-to-all-start) | async-done | bytes 98336 | tf_op jit(solution)/shard_map/all_to_all | solution.py:442
  57.5 1.5 gather_fusion.1
  61.0 0.8 broadcast_in_dim.62.ends_ref
  62.4 14.7 %block_ends.1 = (f32[1,4,5160,128]{3,2,1,0:T(8,128)}, bf16[512,256]{1,0:T(8,128)(2,1)}) custom-call(s32[1]{0:T(128)} %bitcast.2.me_ref, f32[128]{0:T(128)} %thick_ref.5, f32[128]{0:T(128)} %pad_maximum_fusion.gap_ref, f32[4,32,128]{2,1,0:T(8,128)} %broadcast_add_fusion.wave_ref, f32[2,32,128]{2,1,0:T(8,128)} %broadcast_in_dim.62.ends_ref, ...), custom_call_target="tpu_custom_call" | custom-call | tf_op jit(solution)/shard_map/block_ends/pallas_call | solution.py:485
  77.1 6.1 %all-to-all-start.1 = ((bf16[32,16,256]{2,1,0:T(8,128)(2,1)}), bf16[32,16,256]{2,1,0:T(8,128)(2,1)S(1)}, u32[]{:S(2)}, u32[]{:S(2)}) async-start(bf16[32,16,256]{2,1,0:T(8,128)(2,1)} %bitcast.40), calls=%async_computation.1 | async-start | bytes 524288 | tf_op jit(solution)/shard_map/all_to_all | solution.py:506
  84.0 9.5 %all-to-all-done.1 = bf16[32,16,256]{2,1,0:T(8,128)(2,1)S(1)} async-done(((bf16[32,16,256]{2,1,0:T(8,128)(2,1)}), bf16[32,16,256]{2,1,0:T(8,128)(2,1)S(1)}, u32[]{:S(2)}, u32[]{:S(2)}) %all-to-all-start.1) | async-done | bytes 262176 | tf_op jit(solution)/shard_map/all_to_all | solution.py:506
  93.6 8.3 %interface.1 = bf16[2,2,128,256]{3,2,1,0:T(8,128)(2,1)S(1)} custom-call(f32[128]{0:T(128)S(1)} %copy-done.5, f32[128]{0:T(128)S(1)} %copy-done.7, f32[4,16,128]{2,1,0:T(8,128)S(1)} %broadcast_add_fusion.1.wave_ref, bf16[16,512]{1,0:T(8,128)(2,1)S(1)} %copy-done.2, bf16[2,2,128,256]{3,2,1,0:T(8,128)(2,1)S(1)} %bitcast.35), custom_call_target="tpu_custom_call" | custom-call | tf_op jit(solution)/shard_map/interface/pallas_call | solution.py:507
  101.9 12.8 %all_to_all.25 = bf16[32,16,256]{2,1,0:T(8,128)(2,1)} all-to-all(bf16[32,16,256]{2,1,0:T(8,128)(2,1)S(1)} %bitcast.36), channel_id=1, replica_groups=mesh['px'=4,'py'=8] {'px','py'}, dimensions={0} | all-to-all | bytes 524288 | tf_op jit(solution)/shard_map/all_to_all | solution.py:526
  114.7 13.7 %block_solve.1 = (bf16[32,128,128]{2,1,0:T(8,128)(2,1)}, bf16[32,128,128]{2,1,0:T(8,128)(2,1)}, bf16[32,128,128]{2,1,0:T(8,128)(2,1)}, bf16[32,128,128]{2,1,0:T(8,128)(2,1)}, f32[2,128,128]{2,1,0:T(8,128)}) custom-call(s32[1]{0:T(128)} %bitcast.2.me_ref, f32[128]{0:T(128)} %thick_ref.5, f32[128]{0:T(128)} %pad_maximum_fusion.gap_ref, ...), custom_call_target="tpu_custom_call" | custom-call | tf_op jit(solution)/shard_map/block_solve/pallas_call | solution.py:530
  129.0 0.8 collective-permute-start.3
  129.9 2.2 %collective-permute-start.4 = (bf16[32,128,128]{2,1,0:T(8,128)(2,1)}, bf16[32,128,128]{2,1,0:T(8,128)(2,1)S(1)}, u32[]{:S(2)}, u32[]{:S(2)}) collective-permute-start(bf16[32,128,128]{2,1,0:T(8,128)(2,1)} %get-tuple-element.26), channel_id=1, source_target_pairs={{0,24},{8,16},{16,8},{24,0},{1,25},{9,17},{17,9},{25,1},{2,26},{10... | collective-permute-start | bytes 3145736 | tf_op jit(solution)/shard_map/ppermute | solution.py:142
  132.1 1.1 multiply_reduce_fusion
  133.2 14.0 %psum.7 = f32[2,2]{1,0:T(2,128)S(1)} all-reduce(f32[2,2]{1,0:T(2,128)S(1)} %broadcast_select_fusion.1), channel_id=1, replica_groups=mesh['px'=4,'py'=8] {'py'}, use_global_device_ids=true, to_apply=%region_1.2 | all-reduce | flops 4 | bytes 32 | tf_op jit(solution)/shard_map/psum | solution.py:556
  147.2 7.6 %collective-permute-done.5.refs_1_ = bf16[32,128,128]{2,1,0:T(8,128)(2,1)S(1)} collective-permute-done((bf16[32,128,128]{2,1,0:T(8,128)(2,1)}, bf16[32,128,128]{2,1,0:T(8,128)(2,1)S(1)}, u32[]{:S(2)}, u32[]{:S(2)}) %collective-permute-start.5) | collective-permute-done | bytes 1048608 | tf_op jit(solution)/shard_map/ppermute | solution.py:142
  154.7 1.2 copy-done.1
  156.0 3.5 %inverse_y.2.refs_2_ = bf16[2,128,64,128]{3,2,1,0:T(8,128)(2,1)} custom-call(s32[2]{0:T(128)S(1)} %copy-done.3, bf16[256,256]{1,0:T(8,128)(2,1)S(1)} %copy-done, bf16[32,128,128]{2,1,0:T(8,128)(2,1)S(1)} %copy-done.1, bf16[32,128,128]{2,1,0:T(8,128)(2,1)S(1)} %collective-permute-done.5.refs_1_), custom_call_target="tpu_custom_call" | custom-call | tf_op jit(solution)/shard_map/inverse_y/pallas_call | solution.py:121
  159.4 20.7 %all-gather.1 = f32[4,2,2]{2,1,0:T(2,128)S(1)} all-gather(f32[1,2,2]{2,1,0:T(2,128)S(1)} %bitcast.43), channel_id=2, replica_groups=mesh['px'=4,'py'=8] {'px'}, dimensions={0}, use_global_device_ids=true | all-gather | bytes 80 | tf_op jit(solution)/shard_map/all_gather | solution.py:563
  180.7 3.5 %inverse_y.3 = bf16[2,128,64,128]{3,2,1,0:T(8,128)(2,1)} custom-call(s32[2]{0:T(128)S(1)} %copy-done.3, bf16[256,256]{1,0:T(8,128)(2,1)S(1)} %copy-done, bf16[32,128,128]{2,1,0:T(8,128)(2,1)S(1)} %collective-permute-done.3.refs_0_, bf16[32,128,128]{2,1,0:T(8,128)(2,1)S(1)} %collective-permute-done.4.refs_1_, ...), custom_call_target="tpu_custom_call", output_to_operand_aliasing={{}: (4, {})} | custom-call | tf_op jit(solution)/shard_map/inverse_y/pallas_call | solution.py:121
  (75 shorter events, 10.4 us)
Async XLA Ops:
  1.3 13.7 %copy-start.15 = (s32[4]{0:T(128)S(1)}, s32[4]{0:T(128)}, u32[]{:S(2)}) copy-start(s32[4]{0:T(128)} %param.17) | copy-start | bytes 52
  1.3 13.8 %copy-start.14 = (bf16[2,4,128]{2,1,0:T(4,128)(2,1)S(1)}, bf16[2,4,128]{2,1,0:T(4,128)(2,1)}, u32[]{:S(2)}) copy-start(bf16[2,4,128]{2,1,0:T(4,128)(2,1)} %param.16) | copy-start | bytes 6148
  1.3 21.3 %copy-start.4 = (f32[128]{0:T(128)S(1)}, f32[128]{0:T(128)}, u32[]{:S(2)}) copy-start(f32[128]{0:T(128)} %thick_ref.5) | copy-start | bytes 1540
  1.3 22.0 %copy-start.16 = (f32[64]{0:T(128)S(1)}, f32[64]{0:T(128)}, u32[]{:S(2)}) copy-start(f32[64]{0:T(128)} %constant.149.clone) | copy-start | bytes 772
  1.3 22.1 %copy-start.10 = (f32[64,64]{0,1:T(8,128)S(1)}, f32[64,64]{0,1:T(8,128)}, u32[]{:S(2)}) copy-start(f32[64,64]{0,1:T(8,128)} %constant.147.clone) | copy-start | bytes 49156
  1.3 24.0 %copy-start.13 = (f32[4,128]{1,0:T(4,128)S(1)}, f32[4,128]{1,0:T(4,128)}, u32[]{:S(2)}) copy-start(f32[4,128]{1,0:T(4,128)} %constant.156) | copy-start | bytes 6148
  1.3 55.1 %copy-start.9 = (f32[64,64]{1,0:T(8,128)S(1)}, f32[64,64]{1,0:T(8,128)}, u32[]{:S(2)}) copy-start(f32[64,64]{1,0:T(8,128)} %constant.157) | copy-start | bytes 49156
  6.1 51.5 %copy-start.8 = (bf16[512,512]{1,0:T(8,128)(2,1)S(1)}, bf16[512,512]{1,0:T(8,128)(2,1)}, u32[]{:S(2)}) copy-start(bf16[512,512]{1,0:T(8,128)(2,1)} %constant.146.clone.table_ref) | copy-start | bytes 1572868
  6.1 54.9 %collective-permute-start.1 = (bf16[32,128,128]{2,1,0:T(8,128)(2,1)}, bf16[32,128,128]{2,1,0:T(8,128)(2,1)S(1)}, u32[]{:S(2)}, u32[]{:S(2)}) collective-permute-start(bf16[32,128,128]{2,1,0:T(8,128)(2,1)} %get-tuple-element.21), channel_id=1, source_target_pairs={{0,16},{8,24},{16,0},{24,8},{1,17},{9,25},{17,1},{25,9},{2,18},{10... | collective-permute-start | bytes 3145736 | tf_op jit(solution)/shard_map/ppermute | solution.py:142
  9.0 51.9 %collective-permute-start.2 = (bf16[32,128,128]{2,1,0:T(8,128)(2,1)}, bf16[32,128,128]{2,1,0:T(8,128)(2,1)S(1)}, u32[]{:S(2)}, u32[]{:S(2)}) collective-permute-start(bf16[32,128,128]{2,1,0:T(8,128)(2,1)} %get-tuple-element.22), channel_id=1, source_target_pairs={{0,24},{8,16},{16,8},{24,0},{1,25},{9,17},{17,9},{25,1},{2,26},{10... | collective-permute-start | bytes 3145736 | tf_op jit(solution)/shard_map/ppermute | solution.py:142
  15.8 40.1 %all-to-all-start = ((bf16[32,4,3,128]{3,1,2,0:T(4,128)(2,1)}), bf16[32,4,3,128]{3,1,2,0:T(4,128)(2,1)S(1)}, u32[]{:S(2)}, u32[]{:S(2)}) async-start(bf16[32,4,3,128]{3,1,2,0:T(4,128)(2,1)} %broadcast_in_dim.64), calls=%async_computation | async-start | bytes 196608 | tf_op jit(solution)/shard_map/all_to_all | solution.py:442
  20.7 40.2 %collective-permute-start = (bf16[32,128,128]{2,1,0:T(8,128)(2,1)}, bf16[32,128,128]{2,1,0:T(8,128)(2,1)}, u32[]{:S(2)}, u32[]{:S(2)}) collective-permute-start(bf16[32,128,128]{2,1,0:T(8,128)(2,1)} %get-tuple-element.20), channel_id=1, source_target_pairs={{0,8},{8,0},{16,24},{24,16},{1,9},{9,1},{17,25},{25,17},{2,10},{10... | collective-permute-start | bytes 3145736 | tf_op jit(solution)/shard_map/ppermute | solution.py:142
  56.4 37.1 %copy-start.2 = (bf16[16,512]{1,0:T(8,128)(2,1)S(1)}, bf16[16,512]{1,0:T(8,128)(2,1)}, u32[]{:S(2)}) copy-start(bf16[16,512]{1,0:T(8,128)(2,1)} %constant.151.clone.spread_ref) | copy-start | bytes 49156
  56.4 37.1 %copy-start.5 = (f32[128]{0:T(128)S(1)}, f32[128]{0:T(128)}, u32[]{:S(2)}) copy-start(f32[128]{0:T(128)} %thick_ref.5) | copy-start | bytes 1540
  56.5 37.1 %copy-start.7 = (f32[128]{0:T(128)S(1)}, f32[128]{0:T(128)}, u32[]{:S(2)}) copy-start(f32[128]{0:T(128)} %pad_maximum_fusion.gap_ref) | copy-start | bytes 1540
  61.0 1.5 copy-start.12
  77.1 16.5 %all-to-all-start.1 = ((bf16[32,16,256]{2,1,0:T(8,128)(2,1)}), bf16[32,16,256]{2,1,0:T(8,128)(2,1)S(1)}, u32[]{:S(2)}, u32[]{:S(2)}) async-start(bf16[32,16,256]{2,1,0:T(8,128)(2,1)} %bitcast.40), calls=%async_computation.1 | async-start | bytes 524288 | tf_op jit(solution)/shard_map/all_to_all | solution.py:506
  114.7 17.3 %copy-start.6 = (f32[128]{0:T(128)S(1)}, f32[128]{0:T(128)}, u32[]{:S(2)}) copy-start(f32[128]{0:T(128)} %thick_ref.5) | copy-start | bytes 1540
  114.7 40.0 %copy-start = (bf16[256,256]{1,0:T(8,128)(2,1)S(1)}, bf16[256,256]{1,0:T(8,128)(2,1)}, u32[]{:S(2)}) copy-start(bf16[256,256]{1,0:T(8,128)(2,1)} %constant.145.clone.table_ref) | copy-start | bytes 393220
  114.7 40.0 %copy-start.3 = (s32[2]{0:T(128)S(1)}, s32[2]{0:T(128)}, u32[]{:S(2)}) copy-start(s32[2]{0:T(128)} %get-tuple-element.40.me_ref) | copy-start | bytes 28
  128.5 26.3 %collective-permute-start.5 = (bf16[32,128,128]{2,1,0:T(8,128)(2,1)}, bf16[32,128,128]{2,1,0:T(8,128)(2,1)S(1)}, u32[]{:S(2)}, u32[]{:S(2)}) collective-permute-start(bf16[32,128,128]{2,1,0:T(8,128)(2,1)} %get-tuple-element.28), channel_id=1, source_target_pairs={{0,8},{8,0},{16,24},{24,16},{1,9},{9,1},{17,25},{25,17},{2,10},{10... | collective-permute-start | bytes 3145736 | tf_op jit(solution)/shard_map/ppermute | solution.py:142
  129.0 51.6 %collective-permute-start.3 = (bf16[32,128,128]{2,1,0:T(8,128)(2,1)}, bf16[32,128,128]{2,1,0:T(8,128)(2,1)S(1)}, u32[]{:S(2)}, u32[]{:S(2)}) collective-permute-start(bf16[32,128,128]{2,1,0:T(8,128)(2,1)} %get-tuple-element.25), channel_id=1, source_target_pairs={{0,16},{8,24},{16,0},{24,8},{1,17},{9,25},{17,1},{25,9},{2,18},{10... | collective-permute-start | bytes 3145736 | tf_op jit(solution)/shard_map/ppermute | solution.py:142
  129.9 50.8 %collective-permute-start.4 = (bf16[32,128,128]{2,1,0:T(8,128)(2,1)}, bf16[32,128,128]{2,1,0:T(8,128)(2,1)S(1)}, u32[]{:S(2)}, u32[]{:S(2)}) collective-permute-start(bf16[32,128,128]{2,1,0:T(8,128)(2,1)} %get-tuple-element.26), channel_id=1, source_target_pairs={{0,24},{8,16},{16,8},{24,0},{1,25},{9,17},{17,9},{25,1},{2,26},{10... | collective-permute-start | bytes 3145736 | tf_op jit(solution)/shard_map/ppermute | solution.py:142
  154.7 1.2 copy-start.1
  (1 other events, 1.0 us)
